TPU v7x, 128 devices: a whole 4x4x4 slice. The times are simulated.
128 devices in a mesh: dp: 16 (over z_lo, x, core), feat: 8 (over z_hi, y).
Axes of the slice: x: 4, y: 4, z: 4 (z_hi: 2, z_lo: 2; z = z_hi * 2 + z_lo), core: 2. Of those that a mesh axis runs over, the one named last changes fastest.
Arguments:
- embeddings: bfloat16 [2560, 128, 128], P('dp', 'feat'), may hold values from -8 to 8
- proj_weight: bfloat16 [128, 16], P('feat'), may hold values from -0.046875 to 0.046875
- up_weight: bfloat16 [2048, 8192], P('dp', 'feat'), may hold values from -0.125 to 0.125
- down_weight: bfloat16 [8192, 4096], P('feat', 'dp'), may hold values from -0.0625 to 0.0625
- mix_weight: bfloat16 [128, 96], P(None, 'feat'), may hold values from -0.5 to 0.5
- out_gain: float32 [128], replicated, may hold values from 0.1 to 1.9
- cotangent: bfloat16 [2560, 128, 128], P('dp', 'feat'), may hold values from -6 to 6
Outputs:
- layer_out: bfloat16 [2560, 128, 128], P('dp', 'feat')
- gain_grad: float32 [128], replicated
- mix_grad: float32 [128, 96], P(None, 'feat')
- up_grad: bfloat16 [2048, 8192], P('dp', 'feat')
- down_grad: bfloat16 [8192, 4096], P('feat', 'dp')
- proj_grad: float32 [128, 16], P('feat')
All inputs are finite; a program needn't handle non-finite values.
Results may differ from a plain program's by a relative error of at most 0.03.
Values may be sent and summed in bfloat16 or wider, within the bound.
No kernel may reach another device: no remote copies, remote signals or barrier semaphores. Data moves between devices by JAX's collectives and lax.ppermute only.
A program may use at most 128 MiB of HBM per device.

v0:
```python
import jax
import jax.numpy as jnp
from jax import lax
from jax.sharding import PartitionSpec as P


def silu_slope(value):
    sig = jax.nn.sigmoid(value)
    return sig * (1.0 + value * (1.0 - sig))


def per_device(embeddings, proj_weight, up_weight, down_weight, mix_weight, out_gain, cotangent):
    groups = lax.axis_size("feat")
    rows, local_tokens, width = embeddings.shape
    rank = proj_weight.shape[1]
    total_feats = local_tokens * rank * groups
    all_tokens = lax.all_gather(embeddings, "feat", axis=1, tiled=True)
    partial_value = jnp.einsum(
        "bnd,nk->bdk", embeddings, proj_weight, preferred_element_type=jnp.float32
    )
    proj = lax.psum(partial_value.astype(jnp.bfloat16), "feat")
    inter = jnp.einsum("bnd,bdk->bnk", embeddings, proj, preferred_element_type=jnp.float32)
    inter = inter.reshape(rows, local_tokens * rank)
    first_sum, square_sum = lax.psum(
        (jnp.sum(inter, axis=1), jnp.sum(inter * inter, axis=1)), "feat"
    )
    mean1 = first_sum / total_feats
    var1 = square_sum / total_feats - mean1 * mean1
    rstd1 = lax.rsqrt(var1 + 1e-05)[:, None]
    normal1 = (inter - mean1[:, None]) * rstd1
    normed_b = normal1.astype(jnp.bfloat16)
    normed_full = lax.all_gather(normed_b, "feat", axis=1, tiled=True)
    up_full = lax.all_gather(up_weight, "dp", axis=0, tiled=True)
    pre = jnp.dot(normed_full, up_full, preferred_element_type=jnp.float32)
    hidden_b = jax.nn.silu(pre).astype(jnp.bfloat16)
    down_full = lax.all_gather(down_weight, "dp", axis=1, tiled=True)
    fmb_part = jnp.dot(hidden_b, down_full, preferred_element_type=jnp.float32)
    lcb = jnp.einsum("bnd,nl->bld", all_tokens, mix_weight, preferred_element_type=jnp.float32)
    fmb_mine = lax.psum_scatter(
        fmb_part.astype(jnp.bfloat16), "feat", scatter_dimension=1, tiled=True
    ).astype(jnp.float32)
    fmb_tokens = fmb_mine.shape[1] // width
    fmb_mine = fmb_mine.reshape(rows, fmb_tokens, width)
    summed = jnp.concatenate([fmb_mine, lcb], axis=1) + embeddings.astype(jnp.float32)
    mean2 = jnp.mean(summed, axis=2, keepdims=True)
    cent2 = summed - mean2
    rstd2 = lax.rsqrt(jnp.mean(cent2 * cent2, axis=2, keepdims=True) + 1e-05)
    normal2 = cent2 * rstd2
    layer_out = (normal2 * out_gain).astype(jnp.bfloat16)
    cotan = cotangent.astype(jnp.float32)
    gain_grad = lax.psum(jnp.sum(cotan * normal2, axis=(0, 1)), ("dp", "feat"))
    dnorm = cotan * out_gain
    dsum = rstd2 * (
        dnorm
        - jnp.mean(dnorm, axis=2, keepdims=True)
        - normal2 * jnp.mean(dnorm * normal2, axis=2, keepdims=True)
    )
    d_fmb = dsum[:, :fmb_tokens].reshape(rows, fmb_tokens * width)
    d_lcb = dsum[:, fmb_tokens:]
    mix_part = jnp.einsum("bnd,bld->nl", all_tokens, d_lcb, preferred_element_type=jnp.float32)
    d_fmb_b = d_fmb.astype(jnp.bfloat16)
    d_fmb_full = lax.all_gather(d_fmb_b, "feat", axis=1, tiled=True)
    down_part = jnp.dot(hidden_b.T, d_fmb_full, preferred_element_type=jnp.float32)
    down_grad = lax.psum_scatter(
        down_part.astype(jnp.bfloat16), "dp", scatter_dimension=1, tiled=True
    )
    d_hidden = jnp.dot(d_fmb_full, down_full.T, preferred_element_type=jnp.float32)
    d_pre_b = (d_hidden * silu_slope(pre)).astype(jnp.bfloat16)
    up_part = jnp.dot(normed_full.T, d_pre_b, preferred_element_type=jnp.float32)
    up_grad = lax.psum_scatter(up_part.astype(jnp.bfloat16), "dp", scatter_dimension=0, tiled=True)
    normed_part = jnp.dot(d_pre_b, up_full.T, preferred_element_type=jnp.float32)
    d_normed = lax.psum_scatter(
        normed_part.astype(jnp.bfloat16), "feat", scatter_dimension=1, tiled=True
    ).astype(jnp.float32)
    grad_first, grad_second = lax.psum(
        (jnp.sum(d_normed, axis=1), jnp.sum(d_normed * normal1, axis=1)), "feat"
    )
    d_inter = rstd1 * (
        d_normed
        - (grad_first / total_feats)[:, None]
        - normal1 * (grad_second / total_feats)[:, None]
    )
    d_inter = d_inter.reshape(rows, local_tokens, rank)
    proj_part_grad = jnp.einsum(
        "bnd,bnk->bdk", embeddings, d_inter, preferred_element_type=jnp.float32
    )
    d_proj = lax.psum(proj_part_grad.astype(jnp.bfloat16), "feat").astype(jnp.float32)
    proj_rows_grad = jnp.einsum(
        "bnd,bdk->nk", embeddings, d_proj, preferred_element_type=jnp.float32
    )
    mix_grad, proj_grad = lax.psum((mix_part, proj_rows_grad), "dp")
    return (layer_out, gain_grad, mix_grad, up_grad, down_grad, proj_grad)


def solution(mesh):
    placed = (
        P("dp", "feat", None),
        P("feat", None),
        P("dp", "feat"),
        P("feat", "dp"),
        P(None, "feat"),
        P(),
        P("dp", "feat", None),
    )
    return jax.shard_map(
        per_device,
        mesh=mesh,
        in_specs=placed,
        out_specs=(
            P("dp", "feat", None),
            P(),
            P(None, "feat"),
            P("dp", "feat"),
            P("feat", "dp"),
            P("feat", None),
        ),
        check_vma=False,
    )
```

profile of v0, /device:TPU:1, one launch (start us, length us, event | category | flops | bytes accessed | tf_op | source)
XLA Modules:
  0.0 584.2 jit_solution(17787323526332033825)
XLA Ops:
  8.7 2.3 convolution_convert_fusion.5
  12.8 84.1 %all-reduce.6.cloned.1.call-done = bf16[160,128,16]{1,2,0:T(8,128)(2,1)} async-done(((bf16[160,128,16]{1,2,0:T(8,128)(2,1)}), bf16[160,128,16]{1,2,0:T(8,128)(2,1)}) %all-reduce.6.cloned.1.call-update) | async-done | bytes 655376 | tf_op jit(solution)/shard_map/psum | solution.py:21
  96.9 2.3 multiply_reduce_fusion.1
  99.2 1.0 reduce_sum.81
  100.2 0.8 copy.14
  101.1 16.8 %all-reduce.2 = (f32[160]{0:T(256)S(1)}, f32[160]{0:T(256)S(1)}) all-reduce(f32[160]{0:T(256)S(1)} %get-tuple-element.34, f32[160]{0:T(256)S(1)} %reduce_sum.81), channel_id=1, replica_groups=mesh['dp'=16,'feat'=8] {'feat'}, use_global_device_ids=true, to_apply=%region_4.0 | all-reduce | flops 320 | bytes 2560 | tf_op jit(solution)/shard_map/psum | solution.py:24
  118.0 29.7 %all_gather.15 = bf16[160,2048]{1,0:T(8,128)(2,1)S(1)} all-gather(bf16[160,256]{1,0:T(8,128)(2,1)S(1)} %fusion.17), channel_id=1, replica_groups=mesh['dp'=16,'feat'=8] {'feat'}, dimensions={1}, use_global_device_ids=true | all-gather | bytes 737280 | tf_op jit(solution)/shard_map/all_gather | solution.py:32
  147.7 3.2 fusion.21
  150.9 6.1 %convolution_convert_fusion.1 = bf16[160,4096]{1,0:T(8,128)(2,1)} fusion(bf16[1024,4096]{1,0:T(8,128)(2,1)} %all-gather.7.cloned.1.call-done, f32[160,1024]{1,0:T(8,128)S(1)} %fusion.21), kind=kOutput, calls=%fused_computation.1 | convolution fusion | flops 1343651840 | bytes 10354688 | tf_op jit(solution)/shard_map/dot_general | solution.py:37
  157.1 54.6 %all-gather.9.cloned.1.call-done = bf16[160,128,128]{2,1,0:T(8,128)(2,1)} async-done(((bf16[160,16,128]{2,1,0:T(8,128)(2,1)}), bf16[160,128,128]{2,1,0:T(8,128)(2,1)}) %all-gather.9.cloned.1.call-update) | async-done | bytes 5242896 | tf_op jit(solution)/shard_map/all_gather | solution.py:17
  211.7 3.4 convolution_bitcast_fusion
  215.0 50.7 %reduce-scatter.5.cloned.1.call-done = bf16[160,512]{1,0:T(8,128)(2,1)} async-done(((bf16[160,4096]{1,0:T(8,128)(2,1)}), bf16[160,512]{1,0:T(8,128)(2,1)}) %reduce-scatter.5.cloned.1.call-update) | async-done | bytes 163856 | tf_op jit(solution)/shard_map/reduce_scatter | solution.py:39
  265.8 1.7 reshape.56
  267.5 1.4 fusion.20
  269.0 0.8 multiply_reduce_fusion
  270.1 2.4 fusion.5
  272.5 1.7 fusion.4
  275.2 49.3 %all-gather.11.cloned.1.call-done = bf16[160,4096]{1,0:T(8,128)(2,1)} async-done(((bf16[160,512]{1,0:T(8,128)(2,1)}), bf16[160,4096]{1,0:T(8,128)(2,1)}) %all-gather.11.cloned.1.call-update) | async-done | bytes 1310736 | tf_op jit(solution)/shard_map/all_gather | solution.py:62
  324.5 6.9 %fusion.10 = bf16[160,1024]{1,0:T(8,128)(2,1)S(1)} fusion(bf16[160,4096]{1,0:T(8,128)(2,1)} %all-gather.11.cloned.1.call-done, bf16[1024,4096]{1,0:T(8,128)(2,1)} %all-gather.7.cloned.1.call-done, f32[160,1024]{1,0:T(8,128)S(1)} %fusion.21), kind=kOutput, calls=%fused_computation.25 | convolution fusion | flops 1343651840 | bytes 10682368 | tf_op jit(solution)/shard_map/dot_general | solution.py:67
  332.1 2.4 convolution_convert_fusion.3
  334.6 69.9 %reduce-scatter.11.cloned.1.call-done = bf16[160,256]{1,0:T(8,128)(2,1)} async-done(((bf16[160,2048]{1,0:T(8,128)(2,1)}), bf16[160,256]{1,0:T(8,128)(2,1)}) %reduce-scatter.11.cloned.1.call-update) | async-done | bytes 81936 | tf_op jit(solution)/shard_map/reduce_scatter | solution.py:72
  404.4 1.1 convert_reduce_fusion
  405.5 17.8 %all-reduce.1 = (f32[160]{0:T(256)S(1)}, f32[160]{0:T(256)S(1)}) all-reduce(f32[160]{0:T(256)S(1)} %get-tuple-element.22, f32[160]{0:T(256)S(1)} %get-tuple-element.21), channel_id=1, replica_groups=mesh['dp'=16,'feat'=8] {'feat'}, use_global_device_ids=true, to_apply=%region_19.20 | all-reduce | flops 320 | bytes 2560 | tf_op jit(solution)/shard_map/psum | solution.py:75
  423.4 1.0 fusion.15
  425.1 1.3 fusion.9
  426.5 4.2 convolution_convert_fusion.2
  430.8 7.0 %convolution_convert_fusion = bf16[1024,4096]{1,0:T(8,128)(2,1)} fusion(bf16[160,4096]{1,0:T(8,128)(2,1)} %all-gather.11.cloned.1.call-done, f32[160,1024]{1,0:T(8,128)S(1)} %fusion.21), kind=kOutput, calls=%fused_computation | convolution fusion | flops 1347190784 | bytes 10354688 | tf_op jit(solution)/shard_map/dot_general | solution.py:63
  437.8 72.1 %psum.66 = f32[128]{0:T(128)} all-reduce(f32[128]{0:T(128)S(1)} %get-tuple-element.19), channel_id=1, replica_groups=mesh['dp'=16,'feat'=8] {'dp','feat'}, use_global_device_ids=true, to_apply=%region_9.10 | all-reduce | flops 128 | bytes 1024 | tf_op jit(solution)/shard_map/psum | solution.py:51
  509.9 3.9 fusion.11
  513.8 1.5 convolution_bitcast_fusion.1
  515.4 53.1 %all-reduce = (f32[128,12]{0,1:T(8,128)}, f32[16,16]{0,1:T(8,128)S(1)}) all-reduce(f32[128,12]{0,1:T(8,128)S(1)} %fusion.11, f32[16,16]{0,1:T(8,128)S(1)} %convolution_bitcast_fusion.1), channel_id=1, replica_groups=mesh['dp'=16,'feat'=8] {'dp'}, use_global_device_ids=true, to_apply=%region_12.13 | all-reduce | flops 1792 | bytes 14336 | tf_op jit(solution)/shard_map/psum | solution.py:91
  569.2 7.7 %reduce-scatter.9.cloned.1.call-done = bf16[1024,256]{1,0:T(8,128)(2,1)} async-done(((bf16[1024,4096]{1,0:T(8,128)(2,1)}), bf16[1024,256]{1,0:T(8,128)(2,1)}) %reduce-scatter.9.cloned.1.call-update) | async-done | bytes 524304 | tf_op jit(solution)/shard_map/reduce_scatter | solution.py:64
  (51 shorter events, 6.3 us)
Async XLA Ops:
  8.0 0.7 copy-start
  8.0 88.9 %all-reduce.6.cloned.1.call-start = ((), (), s32[]{:S(2)}) async-start(), calls=%async_computation.4 | async-start | bytes 1310720 | tf_op jit(solution)/shard_map/psum | solution.py:21
  11.0 85.9 %copy-start.1 = (bf16[160,16,128]{2,1,0:T(8,128)(2,1)S(1)}, bf16[160,16,128]{2,1,0:T(8,128)(2,1)}, u32[]{:S(2)}) copy-start(bf16[160,16,128]{2,1,0:T(8,128)(2,1)} %param.7) | copy-start | bytes 1966084
  11.0 136.7 %all-gather.5.cloned.1.call-start = ((), (), s32[]{:S(2)}) async-start(), calls=%async_computation.5 | async-start | bytes 4456448 | tf_op jit(solution)/shard_map/all_gather | solution.py:33
  11.6 139.3 %all-gather.7.cloned.1.call-start = ((), (), s32[]{:S(2)}) async-start(), calls=%async_computation.6 | async-start | bytes 8912896 | tf_op jit(solution)/shard_map/all_gather | solution.py:36
  12.2 199.5 %all-gather.9.cloned.1.call-start = ((), (), s32[]{:S(2)}) async-start(), calls=%async_computation.8 | async-start | bytes 5898240 | tf_op jit(solution)/shard_map/all_gather | solution.py:17
  12.8 253.0 %reduce-scatter.5.cloned.1.call-start = ((), (), s32[]{:S(2)}) async-start(), calls=%async_computation.7 | async-start | bytes 1474560 | tf_op jit(solution)/shard_map/reduce_scatter | solution.py:39
  157.0 54.7 %copy-start.5 = (bf16[128,12]{0,1:T(8,128)(2,1)S(1)}, bf16[128,12]{0,1:T(8,128)(2,1)}, u32[]{:S(2)}) copy-start(bf16[128,12]{0,1:T(8,128)(2,1)} %param.11) | copy-start | bytes 9220
  157.0 167.4 %all-gather.11.cloned.1.call-start = ((), (), s32[]{:S(2)}) async-start(), calls=%async_computation.9 | async-start | bytes 1474560 | tf_op jit(solution)/shard_map/all_gather | solution.py:62
  269.0 1.1 copy-start.3
  269.0 1.1 copy-start.6
  274.9 129.5 %reduce-scatter.11.cloned.1.call-start = ((), (), s32[]{:S(2)}) async-start(), calls=%async_computation.12 | async-start | bytes 737280 | tf_op jit(solution)/shard_map/reduce_scatter | solution.py:72
  324.4 7.7 %copy-start.2 = (bf16[2048,1024]{1,0:T(8,128)(2,1)S(1)}, bf16[2048,1024]{1,0:T(8,128)(2,1)}, u32[]{:S(2)}) copy-start(bf16[2048,1024]{1,0:T(8,128)(2,1)} %all-gather.5.cloned.1.call-done) | copy-start | bytes 12582916
  331.4 0.7 copy-start.4
  334.5 179.3 %all-reduce.8.cloned.1.call-start = ((), (), s32[]{:S(2)}) async-start(), calls=%async_computation.13 | async-start | bytes 1310720 | tf_op jit(solution)/shard_map/psum | solution.py:87
  426.4 142.7 %reduce-scatter.7.cloned.1.call-start = ((), (), s32[]{:S(2)}) async-start(), calls=%async_computation.10 | async-start | bytes 4456448 | tf_op jit(solution)/shard_map/reduce_scatter | solution.py:70
  430.7 146.1 %reduce-scatter.9.cloned.1.call-start = ((), (), s32[]{:S(2)}) async-start(), calls=%async_computation.11 | async-start | bytes 8912896 | tf_op jit(solution)/shard_map/reduce_scatter | solution.py:64
Sparse Core Ops, SparseCore 0:
  11.9 84.9 all-reduce.5
  157.1 108.6 reduce-scatter.4
  275.1 49.3 all-gather.10
  334.6 69.7 reduce-scatter.10
  426.6 85.8 all-reduce.7
Sparse Core Ops, SparseCore 1:
  13.2 42.9 all-gather.4
  57.7 61.8 all-gather.6
  121.6 90.0 all-gather.8
  430.8 69.2 reduce-scatter.6
  503.3 73.5 reduce-scatter.8
where the time goes:
time: 588 us; the launch traced here: 584 us
  waiting for transfers between devices  318 us (54%)
  blocking collectives  190 us (32%)
  matrix products  44.4 us (8%)
  between operations  15.7 us (3%)
  other arithmetic  9.64 us (2%)
  local copies, waits for them, and re-layouts  6.29 us (1%)
    psum x1, waiting for transfers between devices, per_device(): proj = lax.psum(partial_value.astype(jnp.bfloat16), 'feat')  84.1 us
    psum x1, blocking collectives, per_device(): gain_grad = lax.psum(jnp.sum(cotan * normal2, axis=(0, 1)), ('dp', 'feat'))  72.1 us
    reduce_scatter x1, waiting for transfers between devices, per_device(): lax.psum_scatter(normed_part.astype(jnp.bfloat16), 'feat', scatter_dimens...  69.9 us
    all_gather x1, waiting for transfers between devices, per_device(): all_tokens = lax.all_gather(embeddings, 'feat', axis=1, tiled=True)  54.6 us
    psum x1, blocking collectives, per_device(): mix_grad, proj_grad = lax.psum((mix_part, proj_rows_grad), 'dp')  53.1 us
    reduce_scatter x1, waiting for transfers between devices, per_device(): lax.psum_scatter(fmb_part.astype(jnp.bfloat16), 'feat', scatter_dimension...  50.7 us
    all_gather x1, waiting for transfers between devices, per_device(): d_fmb_full = lax.all_gather(d_fmb_b, 'feat', axis=1, tiled=True)  49.3 us
    all_gather x1, blocking collectives, per_device(): normed_full = lax.all_gather(normed_b, 'feat', axis=1, tiled=True)  29.7 us
  transfers between devices with their start and end apart: 10, of which 6 were waited for; matrix products, arithmetic and copies ran while one was open for 6% of the time, Pallas kernels for 0%

commit v1 on v0

v1 whole, which is shorter than its diff:
```python
import jax
import jax.numpy as jnp
from jax import lax
from jax.sharding import Mesh, PartitionSpec as P

BF = jnp.bfloat16
F32 = jnp.float32
DP = ("zlo", "x", "core")
FEAT = ("zhi", "y")
ALL = DP + FEAT
EPS = 1e-05
FWD = [(i, (i + 1) % 4) for i in range(4)]
BWD = [(i, (i + 3) % 4) for i in range(4)]
SWAP = [(0, 1), (1, 0)]


def silu_slope(value):
    sig = jax.nn.sigmoid(value)
    return sig * (1.0 + value * (1.0 - sig))


def sibling(a):
    return lax.ppermute(a, "core", SWAP)


def across(a):
    return lax.ppermute(a, "zlo", SWAP)


def right(a):
    return lax.ppermute(a, "x", FWD)


def left(a):
    return lax.ppermute(a, "x", BWD)


def exchange(a, axes):
    return lax.all_to_all(a, axes, 0, 0, tiled=True)


def flip(a, axis, position):
    return jnp.where(position == 0, a, jnp.flip(a, axis))


def turn(a, axis, by):
    return lax.dynamic_slice_in_dim(jnp.concatenate([a, a], axis), by, 4, axis)


def to_relative(a):
    rows, cols = a.shape
    a = a.reshape(rows, 2, 4, 2, cols // 16)
    a = flip(a, 1, lax.axis_index("zlo"))
    a = turn(a, 2, lax.axis_index("x"))
    return a.reshape(rows, cols)


def to_absolute(a):
    rows, cols = a.shape
    a = a.reshape(rows, 2, 4, 2, cols // 16)
    a = flip(a, 1, lax.axis_index("zlo"))
    a = turn(a, 2, lax.rem(4 - lax.axis_index("x"), 4))
    return a.reshape(rows, cols)


def by_core(core, mine, theirs, axis):
    return jnp.where(
        core == 0,
        jnp.concatenate([mine, theirs], axis),
        jnp.concatenate([theirs, mine], axis),
    )


def gather_weights(up, down):
    core = lax.axis_index("core")

    def up_half(which):
        return lax.dynamic_slice_in_dim(up, which * 512, 512, 1)

    def down_half(which):
        return lax.dynamic_slice_in_dim(down, which * 512, 512, 0)

    up_chip = by_core(core, up_half(core), sibling(up_half(1 - core)), 0)
    down_chip = by_core(core, down_half(core), sibling(down_half(1 - core)), 1)
    mine = jnp.concatenate([up_chip, down_chip], 0)
    half = mine.shape[0] // 2

    def around(a):
        from_left, from_right = right(a), left(a)
        far = jnp.concatenate([right(from_left[:half]), left(from_right[half:])], 0)
        return [a, from_right, far, from_left]

    other = across(mine)
    return around(mine) + around(other)


def reduce_weights(pieces):
    half = pieces[0].shape[0] // 2

    def plus(*terms):
        total = terms[0].astype(F32)
        for term in terms[1:]:
            total = total + term.astype(F32)
        return total.astype(BF)

    def around(own, plus_one, far, minus_one):
        from_left = right(far[:half])
        from_right = left(far[half:])
        direct_left = right(plus_one[half:])
        direct_right = left(minus_one[:half])
        relay_left = right(plus(plus_one[:half], from_left))
        relay_right = left(plus(minus_one[half:], from_right))
        return jnp.concatenate(
            [
                plus(own[:half], direct_right, relay_left),
                plus(own[half:], direct_left, relay_right),
            ],
            0,
        )

    other = across(around(*pieces[4:]))
    total = plus(around(*pieces[:4]), other)
    up_chip, down_chip = total[:256], total[256:]
    core = lax.axis_index("core")

    def up_rows(which):
        return lax.dynamic_slice_in_dim(up_chip, which * 128, 128, 0)

    def down_cols(which):
        return lax.dynamic_slice_in_dim(down_chip, which * 256, 256, 1)

    up_grad = by_core(core, up_rows(core), sibling(up_rows(1 - core)), 1)
    down_grad = by_core(core, down_cols(core), sibling(down_cols(1 - core)), 0)
    return up_grad, down_grad


def dot(a, b, dims):
    return lax.dot_general(a, b, (dims, ((), ())), preferred_element_type=F32)


def per_device(embeddings, proj_weight, up_weight, down_weight, mix_weight, out_gain, cotangent):
    weights = gather_weights(up_weight, down_weight)
    up_all = jnp.concatenate([w[:256] for w in weights], 0)
    down_all = jnp.concatenate([w[256:] for w in weights], 1)

    def spread(a):
        return jnp.broadcast_to(a.reshape(1, -1, 128), (8, a.size // 128, 128))

    message = jnp.concatenate(
        [
            embeddings.reshape(8, 320, 128),
            cotangent.reshape(8, 320, 128),
            spread(mix_weight.T),
            spread(proj_weight),
            jnp.zeros((8, 2, 128), BF),
        ],
        1,
    )
    message = exchange(message, FEAT)
    tokens = message[:, :320].reshape(8, 20, 16, 128).transpose(1, 0, 2, 3).reshape(20, 128, 128)
    cotan = message[:, 320:640].reshape(8, 20, 16, 128).transpose(1, 0, 2, 3).astype(F32)
    mix = message[:, 640:652].reshape(96, 128)
    proj_w = message[:, 652:654].reshape(128, 16)

    proj = jnp.einsum("nk,bnd->bkd", proj_w, tokens, preferred_element_type=F32).astype(BF)
    inter = jnp.einsum("bkd,bnd->bkn", proj, tokens, preferred_element_type=F32)
    cent1 = inter - jnp.mean(inter, axis=(1, 2), keepdims=True)
    rstd1 = lax.rsqrt(jnp.mean(cent1 * cent1, axis=(1, 2), keepdims=True) + EPS)
    normal1 = cent1 * rstd1
    normed = to_relative(normal1.astype(BF).transpose(0, 2, 1).reshape(20, 2048))

    normed = exchange(jnp.broadcast_to(normed[None], (8, 20, 2048)), FEAT).reshape(160, 2048)
    normed = jnp.concatenate([normed, sibling(normed)], 0)
    pre = dot(normed, up_all, ((1,), (0,)))
    hidden = jax.nn.silu(pre).astype(BF)
    fmb = dot(hidden, down_all, ((1,), (0,)))
    fmb = (fmb[:160] + sibling(fmb[160:].astype(BF)).astype(F32)).astype(BF)
    fmb = jnp.sum(exchange(fmb.reshape(8, 20, 4096), FEAT).astype(F32), 0)
    fmb = to_absolute(fmb).reshape(20, 8, 4, 128)

    lcb = jnp.einsum("jn,bnd->bjd", mix, tokens, preferred_element_type=F32)
    summed = jnp.concatenate([fmb, lcb.reshape(20, 8, 12, 128)], 2)
    summed = summed + tokens.reshape(20, 8, 16, 128).astype(F32)
    cent2 = summed - jnp.mean(summed, axis=3, keepdims=True)
    rstd2 = lax.rsqrt(jnp.mean(cent2 * cent2, axis=3, keepdims=True) + EPS)
    normal2 = cent2 * rstd2
    layer_out = (normal2 * out_gain).astype(BF)
    gain_part = jnp.sum(cotan * normal2, axis=(0, 1, 2))
    dnorm = cotan * out_gain
    dsum = rstd2 * (
        dnorm
        - jnp.mean(dnorm, axis=3, keepdims=True)
        - normal2 * jnp.mean(dnorm * normal2, axis=3, keepdims=True)
    )
    d_fmb = to_relative(dsum[:, :, :4].astype(BF).reshape(20, 4096))
    d_lcb = dsum[:, :, 4:].astype(BF).reshape(20, 96, 128)

    d_fmb = exchange(jnp.broadcast_to(d_fmb[None], (8, 20, 4096)), FEAT).reshape(160, 4096)
    d_fmb = jnp.concatenate([d_fmb, sibling(d_fmb)], 0)
    d_hidden = dot(d_fmb, down_all, ((1,), (1,)))
    d_pre = (d_hidden * silu_slope(pre)).astype(BF)
    up_part = dot(normed, d_pre, ((0,), (0,))).astype(BF)
    down_part = dot(hidden, d_fmb, ((0,), (0,))).astype(BF)
    pieces = [
        jnp.concatenate(
            [up_part[r * 256 : (r + 1) * 256], down_part[:, r * 512 : (r + 1) * 512]], 0
        )
        for r in range(8)
    ]
    up_grad, down_grad = reduce_weights(pieces)

    d_normed = dot(d_pre, up_all, ((1,), (1,)))
    d_normed = (d_normed[:160] + sibling(d_normed[160:].astype(BF)).astype(F32)).astype(BF)
    message = jnp.concatenate(
        [
            d_normed.reshape(8, 320, 128),
            layer_out.transpose(1, 0, 2, 3).reshape(8, 320, 128),
        ],
        1,
    )
    message = exchange(message, FEAT)
    layer_out = message[:, 320:].reshape(160, 16, 128)
    d_normed = jnp.sum(message[:, :320].astype(F32), 0).reshape(20, 2048)
    d_normed = to_absolute(d_normed).reshape(20, 128, 16).transpose(0, 2, 1)
    d_inter = rstd1 * (
        d_normed
        - jnp.mean(d_normed, axis=(1, 2), keepdims=True)
        - normal1 * jnp.mean(d_normed * normal1, axis=(1, 2), keepdims=True)
    )
    d_proj = jnp.einsum(
        "bkn,bnd->bkd", d_inter.astype(BF), tokens, preferred_element_type=F32
    ).astype(BF)
    proj_part = jnp.einsum("bnd,bkd->nk", tokens, d_proj, preferred_element_type=F32)
    mix_part = jnp.einsum("bjd,bnd->jn", d_lcb, tokens, preferred_element_type=F32)

    last = jnp.concatenate(
        [
            proj_part.reshape(8, 2, 128),
            mix_part.reshape(8, 12, 128),
            jnp.broadcast_to(gain_part, (8, 1, 128)),
            jnp.zeros((8, 1, 128), F32),
        ],
        1,
    ).astype(BF)
    last = jnp.broadcast_to(last[None], (16, 8, 16, 128)).reshape(128, 16, 128)
    last = jnp.sum(exchange(last, ALL).astype(F32), 0)
    proj_grad = last[:2].reshape(16, 16)
    mix_grad = last[2:14].T
    gain_grad = last[14]
    return (layer_out, gain_grad, mix_grad, up_grad, down_grad, proj_grad)


def solution(mesh):
    grid = Mesh(mesh.devices.reshape(2, 4, 2, 2, 4), ALL)
    placed = (
        P(DP, FEAT, None),
        P(FEAT, None),
        P(DP, FEAT),
        P(FEAT, DP),
        P(None, FEAT),
        P(),
        P(DP, FEAT, None),
    )
    return jax.shard_map(
        per_device,
        mesh=grid,
        in_specs=placed,
        out_specs=(
            P(DP, FEAT, None),
            P(),
            P(None, FEAT),
            P(DP, FEAT),
            P(FEAT, DP),
            P(FEAT, None),
        ),
        check_vma=False,
    )
```

time: 588 us -> 284 us (0.48)
  waiting for transfers between devices: 318 us -> 74.2 us
  blocking collectives: 190 us -> 23.8 us
  starting transfers between devices: 0.6 us -> 73.7 us
  local copies, waits for them, and re-layouts: 6.29 us -> 60.6 us
  matrix products: 44.4 us -> 13.8 us
  other arithmetic: 9.64 us -> 34.8 us
  between operations: 15.7 us -> 1.36 us
    psum x4 -> x0, blocking collectives: 160 us -> none  [the longest x1 72.1 us: per_device(): gain_grad = lax.psum(jnp.sum(cotan * normal2, axis=(0, 1)), ('dp', 'feat'))]
    reduce_scatter x4 -> x0, waiting for transfers between devices: 128 us -> none  [the longest x1 69.9 us: per_device(): lax.psum_scatter(normed_part.astype(jnp.bfloat16), 'feat', scatter_dimens...]
    all_gather x4 -> x0, waiting for transfers between devices: 104 us -> none  [the longest x1 54.6 us: per_device(): all_tokens = lax.all_gather(embeddings, 'feat', axis=1, tiled=True)]
    psum x2 -> x0, waiting for transfers between devices: 84.1 us -> none  [the longest x1 84.1 us: per_device(): proj = lax.psum(partial_value.astype(jnp.bfloat16), 'feat')]
    ppermute x0 -> x30, waiting for transfers between devices: none -> 43.4 us  [the longest x10 35.1 us: right(): return lax.ppermute(a, 'x', FWD)]
    ppermute x0 -> x30, starting transfers between devices: none -> 42.3 us  [the longest x10 24.9 us: left(): return lax.ppermute(a, 'x', BWD)]
    all_to_all x0 -> x5, starting transfers between devices: none -> 31.4 us  [exchange(): return lax.all_to_all(a, axes, 0, 0, tiled=True)]
    all_to_all x0 -> x5, waiting for transfers between devices: none -> 30.8 us  [exchange(): return lax.all_to_all(a, axes, 0, 0, tiled=True)]
  transfers between devices with their start and end apart: 10 -> 35, of which waited for: 6 -> 15; matrix products, arithmetic and copies ran while one was open for 6% -> 25% of each run, Pallas kernels for 0% -> 0%
where the time goes in v1:
time: 284 us; the launch traced here: 282 us
  waiting for transfers between devices  74.2 us (26%)
  starting transfers between devices  73.7 us (26%)
  local copies, waits for them, and re-layouts  60.6 us (21%)
  other arithmetic  34.8 us (12%)
  blocking collectives  23.8 us (8%)
  matrix products  13.8 us (5%)
    ppermute x10, waiting for transfers between devices, right(): return lax.ppermute(a, 'x', FWD)  35.1 us
    all_to_all x5, starting transfers between devices, exchange(): return lax.all_to_all(a, axes, 0, 0, tiled=True)  31.4 us
    all_to_all x5, waiting for transfers between devices, exchange(): return lax.all_to_all(a, axes, 0, 0, tiled=True)  30.8 us
    ppermute x10, starting transfers between devices, left(): return lax.ppermute(a, 'x', BWD)  24.9 us
    all_to_all x1, blocking collectives, exchange(): return lax.all_to_all(a, axes, 0, 0, tiled=True)  23.8 us
    unnamed x68, local copies, waits for them, and re-layouts  21 us
    ppermute x8, starting transfers between devices, sibling(): return lax.ppermute(a, 'core', SWAP)  12.8 us
    convert_element_type x8, other arithmetic, plus(): return total.astype(BF)  9.73 us
  transfers between devices with their start and end apart: 35, of which 15 were waited for; matrix products, arithmetic and copies ran while one was open for 25% of the time, Pallas kernels for 0%

profile of v1, /device:TPU:1, one launch (start us, length us, event | category | flops | bytes accessed | tf_op | source)
XLA Modules:
  0.0 282.2 jit_solution(5656732364572224109)
XLA Ops:
  8.3 2.6 collective-permute-start.3
  12.7 6.1 %concatenate.106 = bf16[8,656,128]{2,1,0:T(8,128)(2,1)} concatenate(bf16[8,320,128]{2,1,0:T(8,128)(2,1)S(1)} %bitcast.114, bf16[8,320,128]{2,1,0:T(8,128)(2,1)S(1)} %bitcast.115, bf16[8,12,128]{2,1,0:T(8,128)(2,1)S(1)} %broadcast_in_dim.22, bf16[8,2,128]{2,1,0:T(2,128)(2,1)S(1)} %broadcast_in_dim.24, bf16[8,2,128]{2,1,0:T(2,128)(2,1)S(1)} %broadcast_in_dim.25), dimensions={1} | concatenate | bytes 2686976 | tf_op jit(solution)/shard_map/concatenate | solution.py:149
  18.8 7.2 %all-to-all-start = ((bf16[8,656,128]{2,1,0:T(8,128)(2,1)}), bf16[8,656,128]{2,1,0:T(8,128)(2,1)S(1)}, u32[]{:S(2)}, u32[]{:S(2)}) async-start(bf16[8,656,128]{2,1,0:T(8,128)(2,1)} %concatenate.106), calls=%async_computation | async-start | bytes 2686976 | tf_op jit(solution)/shard_map/all_to_all | solution.py:39
  29.8 3.4 %collective-permute-start.10 = (bf16[384,512]{1,0:T(8,128)(2,1)}, bf16[384,512]{1,0:T(8,128)(2,1)}, u32[]{:S(2)}, u32[]{:S(2)}) collective-permute-start(bf16[384,512]{1,0:T(8,128)(2,1)} %slice.292), channel_id=1, source_target_pairs={{0,48},{16,0},{32,16},{48,32},{1,49},{17,1},{33,17},{49,33},{2,50}... | collective-permute-start | bytes 1179656 | tf_op jit(solution)/shard_map/ppermute | solution.py:35
  34.0 2.7 collective-permute-start.7
  40.3 7.4 %all-to-all-done = bf16[8,656,128]{2,1,0:T(8,128)(2,1)S(1)} async-done(((bf16[8,656,128]{2,1,0:T(8,128)(2,1)}), bf16[8,656,128]{2,1,0:T(8,128)(2,1)S(1)}, u32[]{:S(2)}, u32[]{:S(2)}) %all-to-all-start) | async-done | bytes 1343520 | tf_op jit(solution)/shard_map/all_to_all | solution.py:39
  51.4 6.5 %all-to-all-start.1 = ((bf16[8,20,2048]{2,1,0:T(8,128)(2,1)}), bf16[8,20,2048]{2,1,0:T(8,128)(2,1)S(1)}, u32[]{:S(2)}, u32[]{:S(2)}) async-start(bf16[8,20,2048]{2,1,0:T(8,128)(2,1)} %broadcast_in_dim.27), calls=%async_computation.1 | async-start | bytes 1572864 | tf_op jit(solution)/shard_map/all_to_all | solution.py:39
  69.4 4.0 %collective-permute-start = (bf16[160,2048]{1,0:T(8,128)(2,1)S(1)}, bf16[160,2048]{1,0:T(8,128)(2,1)S(1)}, u32[]{:S(2)}, u32[]{:S(2)}) collective-permute-start(bf16[160,2048]{1,0:T(8,128)(2,1)S(1)} %reshape.146), channel_id=1, source_target_pairs={{0,8},{8,0},{1,9},{9,1},{2,10},{10,2},{3,11},{11,3},{4,12},{12,4},... | collective-permute-start | bytes 1966088 | tf_op jit(solution)/shard_map/ppermute | solution.py:23
  74.6 2.7 collective-permute-start.11
  81.3 8.6 %collective-permute-done.9 = bf16[384,512]{1,0:T(8,128)(2,1)S(1)} collective-permute-done((bf16[384,512]{1,0:T(8,128)(2,1)S(1)}, bf16[384,512]{1,0:T(8,128)(2,1)S(1)}, u32[]{:S(2)}, u32[]{:S(2)}) %collective-permute-start.9) | collective-permute-done | bytes 393248 | tf_op jit(solution)/shard_map/ppermute | solution.py:31
  91.8 2.3 slice_dynamic-update-slice_fusion
  100.5 2.7 collective-permute-done.12
  104.8 5.0 %all-to-all-start.2 = ((bf16[8,20,4096]{2,1,0:T(8,128)(2,1)}), bf16[8,20,4096]{2,1,0:T(8,128)(2,1)S(1)}, u32[]{:S(2)}, u32[]{:S(2)}) async-start(bf16[8,20,4096]{2,1,0:T(8,128)(2,1)} %reshape.147), calls=%async_computation.2 | async-start | bytes 3145728 | tf_op jit(solution)/shard_map/all_to_all | solution.py:39
  115.4 17.3 %all-to-all-done.2 = bf16[8,20,4096]{2,1,0:T(8,128)(2,1)S(1)} async-done(((bf16[8,20,4096]{2,1,0:T(8,128)(2,1)}), bf16[8,20,4096]{2,1,0:T(8,128)(2,1)S(1)}, u32[]{:S(2)}, u32[]{:S(2)}) %all-to-all-start.2) | async-done | bytes 1310752 | tf_op jit(solution)/shard_map/all_to_all | solution.py:39
  133.7 2.1 reshape.148
  144.1 2.6 fusion.9
  148.6 23.8 %all_to_all.30 = bf16[8,20,4096]{2,1,0:T(8,128)(2,1)S(1)} all-to-all(bf16[8,20,4096]{2,1,0:T(8,128)(2,1)S(1)} %broadcast_in_dim.58), channel_id=1, replica_groups=mesh['zlo'=2,'x'=4,'core'=2,'zhi'=2,'y'=4] {'zhi','y'}, dimensions={0} | all-to-all | bytes 2621440 | tf_op jit(solution)/shard_map/all_to_all | solution.py:39
  172.7 2.8 collective-permute-start.13
  181.6 2.4 convolution_convert_fusion
  191.0 2.9 %collective-permute-start.19 = (bf16[384,512]{1,0:T(8,128)(2,1)S(1)}, bf16[384,512]{1,0:T(8,128)(2,1)S(1)}, u32[]{:S(2)}, u32[]{:S(2)}) collective-permute-start(bf16[384,512]{1,0:T(8,128)(2,1)S(1)} %get-tuple-element.30), channel_id=1, source_target_pairs={{0,48},{16,0},{32,16},{48,32},{1,49},{17,1},{33,17},{49,33},{2,50}... | collective-permute-start | bytes 1179656 | tf_op jit(solution)/shard_map/ppermute | solution.py:35
  194.0 2.7 collective-permute-start.25
  198.2 3.5 %collective-permute-done.22 = bf16[384,512]{1,0:T(8,128)(2,1)S(1)} collective-permute-done((bf16[384,512]{1,0:T(8,128)(2,1)S(1)}, bf16[384,512]{1,0:T(8,128)(2,1)S(1)}, u32[]{:S(2)}, u32[]{:S(2)}) %collective-permute-start.22) | collective-permute-done | bytes 393248 | tf_op jit(solution)/shard_map/ppermute | solution.py:31
  202.6 3.1 %collective-permute-start.21 = (bf16[384,512]{1,0:T(8,128)(2,1)}, bf16[384,512]{1,0:T(8,128)(2,1)}, u32[]{:S(2)}, u32[]{:S(2)}) collective-permute-start(bf16[384,512]{1,0:T(8,128)(2,1)} %pad_maximum_fusion.7), channel_id=1, source_target_pairs={{0,48},{16,0},{32,16},{48,32},{1,49},{17,1},{33,17},{49,33},{2,50}... | collective-permute-start | bytes 1179656 | tf_op jit(solution)/shard_map/ppermute | solution.py:35
  206.6 12.0 %collective-permute-done.16 = bf16[384,512]{1,0:T(8,128)(2,1)S(1)} collective-permute-done((bf16[384,512]{1,0:T(8,128)(2,1)S(1)}, bf16[384,512]{1,0:T(8,128)(2,1)S(1)}, u32[]{:S(2)}, u32[]{:S(2)}) %collective-permute-start.16) | collective-permute-done | bytes 393248 | tf_op jit(solution)/shard_map/ppermute | solution.py:31
  222.6 3.7 %all-to-all-start.4 = ((bf16[8,640,128]{2,1,0:T(8,128)(2,1)}), bf16[8,640,128]{2,1,0:T(8,128)(2,1)S(1)}, u32[]{:S(2)}, u32[]{:S(2)}) async-start(bf16[8,640,128]{2,1,0:T(8,128)(2,1)} %pad_maximum_fusion), calls=%async_computation.4 | async-start | bytes 2621440 | tf_op jit(solution)/shard_map/all_to_all | solution.py:39
  227.0 2.1 collective-permute-start.15
  229.0 2.5 add_convert_fusion.5
  231.5 2.7 collective-permute-start.26
  236.5 11.1 %collective-permute-done.17 = bf16[384,512]{1,0:T(8,128)(2,1)S(1)} collective-permute-done((bf16[384,512]{1,0:T(8,128)(2,1)}, bf16[384,512]{1,0:T(8,128)(2,1)S(1)}, u32[]{:S(2)}, u32[]{:S(2)}) %collective-permute-start.17) | collective-permute-done | bytes 393248 | tf_op jit(solution)/shard_map/ppermute | solution.py:31
  258.8 9.0 %all-to-all-start.5 = ((bf16[128,16,128]{2,1,0:T(8,128)(2,1)}), bf16[128,16,128]{2,1,0:T(8,128)(2,1)S(1)}, u32[]{:S(2)}, u32[]{:S(2)}) async-start(bf16[128,16,128]{2,1,0:T(8,128)(2,1)} %bitcast.27), calls=%async_computation.5 | async-start | bytes 1048576 | tf_op jit(solution)/shard_map/all_to_all | solution.py:39
  269.7 2.8 collective-permute-start.29
  275.7 4.5 %all-to-all-done.5 = bf16[128,16,128]{2,1,0:T(8,128)(2,1)S(1)} async-done(((bf16[128,16,128]{2,1,0:T(8,128)(2,1)}), bf16[128,16,128]{2,1,0:T(8,128)(2,1)S(1)}, u32[]{:S(2)}, u32[]{:S(2)}) %all-to-all-start.5) | async-done | bytes 524320 | tf_op jit(solution)/shard_map/all_to_all | solution.py:39
  (225 shorter events, 106.2 us)
Async XLA Ops:
  1.7 4.7 %collective-permute-start.2 = (bf16[512,256]{1,0:T(8,128)(2,1)S(1)}, bf16[512,256]{1,0:T(8,128)(2,1)S(1)}, u32[]{:S(2)}, u32[]{:S(2)}) collective-permute-start(bf16[512,256]{1,0:T(8,128)(2,1)S(1)} %get-tuple-element.45), channel_id=1, source_target_pairs={{0,8},{8,0},{1,9},{9,1},{2,10},{10,2},{3,11},{11,3},{4,12},{12,4},... | collective-permute-start | bytes 786440 | tf_op jit(solution)/shard_map/ppermute | solution.py:23
  8.3 19.7 %collective-permute-start.3 = (bf16[768,512]{1,0:T(8,128)(2,1)}, bf16[768,512]{1,0:T(8,128)(2,1)}, u32[]{:S(2)}, u32[]{:S(2)}) collective-permute-start(bf16[768,512]{1,0:T(8,128)(2,1)} %pad_maximum_fusion.1), channel_id=1, source_target_pairs={{0,48},{16,0},{32,16},{48,32},{1,49},{17,1},{33,17},{49,33},{2,50}... | collective-permute-start | bytes 2359304 | tf_op jit(solution)/shard_map/ppermute | solution.py:35
  10.9 22.3 %collective-permute-start.4 = (bf16[768,512]{1,0:T(8,128)(2,1)}, bf16[768,512]{1,0:T(8,128)(2,1)S(1)}, u32[]{:S(2)}, u32[]{:S(2)}) collective-permute-start(bf16[768,512]{1,0:T(8,128)(2,1)} %pad_maximum_fusion.1), channel_id=1, source_target_pairs={{0,16},{16,32},{32,48},{48,0},{1,17},{17,33},{33,49},{49,1},{2,18}... | collective-permute-start | bytes 2359304 | tf_op jit(solution)/shard_map/ppermute | solution.py:31
  10.9 23.1 %collective-permute-start.6 = (bf16[768,512]{1,0:T(8,128)(2,1)}, bf16[768,512]{1,0:T(8,128)(2,1)}, u32[]{:S(2)}, u32[]{:S(2)}) collective-permute-start(bf16[768,512]{1,0:T(8,128)(2,1)} %pad_maximum_fusion.1), channel_id=1, source_target_pairs={{0,64},{64,0},{1,65},{65,1},{2,66},{66,2},{3,67},{67,3},{4,68},{68... | collective-permute-start | bytes 2359304 | tf_op jit(solution)/shard_map/ppermute | solution.py:27
  18.8 28.8 %all-to-all-start = ((bf16[8,656,128]{2,1,0:T(8,128)(2,1)}), bf16[8,656,128]{2,1,0:T(8,128)(2,1)S(1)}, u32[]{:S(2)}, u32[]{:S(2)}) async-start(bf16[8,656,128]{2,1,0:T(8,128)(2,1)} %concatenate.106), calls=%async_computation | async-start | bytes 2686976 | tf_op jit(solution)/shard_map/all_to_all | solution.py:39
  29.8 33.2 %collective-permute-start.10 = (bf16[384,512]{1,0:T(8,128)(2,1)}, bf16[384,512]{1,0:T(8,128)(2,1)}, u32[]{:S(2)}, u32[]{:S(2)}) collective-permute-start(bf16[384,512]{1,0:T(8,128)(2,1)} %slice.292), channel_id=1, source_target_pairs={{0,48},{16,0},{32,16},{48,32},{1,49},{17,1},{33,17},{49,33},{2,50}... | collective-permute-start | bytes 1179656 | tf_op jit(solution)/shard_map/ppermute | solution.py:35
  34.0 23.9 %collective-permute-start.5 = (bf16[384,512]{1,0:T(8,128)(2,1)}, bf16[384,512]{1,0:T(8,128)(2,1)}, u32[]{:S(2)}, u32[]{:S(2)}) collective-permute-start(bf16[384,512]{1,0:T(8,128)(2,1)} %slice.283), channel_id=1, source_target_pairs={{0,16},{16,32},{32,48},{48,0},{1,17},{17,33},{33,49},{49,1},{2,18}... | collective-permute-start | bytes 1179656 | tf_op jit(solution)/shard_map/ppermute | solution.py:31
  34.0 39.5 %collective-permute-start.7 = (bf16[768,512]{1,0:T(8,128)(2,1)}, bf16[768,512]{1,0:T(8,128)(2,1)}, u32[]{:S(2)}, u32[]{:S(2)}) collective-permute-start(bf16[768,512]{1,0:T(8,128)(2,1)} %collective-permute-done.6), channel_id=1, source_target_pairs={{0,48},{16,0},{32,16},{48,32},{1,49},{17,1},{33,17},{49,33},{2,50}... | collective-permute-start | bytes 2359304 | tf_op jit(solution)/shard_map/ppermute | solution.py:35
  36.7 40.6 %collective-permute-start.8 = (bf16[768,512]{1,0:T(8,128)(2,1)}, bf16[768,512]{1,0:T(8,128)(2,1)}, u32[]{:S(2)}, u32[]{:S(2)}) collective-permute-start(bf16[768,512]{1,0:T(8,128)(2,1)} %collective-permute-done.6), channel_id=1, source_target_pairs={{0,16},{16,32},{32,48},{48,0},{1,17},{17,33},{33,49},{49,1},{2,18}... | collective-permute-start | bytes 2359304 | tf_op jit(solution)/shard_map/ppermute | solution.py:31
  51.4 17.9 %all-to-all-start.1 = ((bf16[8,20,2048]{2,1,0:T(8,128)(2,1)}), bf16[8,20,2048]{2,1,0:T(8,128)(2,1)S(1)}, u32[]{:S(2)}, u32[]{:S(2)}) async-start(bf16[8,20,2048]{2,1,0:T(8,128)(2,1)} %broadcast_in_dim.27), calls=%async_computation.1 | async-start | bytes 1572864 | tf_op jit(solution)/shard_map/all_to_all | solution.py:39
  69.4 24.6 %collective-permute-start = (bf16[160,2048]{1,0:T(8,128)(2,1)S(1)}, bf16[160,2048]{1,0:T(8,128)(2,1)S(1)}, u32[]{:S(2)}, u32[]{:S(2)}) collective-permute-start(bf16[160,2048]{1,0:T(8,128)(2,1)S(1)} %reshape.146), channel_id=1, source_target_pairs={{0,8},{8,0},{1,9},{9,1},{2,10},{10,2},{3,11},{11,3},{4,12},{12,4},... | collective-permute-start | bytes 1966088 | tf_op jit(solution)/shard_map/ppermute | solution.py:23
  74.6 15.3 %collective-permute-start.11 = (bf16[384,512]{1,0:T(8,128)(2,1)S(1)}, bf16[384,512]{1,0:T(8,128)(2,1)S(1)}, u32[]{:S(2)}, u32[]{:S(2)}) collective-permute-start(bf16[384,512]{1,0:T(8,128)(2,1)S(1)} %slice.296), channel_id=1, source_target_pairs={{0,48},{16,0},{32,16},{48,32},{1,49},{17,1},{33,17},{49,33},{2,50}... | collective-permute-start | bytes 1179656 | tf_op jit(solution)/shard_map/ppermute | solution.py:35
  78.3 11.5 %collective-permute-start.9 = (bf16[384,512]{1,0:T(8,128)(2,1)S(1)}, bf16[384,512]{1,0:T(8,128)(2,1)S(1)}, u32[]{:S(2)}, u32[]{:S(2)}) collective-permute-start(bf16[384,512]{1,0:T(8,128)(2,1)S(1)} %slice.288), channel_id=1, source_target_pairs={{0,16},{16,32},{32,48},{48,0},{1,17},{17,33},{33,49},{49,1},{2,18}... | collective-permute-start | bytes 1179656 | tf_op jit(solution)/shard_map/ppermute | solution.py:31
  104.8 28.0 %all-to-all-start.2 = ((bf16[8,20,4096]{2,1,0:T(8,128)(2,1)}), bf16[8,20,4096]{2,1,0:T(8,128)(2,1)S(1)}, u32[]{:S(2)}, u32[]{:S(2)}) async-start(bf16[8,20,4096]{2,1,0:T(8,128)(2,1)} %reshape.147), calls=%async_computation.2 | async-start | bytes 3145728 | tf_op jit(solution)/shard_map/all_to_all | solution.py:39
  172.7 5.5 %collective-permute-start.13 = (bf16[160,4096]{1,0:T(8,128)(2,1)S(1)}, bf16[160,4096]{1,0:T(8,128)(2,1)S(1)}, u32[]{:S(2)}, u32[]{:S(2)}) collective-permute-start(bf16[160,4096]{1,0:T(8,128)(2,1)S(1)} %reshape.151), channel_id=1, source_target_pairs={{0,8},{8,0},{1,9},{9,1},{2,10},{10,2},{3,11},{11,3},{4,12},{12,4},... | collective-permute-start | bytes 3932168 | tf_op jit(solution)/shard_map/ppermute | solution.py:23
  189.7 12.0 %collective-permute-start.22 = (bf16[384,512]{1,0:T(8,128)(2,1)S(1)}, bf16[384,512]{1,0:T(8,128)(2,1)S(1)}, u32[]{:S(2)}, u32[]{:S(2)}) collective-permute-start(bf16[384,512]{1,0:T(8,128)(2,1)S(1)} %pad_maximum_fusion.5), channel_id=1, source_target_pairs={{0,16},{16,32},{32,48},{48,0},{1,17},{17,33},{33,49},{49,1},{2,18}... | collective-permute-start | bytes 1179656 | tf_op jit(solution)/shard_map/ppermute | solution.py:31
  190.9 28.5 %collective-permute-start.14 = (bf16[160,2048]{1,0:T(8,128)(2,1)S(1)}, bf16[160,2048]{1,0:T(8,128)(2,1)S(1)}, u32[]{:S(2)}, u32[]{:S(2)}) collective-permute-start(bf16[160,2048]{1,0:T(8,128)(2,1)S(1)} %slice.367), channel_id=1, source_target_pairs={{0,8},{8,0},{1,9},{9,1},{2,10},{10,2},{3,11},{11,3},{4,12},{12,4},... | collective-permute-start | bytes 1966088 | tf_op jit(solution)/shard_map/ppermute | solution.py:23
  191.0 11.6 %collective-permute-start.19 = (bf16[384,512]{1,0:T(8,128)(2,1)S(1)}, bf16[384,512]{1,0:T(8,128)(2,1)S(1)}, u32[]{:S(2)}, u32[]{:S(2)}) collective-permute-start(bf16[384,512]{1,0:T(8,128)(2,1)S(1)} %get-tuple-element.30), channel_id=1, source_target_pairs={{0,48},{16,0},{32,16},{48,32},{1,49},{17,1},{33,17},{49,33},{2,50}... | collective-permute-start | bytes 1179656 | tf_op jit(solution)/shard_map/ppermute | solution.py:35
  194.0 32.3 %collective-permute-start.18 = (bf16[384,512]{1,0:T(8,128)(2,1)}, bf16[384,512]{1,0:T(8,128)(2,1)}, u32[]{:S(2)}, u32[]{:S(2)}) collective-permute-start(bf16[384,512]{1,0:T(8,128)(2,1)} %get-tuple-element.27), channel_id=1, source_target_pairs={{0,16},{16,32},{32,48},{48,0},{1,17},{17,33},{33,49},{49,1},{2,18}... | collective-permute-start | bytes 1179656 | tf_op jit(solution)/shard_map/ppermute | solution.py:31
  194.0 33.0 %collective-permute-start.25 = (bf16[384,512]{1,0:T(8,128)(2,1)}, bf16[384,512]{1,0:T(8,128)(2,1)}, u32[]{:S(2)}, u32[]{:S(2)}) collective-permute-start(bf16[384,512]{1,0:T(8,128)(2,1)} %get-tuple-element.28), channel_id=1, source_target_pairs={{0,48},{16,0},{32,16},{48,32},{1,49},{17,1},{33,17},{49,33},{2,50}... | collective-permute-start | bytes 1179656 | tf_op jit(solution)/shard_map/ppermute | solution.py:35
  201.7 16.9 %collective-permute-start.16 = (bf16[384,512]{1,0:T(8,128)(2,1)S(1)}, bf16[384,512]{1,0:T(8,128)(2,1)S(1)}, u32[]{:S(2)}, u32[]{:S(2)}) collective-permute-start(bf16[384,512]{1,0:T(8,128)(2,1)S(1)} %pad_maximum_fusion.9), channel_id=1, source_target_pairs={{0,16},{16,32},{32,48},{48,0},{1,17},{17,33},{33,49},{49,1},{2,18}... | collective-permute-start | bytes 1179656 | tf_op jit(solution)/shard_map/ppermute | solution.py:31
  202.6 28.9 %collective-permute-start.21 = (bf16[384,512]{1,0:T(8,128)(2,1)}, bf16[384,512]{1,0:T(8,128)(2,1)}, u32[]{:S(2)}, u32[]{:S(2)}) collective-permute-start(bf16[384,512]{1,0:T(8,128)(2,1)} %pad_maximum_fusion.7), channel_id=1, source_target_pairs={{0,48},{16,0},{32,16},{48,32},{1,49},{17,1},{33,17},{49,33},{2,50}... | collective-permute-start | bytes 1179656 | tf_op jit(solution)/shard_map/ppermute | solution.py:35
  218.6 10.5 %collective-permute-start.20 = (bf16[384,512]{1,0:T(8,128)(2,1)}, bf16[384,512]{1,0:T(8,128)(2,1)}, u32[]{:S(2)}, u32[]{:S(2)}) collective-permute-start(bf16[384,512]{1,0:T(8,128)(2,1)} %add_convert_fusion.6), channel_id=1, source_target_pairs={{0,48},{16,0},{32,16},{48,32},{1,49},{17,1},{33,17},{49,33},{2,50}... | collective-permute-start | bytes 1179656 | tf_op jit(solution)/shard_map/ppermute | solution.py:35
  219.4 14.8 %collective-permute-start.23 = (bf16[384,512]{1,0:T(8,128)(2,1)}, bf16[384,512]{1,0:T(8,128)(2,1)}, u32[]{:S(2)}, u32[]{:S(2)}) collective-permute-start(bf16[384,512]{1,0:T(8,128)(2,1)} %add_convert_fusion.4), channel_id=1, source_target_pairs={{0,16},{16,32},{32,48},{48,0},{1,17},{17,33},{33,49},{49,1},{2,18}... | collective-permute-start | bytes 1179656 | tf_op jit(solution)/shard_map/ppermute | solution.py:31
  222.6 28.7 %all-to-all-start.4 = ((bf16[8,640,128]{2,1,0:T(8,128)(2,1)}), bf16[8,640,128]{2,1,0:T(8,128)(2,1)S(1)}, u32[]{:S(2)}, u32[]{:S(2)}) async-start(bf16[8,640,128]{2,1,0:T(8,128)(2,1)} %pad_maximum_fusion), calls=%async_computation.4 | async-start | bytes 2621440 | tf_op jit(solution)/shard_map/all_to_all | solution.py:39
  226.3 22.1 %collective-permute-start.24 = (bf16[384,512]{1,0:T(8,128)(2,1)}, bf16[384,512]{1,0:T(8,128)(2,1)S(1)}, u32[]{:S(2)}, u32[]{:S(2)}) collective-permute-start(bf16[384,512]{1,0:T(8,128)(2,1)} %get-tuple-element.29), channel_id=1, source_target_pairs={{0,16},{16,32},{32,48},{48,0},{1,17},{17,33},{33,49},{49,1},{2,18}... | collective-permute-start | bytes 1179656 | tf_op jit(solution)/shard_map/ppermute | solution.py:31
  227.0 9.5 %collective-permute-start.15 = (bf16[384,512]{1,0:T(8,128)(2,1)}, bf16[384,512]{1,0:T(8,128)(2,1)S(1)}, u32[]{:S(2)}, u32[]{:S(2)}) collective-permute-start(bf16[384,512]{1,0:T(8,128)(2,1)} %pad_maximum_fusion.11), channel_id=1, source_target_pairs={{0,48},{16,0},{32,16},{48,32},{1,49},{17,1},{33,17},{49,33},{2,50}... | collective-permute-start | bytes 1179656 | tf_op jit(solution)/shard_map/ppermute | solution.py:35
  229.0 18.5 %collective-permute-start.17 = (bf16[384,512]{1,0:T(8,128)(2,1)}, bf16[384,512]{1,0:T(8,128)(2,1)S(1)}, u32[]{:S(2)}, u32[]{:S(2)}) collective-permute-start(bf16[384,512]{1,0:T(8,128)(2,1)} %add_convert_fusion.8), channel_id=1, source_target_pairs={{0,16},{16,32},{32,48},{48,0},{1,17},{17,33},{33,49},{49,1},{2,18}... | collective-permute-start | bytes 1179656 | tf_op jit(solution)/shard_map/ppermute | solution.py:31
  231.5 16.9 %collective-permute-start.26 = (bf16[384,512]{1,0:T(8,128)(2,1)S(1)}, bf16[384,512]{1,0:T(8,128)(2,1)S(1)}, u32[]{:S(2)}, u32[]{:S(2)}) collective-permute-start(bf16[384,512]{1,0:T(8,128)(2,1)S(1)} %get-tuple-element.26), channel_id=1, source_target_pairs={{0,48},{16,0},{32,16},{48,32},{1,49},{17,1},{33,17},{49,33},{2,50}... | collective-permute-start | bytes 1179656 | tf_op jit(solution)/shard_map/ppermute | solution.py:35
  250.6 17.7 %collective-permute-start.27 = (bf16[768,512]{1,0:T(8,128)(2,1)}, bf16[768,512]{1,0:T(8,128)(2,1)}, u32[]{:S(2)}, u32[]{:S(2)}) collective-permute-start(bf16[768,512]{1,0:T(8,128)(2,1)} %pad_maximum_fusion.2), channel_id=1, source_target_pairs={{0,64},{64,0},{1,65},{65,1},{2,66},{66,2},{3,67},{67,3},{4,68},{68... | collective-permute-start | bytes 2359304 | tf_op jit(solution)/shard_map/ppermute | solution.py:27
  258.8 21.5 %all-to-all-start.5 = ((bf16[128,16,128]{2,1,0:T(8,128)(2,1)}), bf16[128,16,128]{2,1,0:T(8,128)(2,1)S(1)}, u32[]{:S(2)}, u32[]{:S(2)}) async-start(bf16[128,16,128]{2,1,0:T(8,128)(2,1)} %bitcast.27), calls=%async_computation.5 | async-start | bytes 1048576 | tf_op jit(solution)/shard_map/all_to_all | solution.py:39
  269.7 5.0 %collective-permute-start.29 = (bf16[512,256]{1,0:T(8,128)(2,1)S(1)}, bf16[512,256]{1,0:T(8,128)(2,1)S(1)}, u32[]{:S(2)}, u32[]{:S(2)}) collective-permute-start(bf16[512,256]{1,0:T(8,128)(2,1)S(1)} %get-tuple-element.44), channel_id=1, source_target_pairs={{0,8},{8,0},{1,9},{9,1},{2,10},{10,2},{3,11},{11,3},{4,12},{12,4},... | collective-permute-start | bytes 786440 | tf_op jit(solution)/shard_map/ppermute | solution.py:23
  (31 other events, 173.7 us)

commit v2 on v0

v2 whole, which is shorter than its diff:
```python
import jax
import jax.numpy as jnp
from jax import lax
from jax.experimental import pallas as pl
from jax.experimental.pallas import tpu as pltpu
from jax.sharding import Mesh, PartitionSpec as P

BF = jnp.bfloat16
F32 = jnp.float32
DP = ("zlo", "x", "core")
FEAT = ("zhi", "y")
ALL = DP + FEAT
EPS = 1e-05
FWD = [(i, (i + 1) % 4) for i in range(4)]
BWD = [(i, (i + 3) % 4) for i in range(4)]
SWAP = [(0, 1), (1, 0)]
OWN, CORE, CHIP = 20, 160, 320


def sibling(a):
    return lax.ppermute(a, "core", SWAP)


def across(a):
    return lax.ppermute(a, "zlo", SWAP)


def right(a):
    return lax.ppermute(a, "x", FWD)


def left(a):
    return lax.ppermute(a, "x", BWD)


def exchange(a, axes):
    return lax.all_to_all(a, axes, 0, 0, tiled=True)


def together(*arrays):
    return lax.optimization_barrier(arrays)


def dot(a, b, dims):
    return lax.dot_general(a, b, (dims, ((), ())), preferred_element_type=F32)


def shape(dims, dtype=BF):
    return jax.ShapeDtypeStruct(dims, dtype)


def call(body, outs, *args, scratch=(), scalars=0, remote_in=0, remote_out=0, room=16):
    whole = pl.BlockSpec(memory_space=pltpu.VMEM)
    small = pl.BlockSpec(memory_space=pltpu.SMEM)
    there = pl.BlockSpec(memory_space=pl.ANY)
    return pl.pallas_call(
        body,
        out_shape=outs,
        in_specs=[small] * scalars
        + [whole] * (len(args) - scalars - remote_in)
        + [there] * remote_in,
        out_specs=[there] * remote_out + [whole] * (len(outs) - remote_out),
        scratch_shapes=list(scratch),
        compiler_params=pltpu.CompilerParams(vmem_limit_bytes=room * 1024 * 1024),
    )(*args)


def one_where(dims, test):
    rows = lax.broadcasted_iota(jnp.int32, dims, 0)
    cols = lax.broadcasted_iota(jnp.int32, dims, 1)
    return test(rows, cols).astype(F32).astype(BF)


def many(start, size):
    return pl.ds(pl.multiple_of(start, size), size)


def halves(core, width):
    return many(core * width, width), many((1 - core) * width, width)


def chip_rows(core):
    return one_where((256, 128), lambda r, c: r == (c % 16) * 16 + core * 8 + c // 16)


def send_kernel(place, up, down, sent, sems):
    unused, other = halves(place[0], 512)
    low, high = many((1 - place[0]) * 512, 256), many((1 - place[0]) * 512 + 256, 256)
    copies = [
        pltpu.make_async_copy(up.at[:, other], sent.at[pl.ds(0, 128)], sems.at[0]),
        pltpu.make_async_copy(
            down.at[low], sent.at[pl.ds(128, 256), pl.ds(0, 256)], sems.at[1]
        ),
        pltpu.make_async_copy(
            down.at[high], sent.at[pl.ds(128, 256), pl.ds(256, 256)], sems.at[2]
        ),
    ]
    for copy in copies:
        copy.start()
    for copy in copies:
        copy.wait()


def message_kernel(place, proj, mix, token, emb, message, sems):
    copy = pltpu.make_async_copy(emb, message.at[:, pl.ds(0, 320)], sems.at[0])
    copy.start()
    here = one_where((16, 128), lambda n, lane: lane == place[3] * 16 + n)
    proj_rows = dot(proj[...], here, ((0,), (0,))).astype(BF)
    shift = one_where((16, 12), lambda u, c: u == c + 4)
    mix_rows = dot(shift, mix[...], ((1,), (0,))).astype(BF)
    for group in range(8):
        message[group, 320:336] = proj_rows
        message[group, 336:352] = mix_rows
    copy.wait()


def piece_kernel(place, got, up, down, piece, mine_up, mine_down, sems):
    core = place[0]
    mine, unused = halves(core, 512)
    copies = [
        pltpu.make_async_copy(up.at[:, mine], mine_up, sems.at[0]),
        pltpu.make_async_copy(down.at[mine], mine_down, sems.at[1]),
    ]
    for copy in copies:
        copy.start()
    mine_at, other_at = halves(core, 256)
    piece[16:32, :, other_at] = got[128:, :256].reshape(16, 16, 256)
    piece[32:, :, other_at] = got[128:, 256:].reshape(16, 16, 256)
    rows = dot(chip_rows(1 - core), got[:128], ((1,), (0,)))
    copies[0].wait()
    rows += dot(chip_rows(core), mine_up[...], ((1,), (0,)))
    piece[:16] = rows.astype(BF).reshape(16, 16, 512)
    copies[1].wait()
    piece[16:, :, mine_at] = mine_down[...].reshape(32, 16, 256)


def total_of(refs):
    total = refs[0][...].astype(F32)
    for ref in refs[1:]:
        total += ref[...].astype(F32)
    return total.astype(BF)


def add_kernel(*refs):
    refs[-1][...] = total_of(refs[:-1])


def add(*terms):
    return call(add_kernel, [shape(terms[0].shape)], *terms)[0]


def add_both_kernel(own, from_right, relayed, minus, returned, over, on):
    over[...] = total_of((own, from_right, relayed))
    on[...] = total_of((minus, returned))


def join_kernel(own, got, layer, out):
    out[:, :16] = total_of((own, got))
    out[:, 16:] = layer[...]


def split_kernel(place, own, one, two, three, up_kept, down_kept, sent):
    core = place[0]
    total = total_of((own, one, two, three))
    up, down = total[:16].reshape(256, 512), total[16:].reshape(512, 512)
    up_kept[...] = dot(chip_rows(core), up, ((0,), (0,))).astype(BF)
    sent[:128] = dot(chip_rows(1 - core), up, ((0,), (0,))).astype(BF)
    first, second = down[:, :256], down[:, 256:]
    down_kept[...] = jnp.where(core == 0, first, second)
    other = jnp.where(core == 0, second, first)
    sent[128:, :256] = other[:256]
    sent[128:, 256:] = other[256:]


def finish_kernel(place, up_kept, down_kept, got, up, down):
    mine, other = halves(place[0], 512)
    up[:, mine] = up_kept[...]
    up[:, other] = got[:128]
    down[mine, :] = down_kept[...]
    down[other, :] = jnp.concatenate([got[128:, :256], got[128:, 256:]], 0)


def unpack(ref, width, start, size):
    quarter = start // (width // 4)
    tail = width + start - quarter * (width // 4)
    rest = ref[:, :16, tail : tail + size].astype(F32)
    rest = [rest[f, 4 * quarter : 4 * quarter + 4] for f in range(8)]
    rest = jnp.concatenate(rest, 0).astype(BF)
    return [ref[:, :16, start : start + size].reshape(128, size), rest]


def pack(part, ref, tails, width, start, size):
    quarter = start // (width // 4)
    tail = start - quarter * (width // 4)
    ref[:, :, start : start + size] = part[:128].astype(BF).reshape(8, 16, size)
    for f in range(8):
        row = 16 * f + 4 * quarter
        tails[row : row + 4, tail : tail + size] = part[128 + 4 * f : 132 + 4 * f]
    if quarter == 3:
        rest = tails[:, tail : tail + size].astype(BF)
        ref[:, :, width + tail : width + tail + size] = rest.reshape(8, 16, size)


def chip_of(place, r):
    return jnp.bitwise_xor(place[1], r // 4) * 4 + lax.rem(place[2] + r % 4, 4)


def second_part(piece):
    if len(piece) == 1:
        return piece[0][16:].reshape(512, 512)
    low, high = piece
    return jnp.concatenate([low[16:].reshape(128, 512), high[...].reshape(384, 512)], 0)


def pieces_of(refs, late, sems):
    a, b, c, d, e, f, g, h, low, high = refs
    copies = [
        pltpu.make_async_copy(low, late.at[pl.ds(0, 24)], sems.at[0]),
        pltpu.make_async_copy(high, late.at[pl.ds(24, 24)], sems.at[1]),
    ]
    for copy in copies:
        copy.start()
    return [(0, [a]), (1, [b]), (2, [c, d]), (3, [e]), (4, [f]), (5, [g]), (7, [h]), (6, [late])], copies


def features_kernel(message, cot, payload, normal, rstds, tails):
    for b in range(OWN):
        payload[:, 16:, 128 * b : 128 * b + 128] = cot[:, 16 * b : 16 * b + 16]
    proj_w = message[0, 320:336].astype(F32)
    for f in range(1, 8):
        proj_w += message[f, 320:336].astype(F32)
    proj_w = proj_w.astype(BF)

    def sample(b, carry):
        tokens = message[:, many(b * 16, 16)].reshape(128, 128)
        proj = dot(proj_w, tokens, ((1,), (0,))).astype(BF)
        inter = dot(proj, tokens, ((1,), (1,)))
        cent = inter - jnp.sum(inter, keepdims=True) * (1.0 / 2048)
        rstd = lax.rsqrt(jnp.sum(cent * cent, keepdims=True) * (1.0 / 2048) + EPS)
        normal[b] = cent * rstd
        rstds[b] = jnp.broadcast_to(rstd, (16, 128))
        return carry

    lax.fori_loop(0, OWN, sample, 0, unroll=5)
    for k in range(16):
        block = normal[:, k, :]
        quarter, tail = k // 4 * 4, k % 4 * 128
        tails[quarter : quarter + 4, tail : tail + 128] = block[16:]
        block = block[:16].astype(BF)
        for f in range(8):
            payload[f, :16, 128 * k : 128 * k + 128] = block
    block = tails[...].astype(BF)
    for f in range(8):
        payload[f, :16, 2048:] = block


def forward_kernel(place, own, sib, *refs):
    hidden, pre, rows, held, fmb_own, fmb_sib, tail_own, tail_sib, late, sems = refs[10:]
    weights, copies = pieces_of(refs[:10], late, sems)
    for r, piece in weights:
        if r == 6:
            for copy in copies:
                copy.wait()
        held[:, many(chip_of(place, r) * 16, 16)] = piece[0][:16]
    total = jnp.zeros((CHIP, 512), F32)
    for j in range(8):
        part = unpack(own, 2048, 256 * j, 256) + unpack(sib, 2048, 256 * j, 256)
        part = jnp.concatenate(part, 0)
        rows[:, 256 * j : 256 * j + 256] = part
        matrix = held[2 * j : 2 * j + 2].reshape(256, 512)
        total += dot(part, matrix, ((1,), (0,)))
    pre[...] = total
    act = (total / (1.0 + jnp.exp(-total))).astype(BF)
    hidden[...] = act
    for r, piece in sorted(weights, key=lambda item: item[0]):
        part = dot(act, second_part(piece), ((1,), (0,)))
        pack(part[:CORE], fmb_own, tail_own, 4096, 512 * r, 512)
        pack(part[CORE:], fmb_sib, tail_sib, 4096, 512 * r, 512)


def backward_kernel(place, d_own, d_sib, rows, hidden, pre, held, *refs):
    grads, (dn_own, dn_sib) = refs[10:18], refs[18:20]
    d_rows, made, made_down, tail_own, tail_sib, late, sems, out_sems = refs[20:]
    weights, copies = pieces_of(refs[:10], late, sems)
    total = jnp.zeros((CHIP, 512), F32)
    for r, piece in weights:
        part = unpack(d_own, 4096, 512 * r, 512) + unpack(d_sib, 4096, 512 * r, 512)
        part = jnp.concatenate(part, 0)
        d_rows[:, 512 * r : 512 * r + 512] = part
        if r == 6:
            for copy in copies:
                copy.wait()
        total += dot(part, second_part(piece), ((1,), (1,)))
    sends = []

    def send(source, there, sem):
        sends.append(pltpu.make_async_copy(source, there, out_sems.at[sem]))
        sends[-1].start()

    act = hidden[...].T
    for r in (6, 7, 2, 5, 4, 1, 3, 0):
        part = dot(act, d_rows[:, 512 * r : 512 * r + 512], ((1,), (0,)))
        made_down[r] = part.astype(BF).reshape(32, 16, 512)
        send(made_down.at[r], grads[r].at[pl.ds(16, 32)], 8 + r)
    sig = 1.0 / (1.0 + jnp.exp(-pre[...]))
    d_pre = (total * (sig * (1.0 + pre[...] * (1.0 - sig)))).astype(BF)
    for j in range(8):
        part = dot(rows[:, 256 * j : 256 * j + 256], d_pre, ((0,), (0,)))
        made[2 * j : 2 * j + 2] = part.astype(BF).reshape(2, 128, 512)
    for r in range(8):
        send(made.at[:, many(chip_of(place, r) * 16, 16)], grads[r].at[pl.ds(0, 16)], r)
    for j in range(8):
        part = dot(d_pre, held[2 * j : 2 * j + 2].reshape(256, 512), ((1,), (1,)))
        pack(part[:CORE], dn_own, tail_own, 2048, 256 * j, 256)
        pack(part[CORE:], dn_sib, tail_sib, 2048, 256 * j, 256)
    for copy in sends:
        copy.wait()


def norm_kernel(
    place, parts, message, cot, gain, layer, d_fmb, mix_part, gain_part, fm, grad, tails
):
    def added(cols):
        total = parts[0, :, cols].astype(F32)
        for f in range(1, 8):
            total += parts[f, :, cols].astype(F32)
        return total

    fm[...] = jnp.zeros_like(fm)
    tails[...] = added(slice(4096, 5120))
    for r in range(8):
        main = added(slice(512 * r, 512 * r + 512))
        quarter, tail = r // 2 * 4, r % 2 * 512
        for u in range(4):
            at = slice(128 * u, 128 * u + 128)
            fm[:16, chip_of(place, r), u, :] = main[:, at]
            at = slice(tail + 128 * u, tail + 128 * u + 128)
            fm[16:, chip_of(place, r), u, :] = tails[quarter : quarter + 4, at]
    mix_part[...] = jnp.zeros_like(mix_part)
    gain_part[...] = jnp.zeros_like(gain_part)
    scale = gain[...]
    mixing = message[:, 336:352].reshape(128, 128)

    def mean(a):
        return jnp.sum(a, axis=1, keepdims=True) * (1.0 / 128)

    def sample(b, carry):
        at = many(b * 16, 16)
        tokens = message[:, at].reshape(128, 128)
        cotan = cot[:, 16:, many(b * 128, 128)].reshape(128, 128).astype(F32)
        lcb = dot(mixing, tokens, ((1,), (0,)))
        summed = lcb + fm[b].reshape(128, 128) + tokens.astype(F32)
        cent = summed - mean(summed)
        rstd = lax.rsqrt(mean(cent * cent) + EPS)
        normal = cent * rstd
        layer[:, :, many(b * 128, 128)] = (normal * scale).astype(BF).reshape(8, 16, 128)
        gain_part[...] += jnp.sum((cotan * normal).reshape(16, 8, 128), axis=0)
        dnorm = cotan * scale
        dsum = rstd * (dnorm - mean(dnorm) - normal * mean(dnorm * normal))
        grad[b] = dsum.reshape(8, 16, 128)
        mix_part[...] += dot(dsum.astype(BF), tokens, ((1,), (1,)))
        return carry

    lax.fori_loop(0, OWN, sample, 0, unroll=5)
    for r in range(8):
        quarter, tail = r // 2 * 4, r % 2 * 512
        for u in range(4):
            block = grad[:, chip_of(place, r), u, :]
            at = slice(tail + 128 * u, tail + 128 * u + 128)
            tails[quarter : quarter + 4, at] = block[16:]
            block = block[:16].astype(BF)
            for f in range(8):
                d_fmb[f, :, 512 * r + 128 * u : 512 * r + 128 * u + 128] = block
    block = tails[...].astype(BF)
    for f in range(8):
        d_fmb[f, :, 4096:] = block


def last_kernel(back, normal, rstds, message, mix_part, gain_part, last, grad, proj_part):
    total = back[0, :16].astype(F32)
    for f in range(1, 8):
        total += back[f, :16].astype(F32)
    for k in range(16):
        quarter, tail = k // 4 * 4, 2048 + k % 4 * 128
        grad[:16, k, :] = total[:, 128 * k : 128 * k + 128]
        grad[16:, k, :] = total[quarter : quarter + 4, tail : tail + 128]
    proj_part[...] = jnp.zeros_like(proj_part)

    def sample(b, carry):
        tokens = message[:, many(b * 16, 16)].reshape(128, 128)
        d_normed, norm = grad[b], normal[b]
        first = jnp.sum(d_normed, keepdims=True) * (1.0 / 2048)
        second = jnp.sum(d_normed * norm, keepdims=True) * (1.0 / 2048)
        d_inter = rstds[b] * (d_normed - first - norm * second)
        d_proj = dot(d_inter.astype(BF), tokens, ((1,), (0,)))
        proj_part[...] += dot(d_proj.astype(BF), tokens, ((1,), (1,)))
        return carry

    lax.fori_loop(0, OWN, sample, 0, unroll=5)
    repeat = one_where((16, 128), lambda k, lane: lane % 16 == k)
    spread = dot(proj_part[...].astype(BF), repeat, ((0,), (0,)))
    token = lax.broadcasted_iota(jnp.int32, (128, 128), 0)
    lane = lax.broadcasted_iota(jnp.int32, (128, 128), 1)
    spread = jnp.where(token % 8 == lane // 16, spread, 0.0).astype(BF)
    collect = one_where(
        (128, 128), lambda r, n: (r % 16 < 2) & (n // 8 == (r // 16) * 2 + r % 16)
    )
    rows = dot(collect, spread, ((1,), (0,)))
    gain = jnp.sum(gain_part[...], axis=0, keepdims=True)
    rows += jnp.where(token % 16 == 2, jnp.broadcast_to(gain, (128, 128)), 0.0)
    rows += jnp.where(token % 16 >= 4, mix_part[...], 0.0)
    rows = rows.astype(BF).reshape(8, 16, 128)
    for d in range(16):
        last[8 * d : 8 * d + 8] = rows


def unfold_kernel(back, layer):
    for b in range(OWN):
        layer[:, b] = back[:, 16:, 128 * b : 128 * b + 128]


def finish_weights(place, own, from_left, relayed, other):
    up_kept, down_kept, sent = call(
        split_kernel,
        [shape((128, 512)), shape((512, 256)), shape((384, 512))],
        place,
        own,
        from_left,
        relayed,
        other,
        scalars=1,
    )
    return call(
        finish_kernel,
        [shape((128, 1024)), shape((1024, 256))],
        place,
        up_kept,
        down_kept,
        sibling(sent),
        scalars=1,
    )


def per_device(embeddings, proj_weight, up_weight, down_weight, mix_weight, out_gain, cotangent):
    place = jnp.stack(
        [lax.axis_index(axis) for axis in ("core", "zlo", "x")]
        + [lax.axis_index("zhi") * 4 + lax.axis_index("y")]
    ).astype(jnp.int32)
    (sent,) = call(
        send_kernel,
        [shape((384, 512))],
        place,
        up_weight,
        down_weight,
        scratch=[pltpu.SemaphoreType.DMA((3,))],
        scalars=1,
        remote_in=2,
        room=60,
    )
    (mine,) = call(
        piece_kernel,
        [shape((48, 16, 512))],
        place,
        sibling(sent),
        up_weight,
        down_weight,
        scratch=[
            pltpu.VMEM((128, 512), BF),
            pltpu.VMEM((512, 256), BF),
            pltpu.SemaphoreType.DMA((2,)),
        ],
        scalars=1,
        remote_in=2,
        room=60,
    )
    other = across(mine)
    near_left, near_right = right(mine), left(mine)
    (message,) = call(
        message_kernel,
        [shape((8, 352, 128))],
        place,
        proj_weight,
        mix_weight.T,
        sibling(mine[0]),
        embeddings.reshape(8, 320, 128),
        scratch=[pltpu.SemaphoreType.DMA((1,))],
        scalars=1,
        remote_in=1,
        room=60,
    )
    message = exchange(message, FEAT)
    message, near_left, near_right, other = together(message, near_left, near_right, other)
    other_left, other_right = right(other), left(other)
    far_low, far_high = right(near_left[:24]), left(near_right[24:])

    payload, normal1, rstd1 = call(
        features_kernel,
        [shape((8, 32, 2560)), shape((OWN, 16, 128), F32), shape((OWN, 16, 128), F32)],
        message,
        cotangent.reshape(8, 320, 128),
        scratch=[pltpu.VMEM((16, 512), F32)],
    )
    payload, far_low, far_high = together(payload, far_low, far_high)
    normed = exchange(payload, FEAT)
    normed, other_left, other_right = together(normed, other_left, other_right)
    other_low, other_high = right(other_left[:24]), left(other_right[24:])
    weights = [mine, near_right, far_low, far_high, near_left]
    weights += [other, other_right, other_left, other_low, other_high]
    hidden, pre, rows, first, fmb_own, fmb_sib = call(
        forward_kernel,
        [
            shape((CHIP, 512)),
            shape((CHIP, 512), F32),
            shape((CHIP, 2048)),
            shape((16, 128, 512)),
            shape((8, 16, 5120)),
            shape((8, 16, 5120)),
        ],
        place,
        normed,
        sibling(normed),
        *weights,
        scratch=[
            pltpu.VMEM((128, 1024), F32),
            pltpu.VMEM((128, 1024), F32),
            pltpu.VMEM((48, 16, 512), BF),
            pltpu.SemaphoreType.DMA((2,)),
        ],
        scalars=1,
        remote_in=2,
    )
    fmb = exchange(add(fmb_own, sibling(fmb_sib)), FEAT)

    layer_out, d_fmb, mix_part, gain_part = call(
        norm_kernel,
        [
            shape((8, 16, 2560)),
            shape((8, 16, 5120)),
            shape((128, 128), F32),
            shape((8, 128), F32),
        ],
        place,
        fmb,
        message,
        normed,
        out_gain.reshape(1, 128),
        scratch=[
            pltpu.VMEM((OWN, 8, 16, 128), F32),
            pltpu.VMEM((OWN, 8, 16, 128), F32),
            pltpu.VMEM((16, 1024), F32),
        ],
        scalars=1,
    )

    d_fmb = exchange(d_fmb, FEAT)
    outs = call(
        backward_kernel,
        [shape((48, 16, 512))] * 8 + [shape((8, 16, 2560))] * 2,
        place,
        d_fmb,
        sibling(d_fmb),
        rows,
        hidden,
        pre,
        first,
        *weights,
        scratch=[
            pltpu.VMEM((CHIP, 4096), BF),
            pltpu.VMEM((16, 128, 512), BF),
            pltpu.VMEM((8, 32, 16, 512), BF),
            pltpu.VMEM((128, 512), F32),
            pltpu.VMEM((128, 512), F32),
            pltpu.VMEM((48, 16, 512), BF),
            pltpu.SemaphoreType.DMA((2,)),
            pltpu.SemaphoreType.DMA((16,)),
        ],
        scalars=1,
        remote_in=2,
        remote_out=8,
        room=24,
    )
    own0, plus0, far0, minus0, own1, plus1, far1, minus1, dn_own, dn_sib = outs

    from_left, from_right = right(far1), left(minus1)
    (back,) = call(join_kernel, [shape((8, 32, 2560))], dn_own, sibling(dn_sib), layer_out)
    back = exchange(back, FEAT)
    from_left, from_right, far0 = together(from_left, from_right, far0)
    relayed, returned = right(add(plus1, from_left)), left(far0)
    (last,) = call(
        last_kernel,
        [shape((128, 16, 128))],
        back,
        normal1,
        rstd1,
        message,
        mix_part,
        gain_part,
        scratch=[pltpu.VMEM((OWN, 16, 128), F32), pltpu.VMEM((16, 128), F32)],
    )
    relayed, returned, plus0, last = together(relayed, returned, plus0, last)
    from_left = right(plus0)
    over, on = call(
        add_both_kernel,
        [shape((48, 16, 512))] * 2,
        own1,
        from_right,
        relayed,
        minus0,
        returned,
    )
    other, relayed = across(over), left(on)
    last = exchange(last, ALL)
    up_grad, down_grad = finish_weights(place, own0, from_left, relayed, other)
    up_grad, down_grad, last = together(up_grad, down_grad, last)
    (layer_out,) = call(unfold_kernel, [shape((8, OWN, 16, 128))], back)
    last = jnp.sum(last.astype(F32), 0)
    proj_grad = last[:2].reshape(16, 16)
    mix_grad = last[4:].T
    gain_grad = last[2]
    layer_out = layer_out.reshape(160, 16, 128)
    return (layer_out, gain_grad, mix_grad, up_grad, down_grad, proj_grad)


def solution(mesh):
    grid = Mesh(mesh.devices.reshape(2, 4, 2, 2, 4), ALL)
    placed = (
        P(DP, FEAT, None),
        P(FEAT, None),
        P(DP, FEAT),
        P(FEAT, DP),
        P(None, FEAT),
        P(),
        P(DP, FEAT, None),
    )
    return jax.shard_map(
        per_device,
        mesh=grid,
        in_specs=placed,
        out_specs=(
            P(DP, FEAT, None),
            P(),
            P(None, FEAT),
            P(DP, FEAT),
            P(FEAT, DP),
            P(FEAT, None),
        ),
        check_vma=False,
    )
```

time: 588 us -> 259 us (0.44)
  waiting for transfers between devices: 318 us -> 75 us
  blocking collectives: 190 us -> 67.5 us
  starting transfers between devices: 0.6 us -> 50 us
  Pallas kernels: 0 us -> 46.1 us
  matrix products: 44.4 us -> 0 us
  between operations: 15.7 us -> 0.97 us
  local copies, waits for them, and re-layouts: 6.29 us -> 17.2 us
  other arithmetic: 9.64 us -> 0.75 us
    psum x4 -> x0, blocking collectives: 160 us -> none  [the longest x1 72.1 us: per_device(): gain_grad = lax.psum(jnp.sum(cotan * normal2, axis=(0, 1)), ('dp', 'feat'))]
    reduce_scatter x4 -> x0, waiting for transfers between devices: 128 us -> none  [the longest x1 69.9 us: per_device(): lax.psum_scatter(normed_part.astype(jnp.bfloat16), 'feat', scatter_dimens...]
    all_gather x4 -> x0, waiting for transfers between devices: 104 us -> none  [the longest x1 54.6 us: per_device(): all_tokens = lax.all_gather(embeddings, 'feat', axis=1, tiled=True)]
    psum x2 -> x0, waiting for transfers between devices: 84.1 us -> none  [the longest x1 84.1 us: per_device(): proj = lax.psum(partial_value.astype(jnp.bfloat16), 'feat')]
    ppermute x0 -> x23, waiting for transfers between devices: none -> 71 us  [the longest x7 37.1 us: right(): return lax.ppermute(a, 'x', FWD)]
    all_to_all x0 -> x3, blocking collectives: none -> 67.5 us  [exchange(): return lax.all_to_all(a, axes, 0, 0, tiled=True)]
    pallas_call x0 -> x15, Pallas kernels: none -> 46.1 us  [call(): pl.pallas_call(body, out_shape=outs, in_specs=[small] * scalars + [whole]...]
    dot_general x12 -> x0, matrix products: 44.4 us -> none  [the longest x1 6.96 us: per_device(): jnp.dot(hidden_b.T, d_fmb_full, preferred_element_type=jnp.float32)]
  transfers between devices with their start and end apart: 10 -> 26, of which waited for: 6 -> 16; matrix products, arithmetic and copies ran while one was open for 6% -> 1% of each run, Pallas kernels for 0% -> 7%
where the time goes in v2:
time: 259 us; the launch traced here: 258 us
  waiting for transfers between devices  75 us (29%)
  blocking collectives  67.5 us (26%)
  starting transfers between devices  50 us (19%)
  Pallas kernels  46.1 us (18%)
  local copies, waits for them, and re-layouts  17.2 us (7%)
    all_to_all x3, blocking collectives, exchange(): return lax.all_to_all(a, axes, 0, 0, tiled=True)  67.5 us
    pallas_call x15, Pallas kernels, call(): pl.pallas_call(body, out_shape=outs, in_specs=[small] * scalars + [whole]...  46.1 us
    ppermute x7, waiting for transfers between devices, right(): return lax.ppermute(a, 'x', FWD)  37.1 us
    ppermute x7, waiting for transfers between devices, left(): return lax.ppermute(a, 'x', BWD)  22.1 us
    all_to_all x3, starting transfers between devices, exchange(): return lax.all_to_all(a, axes, 0, 0, tiled=True)  15.9 us
    ppermute x7, starting transfers between devices, left(): return lax.ppermute(a, 'x', BWD)  15.5 us
    ppermute x7, starting transfers between devices, sibling(): return lax.ppermute(a, 'core', SWAP)  14.7 us
    unnamed x60, local copies, waits for them, and re-layouts  12.6 us
  transfers between devices with their start and end apart: 26, of which 16 were waited for; matrix products, arithmetic and copies ran while one was open for 1% of the time, Pallas kernels for 7%

profile of v2, /device:TPU:1, one launch (start us, length us, event | category | flops | bytes accessed | tf_op | source)
XLA Modules:
  0.0 257.6 jit_solution(11209118560112418399)
XLA Ops:
  1.3 2.5 shard_map.118
  7.5 3.1 %shard_map.119.refs_0_ = bf16[48,16,512]{2,1,0:T(8,128)(2,1)} custom-call(s32[4]{0:T(128)} %pad_add_fusion.place, bf16[384,512]{1,0:T(8,128)(2,1)} %copy-done.28, bf16[128,1024]{1,0:T(8,128)(2,1)} %up.3, bf16[1024,256]{1,0:T(8,128)(2,1)} %down.3), custom_call_target="tpu_custom_call" | custom-call | tf_op jit(solution)/shard_map/pallas_call | solution.py:56
  12.5 2.5 collective-permute-start.3
  18.1 2.8 %shard_map.120 = bf16[8,352,128]{2,1,0:T(8,128)(2,1)} custom-call(s32[4]{0:T(128)} %pad_add_fusion.place, bf16[16,16]{1,0:T(8,128)(2,1)} %proj.1, bf16[12,128]{1,0:T(8,128)(2,1)} %bitcast.19, bf16[16,512]{1,0:T(8,128)(2,1)} %copy-done.29, bf16[8,320,128]{2,1,0:T(8,128)(2,1)} %bitcast.17), custom_call_target="tpu_custom_call" | custom-call | tf_op jit(solution)/shard_map/pallas_call | solution.py:56
  20.9 20.4 %all_to_all.30.message = bf16[8,352,128]{2,1,0:T(8,128)(2,1)S(1)} all-to-all(bf16[8,352,128]{2,1,0:T(8,128)(2,1)} %shard_map.120), channel_id=1, replica_groups=mesh['zlo'=2,'x'=4,'core'=2,'zhi'=2,'y'=4] {'zhi','y'}, dimensions={0} | all-to-all | bytes 1441792 | tf_op jit(solution)/shard_map/all_to_all | solution.py:37
  41.4 3.0 %collective-permute-start.6 = (bf16[24,16,512]{2,1,0:T(8,128)(2,1)S(1)}, bf16[24,16,512]{2,1,0:T(8,128)(2,1)S(1)}, u32[]{:S(2)}, u32[]{:S(2)}) collective-permute-start(bf16[24,16,512]{2,1,0:T(8,128)(2,1)S(1)} %slice.26), channel_id=1, source_target_pairs={{0,48},{16,0},{32,16},{48,32},{1,49},{17,1},{33,17},{49,33},{2,50}... | collective-permute-start | bytes 1179656 | tf_op jit(solution)/shard_map/ppermute | solution.py:33
  44.4 4.2 %shard_map.121 = (bf16[8,32,2560]{2,1,0:T(8,128)(2,1)S(1)}, f32[20,16,128]{2,1,0:T(8,128)S(1)}, f32[20,16,128]{2,1,0:T(8,128)S(1)}) custom-call(bf16[8,352,128]{2,1,0:T(8,128)(2,1)S(1)} %all_to_all.30.message, bf16[8,320,128]{2,1,0:T(8,128)(2,1)S(1)} %bitcast.15), custom_call_target="tpu_custom_call" | custom-call | tf_op jit(solution)/shard_map/pallas_call | solution.py:56
  51.3 3.1 %collective-permute-done.5.refs_2_ = bf16[24,16,512]{2,1,0:T(8,128)(2,1)S(1)} collective-permute-done((bf16[24,16,512]{2,1,0:T(8,128)(2,1)S(1)}, bf16[24,16,512]{2,1,0:T(8,128)(2,1)S(1)}, u32[]{:S(2)}, u32[]{:S(2)}) %collective-permute-start.5) | collective-permute-done | bytes 393248 | tf_op jit(solution)/shard_map/ppermute | solution.py:29
  55.1 3.9 %all-to-all-start.1 = ((bf16[8,32,2560]{2,1,0:T(8,128)(2,1)}), bf16[8,32,2560]{2,1,0:T(8,128)(2,1)S(1)}, u32[]{:S(2)}, u32[]{:S(2)}) async-start(bf16[8,32,2560]{2,1,0:T(8,128)(2,1)} %copy-done.14), calls=%async_computation.1 | async-start | bytes 2621440 | tf_op jit(solution)/shard_map/all_to_all | solution.py:37
  60.6 15.2 %collective-permute-done.8.refs_6_ = bf16[48,16,512]{2,1,0:T(8,128)(2,1)S(1)} collective-permute-done((bf16[48,16,512]{2,1,0:T(8,128)(2,1)}, bf16[48,16,512]{2,1,0:T(8,128)(2,1)S(1)}, u32[]{:S(2)}, u32[]{:S(2)}) %collective-permute-start.8) | collective-permute-done | bytes 786464 | tf_op jit(solution)/shard_map/ppermute | solution.py:33
  83.0 2.7 %collective-permute-start.11 = (bf16[24,16,512]{2,1,0:T(8,128)(2,1)S(1)}, bf16[24,16,512]{2,1,0:T(8,128)(2,1)S(1)}, u32[]{:S(2)}, u32[]{:S(2)}) collective-permute-start(bf16[24,16,512]{2,1,0:T(8,128)(2,1)S(1)} %slice.28), channel_id=1, source_target_pairs={{0,48},{16,0},{32,16},{48,32},{1,49},{17,1},{33,17},{49,33},{2,50}... | collective-permute-start | bytes 1179656 | tf_op jit(solution)/shard_map/ppermute | solution.py:33
  85.7 9.2 %collective-permute-done.10.refs_8_ = bf16[24,16,512]{2,1,0:T(8,128)(2,1)S(1)} collective-permute-done((bf16[24,16,512]{2,1,0:T(8,128)(2,1)S(1)}, bf16[24,16,512]{2,1,0:T(8,128)(2,1)S(1)}, u32[]{:S(2)}, u32[]{:S(2)}) %collective-permute-start.10) | collective-permute-done | bytes 393248 | tf_op jit(solution)/shard_map/ppermute | solution.py:29
  99.4 4.1 %shard_map.122 = (bf16[320,512]{1,0:T(8,128)(2,1)S(1)}, f32[320,512]{1,0:T(8,128)S(1)}, bf16[320,2048]{1,0:T(8,128)(2,1)S(1)}, bf16[16,128,512]{2,1,0:T(8,128)(2...) custom-call(s32[4]{0:T(128)S(1)} %copy-done.26, ...), custom_call_target="tpu_custom_call" | custom-call | tf_op jit(solution)/shard_map/pallas_call | solution.py:56
  104.4 2.7 %collective-permute-done.12.refs_1_ = bf16[8,16,5120]{2,1,0:T(8,128)(2,1)S(1)} collective-permute-done((bf16[8,16,5120]{2,1,0:T(8,128)(2,1)S(1)}, bf16[8,16,5120]{2,1,0:T(8,128)(2,1)S(1)}, u32[]{:S(2)}, u32[]{:S(2)}) %collective-permute-start.12) | collective-permute-done | bytes 1310752 | tf_op jit(solution)/shard_map/ppermute | solution.py:21
  107.4 25.8 %all_to_all.31.parts = bf16[8,16,5120]{2,1,0:T(8,128)(2,1)S(1)} all-to-all(bf16[8,16,5120]{2,1,0:T(8,128)(2,1)S(1)} %shard_map.123), channel_id=1, replica_groups=mesh['zlo'=2,'x'=4,'core'=2,'zhi'=2,'y'=4] {'zhi','y'}, dimensions={0} | all-to-all | bytes 2621440 | tf_op jit(solution)/shard_map/all_to_all | solution.py:37
  133.2 5.5 %shard_map.124 = (bf16[8,16,2560]{2,1,0:T(8,128)(2,1)S(1)}, bf16[8,16,5120]{2,1,0:T(8,128)(2,1)S(1)}, f32[128,128]{1,0:T(8,128)S(1)}, f32[8,128]{1,0:T(8,128)S(1)}) custom-call(s32[4]{0:T(128)S(1)} %copy-done.26, bf16[8,16,5120]{2,1,0:T(8,128)(2,1)S(1)} %all_to_all.31.parts, bf16[8,352,128]{2,1,0:T(8,128)(2,1)S(1)} %all_to_all.30.message, ...), custom_call_target="tpu_custom_call" | custom-call | tf_op jit(solution)/shard_map/pallas_call | solution.py:56
  138.7 21.3 %all_to_all.32.d_own = bf16[8,16,5120]{2,1,0:T(8,128)(2,1)S(1)} all-to-all(bf16[8,16,5120]{2,1,0:T(8,128)(2,1)S(1)} %get-tuple-element.69), channel_id=1, replica_groups=mesh['zlo'=2,'x'=4,'core'=2,'zhi'=2,'y'=4] {'zhi','y'}, dimensions={0} | all-to-all | bytes 2621440 | tf_op jit(solution)/shard_map/all_to_all | solution.py:37
  162.3 2.7 %collective-permute-done.13.d_sib = bf16[8,16,5120]{2,1,0:T(8,128)(2,1)S(1)} collective-permute-done((bf16[8,16,5120]{2,1,0:T(8,128)(2,1)S(1)}, bf16[8,16,5120]{2,1,0:T(8,128)(2,1)S(1)}, u32[]{:S(2)}, u32[]{:S(2)}) %collective-permute-start.13) | collective-permute-done | bytes 1310752 | tf_op jit(solution)/shard_map/ppermute | solution.py:21
  164.9 8.7 %shard_map.125 = (bf16[48,16,512]{2,1,0:T(8,128)(2,1)S(1)}, bf16[48,16,512]{2,1,0:T(8,128)(2,1)}, bf16[48,16,512]{2,1,0:T(8,128)(2,1)}, bf16[48,16,512]{2,1,0:T(...) custom-call(s32[4]{0:T(128)S(1)} %copy-done.26, ...), custom_call_target="tpu_custom_call" | custom-call | tf_op jit(solution)/shard_map/pallas_call | solution.py:56
  176.7 2.7 %collective-permute-start.16 = (bf16[48,16,512]{2,1,0:T(8,128)(2,1)}, bf16[48,16,512]{2,1,0:T(8,128)(2,1)}, u32[]{:S(2)}, u32[]{:S(2)}) collective-permute-start(bf16[48,16,512]{2,1,0:T(8,128)(2,1)} %get-tuple-element.80), channel_id=1, source_target_pairs={{0,48},{16,0},{32,16},{48,32},{1,49},{17,1},{33,17},{49,33},{2,50}... | collective-permute-start | bytes 2359304 | tf_op jit(solution)/shard_map/ppermute | solution.py:33
  180.7 3.6 %all-to-all-start.4 = ((bf16[8,32,2560]{2,1,0:T(8,128)(2,1)}), bf16[8,32,2560]{2,1,0:T(8,128)(2,1)S(1)}, u32[]{:S(2)}, u32[]{:S(2)}) async-start(bf16[8,32,2560]{2,1,0:T(8,128)(2,1)} %shard_map.126), calls=%async_computation.4 | async-start | bytes 2621440 | tf_op jit(solution)/shard_map/all_to_all | solution.py:37
  184.3 13.1 %collective-permute-done.15.refs_1_ = bf16[48,16,512]{2,1,0:T(8,128)(2,1)} collective-permute-done((bf16[48,16,512]{2,1,0:T(8,128)(2,1)}, bf16[48,16,512]{2,1,0:T(8,128)(2,1)}, u32[]{:S(2)}, u32[]{:S(2)}) %collective-permute-start.15) | collective-permute-done | bytes 786464 | tf_op jit(solution)/shard_map/ppermute | solution.py:29
  197.4 2.3 shard_map.128
  204.4 3.7 %shard_map.129 = bf16[128,16,128]{2,1,0:T(8,128)(2,1)} custom-call(bf16[8,32,2560]{2,1,0:T(8,128)(2,1)S(1)} %all-to-all-done.4.back, f32[20,16,128]{2,1,0:T(8,128)S(1)} %copy-done.23, f32[20,16,128]{2,1,0:T(8,128)S(1)} %copy-done.25, bf16[8,352,128]{2,1,0:T(8,128)(2,1)S(1)} %all_to_all.30.message, f32[128,128]{1,0:T(8,128)S(1)} %get-tuple-element.87.mix_part, ...), custom_call_target="tpu_custom_call" | custom-call | tf_op jit(solution)/shard_map/pallas_call | solution.py:56
  208.1 11.1 %collective-permute-done.17.relayed = bf16[48,16,512]{2,1,0:T(8,128)(2,1)S(1)} collective-permute-done((bf16[48,16,512]{2,1,0:T(8,128)(2,1)}, bf16[48,16,512]{2,1,0:T(8,128)(2,1)S(1)}, u32[]{:S(2)}, u32[]{:S(2)}) %collective-permute-start.17) | collective-permute-done | bytes 786464 | tf_op jit(solution)/shard_map/ppermute | solution.py:29
  219.2 2.8 %shard_map.130 = (bf16[48,16,512]{2,1,0:T(8,128)(2,1)}, bf16[48,16,512]{2,1,0:T(8,128)(2,1)}) custom-call(bf16[48,16,512]{2,1,0:T(8,128)(2,1)S(1)} %copy-done.20, bf16[48,16,512]{2,1,0:T(8,128)(2,1)} %collective-permute-done.16.from_right, bf16[48,16,512]{2,1,0:T(8,128)(2,1)S(1)} %collective-permute-done.17.relayed, bf16[48,16,512]{2,1,0:T(8,128)(2,1)S(1)} %copy-done.18, ...), custom_call_target="tpu_custom_call" | custom-call | tf_op jit(solution)/shard_map/pallas_call | solution.py:56
  222.1 2.5 collective-permute-start.20
  224.6 8.5 %all-to-all-start.5 = ((bf16[128,16,128]{2,1,0:T(8,128)(2,1)}), bf16[128,16,128]{2,1,0:T(8,128)(2,1)S(1)}, u32[]{:S(2)}, u32[]{:S(2)}) async-start(bf16[128,16,128]{2,1,0:T(8,128)(2,1)} %shard_map.129), calls=%async_computation.5 | async-start | bytes 1048576 | tf_op jit(solution)/shard_map/all_to_all | solution.py:37
  233.0 6.6 %collective-permute-done.20.two = bf16[48,16,512]{2,1,0:T(8,128)(2,1)} collective-permute-done((bf16[48,16,512]{2,1,0:T(8,128)(2,1)}, bf16[48,16,512]{2,1,0:T(8,128)(2,1)}, u32[]{:S(2)}, u32[]{:S(2)}) %collective-permute-start.20) | collective-permute-done | bytes 786464 | tf_op jit(solution)/shard_map/ppermute | solution.py:33
  239.7 3.7 %collective-permute-done.21.three = bf16[48,16,512]{2,1,0:T(8,128)(2,1)} collective-permute-done((bf16[48,16,512]{2,1,0:T(8,128)(2,1)}, bf16[48,16,512]{2,1,0:T(8,128)(2,1)}, u32[]{:S(2)}, u32[]{:S(2)}) %collective-permute-start.21) | collective-permute-done | bytes 786464 | tf_op jit(solution)/shard_map/ppermute | solution.py:25
  243.4 2.5 shard_map.131
  245.9 7.0 %collective-permute-start.22 = (bf16[384,512]{1,0:T(8,128)(2,1)S(1)}, bf16[384,512]{1,0:T(8,128)(2,1)S(1)}, u32[]{:S(2)}, u32[]{:S(2)}) collective-permute-start(bf16[384,512]{1,0:T(8,128)(2,1)S(1)} %get-tuple-element.99), channel_id=1, source_target_pairs={{0,8},{8,0},{1,9},{9,1},{2,10},{10,2},{3,11},{11,3},{4,12},{12,4},... | collective-permute-start | bytes 1179656 | tf_op jit(solution)/shard_map/ppermute | solution.py:21
  (109 shorter events, 43.4 us)
Async XLA Ops:
  3.7 3.1 %collective-permute-start = (bf16[384,512]{1,0:T(8,128)(2,1)}, bf16[384,512]{1,0:T(8,128)(2,1)S(1)}, u32[]{:S(2)}, u32[]{:S(2)}) collective-permute-start(bf16[384,512]{1,0:T(8,128)(2,1)} %shard_map.118), channel_id=1, source_target_pairs={{0,8},{8,0},{1,9},{9,1},{2,10},{10,2},{3,11},{11,3},{4,12},{12,4},... | collective-permute-start | bytes 1179656 | tf_op jit(solution)/shard_map/ppermute | solution.py:21
  10.7 30.7 %collective-permute-start.4 = (bf16[48,16,512]{2,1,0:T(8,128)(2,1)}, bf16[48,16,512]{2,1,0:T(8,128)(2,1)S(1)}, u32[]{:S(2)}, u32[]{:S(2)}) collective-permute-start(bf16[48,16,512]{2,1,0:T(8,128)(2,1)} %shard_map.119.refs_0_), channel_id=1, source_target_pairs={{0,64},{64,0},{1,65},{65,1},{2,66},{66,2},{3,67},{67,3},{4,68},{68... | collective-permute-start | bytes 2359304 | tf_op jit(solution)/shard_map/ppermute | solution.py:25
  12.5 28.9 %collective-permute-start.3 = (bf16[48,16,512]{2,1,0:T(8,128)(2,1)}, bf16[48,16,512]{2,1,0:T(8,128)(2,1)S(1)}, u32[]{:S(2)}, u32[]{:S(2)}) collective-permute-start(bf16[48,16,512]{2,1,0:T(8,128)(2,1)} %shard_map.119.refs_0_), channel_id=1, source_target_pairs={{0,48},{16,0},{32,16},{48,32},{1,49},{17,1},{33,17},{49,33},{2,50}... | collective-permute-start | bytes 2359304 | tf_op jit(solution)/shard_map/ppermute | solution.py:33
  14.9 26.4 %collective-permute-start.2 = (bf16[48,16,512]{2,1,0:T(8,128)(2,1)}, bf16[48,16,512]{2,1,0:T(8,128)(2,1)S(1)}, u32[]{:S(2)}, u32[]{:S(2)}) collective-permute-start(bf16[48,16,512]{2,1,0:T(8,128)(2,1)} %shard_map.119.refs_0_), channel_id=1, source_target_pairs={{0,16},{16,32},{32,48},{48,0},{1,17},{17,33},{33,49},{49,1},{2,18}... | collective-permute-start | bytes 2359304 | tf_op jit(solution)/shard_map/ppermute | solution.py:29
  15.7 1.8 collective-permute-start.1
  41.4 9.8 %collective-permute-start.6 = (bf16[24,16,512]{2,1,0:T(8,128)(2,1)S(1)}, bf16[24,16,512]{2,1,0:T(8,128)(2,1)S(1)}, u32[]{:S(2)}, u32[]{:S(2)}) collective-permute-start(bf16[24,16,512]{2,1,0:T(8,128)(2,1)S(1)} %slice.26), channel_id=1, source_target_pairs={{0,48},{16,0},{32,16},{48,32},{1,49},{17,1},{33,17},{49,33},{2,50}... | collective-permute-start | bytes 1179656 | tf_op jit(solution)/shard_map/ppermute | solution.py:33
  44.4 10.0 %collective-permute-start.5 = (bf16[24,16,512]{2,1,0:T(8,128)(2,1)S(1)}, bf16[24,16,512]{2,1,0:T(8,128)(2,1)S(1)}, u32[]{:S(2)}, u32[]{:S(2)}) collective-permute-start(bf16[24,16,512]{2,1,0:T(8,128)(2,1)S(1)} %slice.25), channel_id=1, source_target_pairs={{0,16},{16,32},{32,48},{48,0},{1,17},{17,33},{33,49},{49,1},{2,18}... | collective-permute-start | bytes 1179656 | tf_op jit(solution)/shard_map/ppermute | solution.py:29
  55.1 39.8 %copy-start.26 = (s32[4]{0:T(128)S(1)}, s32[4]{0:T(128)}, u32[]{:S(2)}) copy-start(s32[4]{0:T(128)} %pad_add_fusion.place) | copy-start | bytes 52
  55.1 24.0 %all-to-all-start.1 = ((bf16[8,32,2560]{2,1,0:T(8,128)(2,1)}), bf16[8,32,2560]{2,1,0:T(8,128)(2,1)S(1)}, u32[]{:S(2)}, u32[]{:S(2)}) async-start(bf16[8,32,2560]{2,1,0:T(8,128)(2,1)} %copy-done.14), calls=%async_computation.1 | async-start | bytes 2621440 | tf_op jit(solution)/shard_map/all_to_all | solution.py:37
  59.1 35.9 %copy-start = (bf16[48,16,512]{2,1,0:T(8,128)(2,1)S(1)}, bf16[48,16,512]{2,1,0:T(8,128)(2,1)}, u32[]{:S(2)}) copy-start(bf16[48,16,512]{2,1,0:T(8,128)(2,1)} %shard_map.119.refs_0_) | copy-start | bytes 2359300
  59.1 16.7 %collective-permute-start.8 = (bf16[48,16,512]{2,1,0:T(8,128)(2,1)}, bf16[48,16,512]{2,1,0:T(8,128)(2,1)S(1)}, u32[]{:S(2)}, u32[]{:S(2)}) collective-permute-start(bf16[48,16,512]{2,1,0:T(8,128)(2,1)} %copy-done.9), channel_id=1, source_target_pairs={{0,48},{16,0},{32,16},{48,32},{1,49},{17,1},{33,17},{49,33},{2,50}... | collective-permute-start | bytes 2359304 | tf_op jit(solution)/shard_map/ppermute | solution.py:33
  59.4 17.9 %collective-permute-start.7 = (bf16[48,16,512]{2,1,0:T(8,128)(2,1)}, bf16[48,16,512]{2,1,0:T(8,128)(2,1)}, u32[]{:S(2)}, u32[]{:S(2)}) collective-permute-start(bf16[48,16,512]{2,1,0:T(8,128)(2,1)} %copy-done.9), channel_id=1, source_target_pairs={{0,16},{16,32},{32,48},{48,0},{1,17},{17,33},{33,49},{49,1},{2,18}... | collective-permute-start | bytes 2359304 | tf_op jit(solution)/shard_map/ppermute | solution.py:29
  79.2 15.8 %collective-permute-start.9 = (bf16[8,32,2560]{2,1,0:T(8,128)(2,1)S(1)}, bf16[8,32,2560]{2,1,0:T(8,128)(2,1)S(1)}, u32[]{:S(2)}, u32[]{:S(2)}) collective-permute-start(bf16[8,32,2560]{2,1,0:T(8,128)(2,1)S(1)} %all-to-all-done.1.own.cot), channel_id=1, source_target_pairs={{0,8},{8,0},{1,9},{9,1},{2,10},{10,2},{3,11},{11,3},{4,12},{12,4},... | collective-permute-start | bytes 3932168 | tf_op jit(solution)/shard_map/ppermute | solution.py:21
  83.0 12.0 %collective-permute-start.10 = (bf16[24,16,512]{2,1,0:T(8,128)(2,1)S(1)}, bf16[24,16,512]{2,1,0:T(8,128)(2,1)S(1)}, u32[]{:S(2)}, u32[]{:S(2)}) collective-permute-start(bf16[24,16,512]{2,1,0:T(8,128)(2,1)S(1)} %slice.27), channel_id=1, source_target_pairs={{0,16},{16,32},{32,48},{48,0},{1,17},{17,33},{33,49},{49,1},{2,18}... | collective-permute-start | bytes 1179656 | tf_op jit(solution)/shard_map/ppermute | solution.py:29
  83.0 11.9 %collective-permute-start.11 = (bf16[24,16,512]{2,1,0:T(8,128)(2,1)S(1)}, bf16[24,16,512]{2,1,0:T(8,128)(2,1)S(1)}, u32[]{:S(2)}, u32[]{:S(2)}) collective-permute-start(bf16[24,16,512]{2,1,0:T(8,128)(2,1)S(1)} %slice.28), channel_id=1, source_target_pairs={{0,48},{16,0},{32,16},{48,32},{1,49},{17,1},{33,17},{49,33},{2,50}... | collective-permute-start | bytes 1179656 | tf_op jit(solution)/shard_map/ppermute | solution.py:33
  103.5 3.6 %collective-permute-start.12 = (bf16[8,16,5120]{2,1,0:T(8,128)(2,1)S(1)}, bf16[8,16,5120]{2,1,0:T(8,128)(2,1)S(1)}, u32[]{:S(2)}, u32[]{:S(2)}) collective-permute-start(bf16[8,16,5120]{2,1,0:T(8,128)(2,1)S(1)} %get-tuple-element.68), channel_id=1, source_target_pairs={{0,8},{8,0},{1,9},{9,1},{2,10},{10,2},{3,11},{11,3},{4,12},{12,4},... | collective-permute-start | bytes 3932168 | tf_op jit(solution)/shard_map/ppermute | solution.py:21
  107.4 25.8 %copy-start.27 = (f32[128]{0:T(128)S(1)}, f32[128]{0:T(128)}, u32[]{:S(2)}) copy-start(f32[128]{0:T(128)} %param.12) | copy-start | bytes 1540
  138.7 26.2 %copy-start.5 = (bf16[48,16,512]{2,1,0:T(8,128)(2,1)S(1)}, bf16[48,16,512]{2,1,0:T(8,128)(2,1)}, u32[]{:S(2)}) copy-start(bf16[48,16,512]{2,1,0:T(8,128)(2,1)} %copy-done.3) | copy-start | bytes 2359300
  138.7 26.2 %copy-start.8 = (bf16[48,16,512]{2,1,0:T(8,128)(2,1)S(1)}, bf16[48,16,512]{2,1,0:T(8,128)(2,1)}, u32[]{:S(2)}) copy-start(bf16[48,16,512]{2,1,0:T(8,128)(2,1)} %copy-done.6) | copy-start | bytes 2359300
  138.7 26.2 %copy-start.11 = (bf16[48,16,512]{2,1,0:T(8,128)(2,1)S(1)}, bf16[48,16,512]{2,1,0:T(8,128)(2,1)}, u32[]{:S(2)}) copy-start(bf16[48,16,512]{2,1,0:T(8,128)(2,1)} %copy-done.9) | copy-start | bytes 2359300
  160.1 4.9 %collective-permute-start.13 = (bf16[8,16,5120]{2,1,0:T(8,128)(2,1)S(1)}, bf16[8,16,5120]{2,1,0:T(8,128)(2,1)S(1)}, u32[]{:S(2)}, u32[]{:S(2)}) collective-permute-start(bf16[8,16,5120]{2,1,0:T(8,128)(2,1)S(1)} %all_to_all.32.d_own), channel_id=1, source_target_pairs={{0,8},{8,0},{1,9},{9,1},{2,10},{10,2},{3,11},{11,3},{4,12},{12,4},... | collective-permute-start | bytes 3932168 | tf_op jit(solution)/shard_map/ppermute | solution.py:21
  176.3 3.1 %collective-permute-start.14 = (bf16[8,16,2560]{2,1,0:T(8,128)(2,1)S(1)}, bf16[8,16,2560]{2,1,0:T(8,128)(2,1)S(1)}, u32[]{:S(2)}, u32[]{:S(2)}) collective-permute-start(bf16[8,16,2560]{2,1,0:T(8,128)(2,1)S(1)} %get-tuple-element.75), channel_id=1, source_target_pairs={{0,8},{8,0},{1,9},{9,1},{2,10},{10,2},{3,11},{11,3},{4,12},{12,4},... | collective-permute-start | bytes 1966088 | tf_op jit(solution)/shard_map/ppermute | solution.py:21
  176.7 20.6 %collective-permute-start.15 = (bf16[48,16,512]{2,1,0:T(8,128)(2,1)}, bf16[48,16,512]{2,1,0:T(8,128)(2,1)}, u32[]{:S(2)}, u32[]{:S(2)}) collective-permute-start(bf16[48,16,512]{2,1,0:T(8,128)(2,1)} %get-tuple-element.79), channel_id=1, source_target_pairs={{0,16},{16,32},{32,48},{48,0},{1,17},{17,33},{33,49},{49,1},{2,18}... | collective-permute-start | bytes 2359304 | tf_op jit(solution)/shard_map/ppermute | solution.py:29
  176.7 20.6 %collective-permute-start.16 = (bf16[48,16,512]{2,1,0:T(8,128)(2,1)}, bf16[48,16,512]{2,1,0:T(8,128)(2,1)}, u32[]{:S(2)}, u32[]{:S(2)}) collective-permute-start(bf16[48,16,512]{2,1,0:T(8,128)(2,1)} %get-tuple-element.80), channel_id=1, source_target_pairs={{0,48},{16,0},{32,16},{48,32},{1,49},{17,1},{33,17},{49,33},{2,50}... | collective-permute-start | bytes 2359304 | tf_op jit(solution)/shard_map/ppermute | solution.py:33
  180.7 23.7 %all-to-all-start.4 = ((bf16[8,32,2560]{2,1,0:T(8,128)(2,1)}), bf16[8,32,2560]{2,1,0:T(8,128)(2,1)S(1)}, u32[]{:S(2)}, u32[]{:S(2)}) async-start(bf16[8,32,2560]{2,1,0:T(8,128)(2,1)} %shard_map.126), calls=%async_computation.4 | async-start | bytes 2621440 | tf_op jit(solution)/shard_map/all_to_all | solution.py:37
  199.6 19.6 %collective-permute-start.17 = (bf16[48,16,512]{2,1,0:T(8,128)(2,1)}, bf16[48,16,512]{2,1,0:T(8,128)(2,1)S(1)}, u32[]{:S(2)}, u32[]{:S(2)}) collective-permute-start(bf16[48,16,512]{2,1,0:T(8,128)(2,1)} %shard_map.128), channel_id=1, source_target_pairs={{0,16},{16,32},{32,48},{48,0},{1,17},{17,33},{33,49},{49,1},{2,18}... | collective-permute-start | bytes 2359304 | tf_op jit(solution)/shard_map/ppermute | solution.py:29
  200.4 18.8 %collective-permute-start.18 = (bf16[48,16,512]{2,1,0:T(8,128)(2,1)}, bf16[48,16,512]{2,1,0:T(8,128)(2,1)}, u32[]{:S(2)}, u32[]{:S(2)}) collective-permute-start(bf16[48,16,512]{2,1,0:T(8,128)(2,1)} %get-tuple-element.83), channel_id=1, source_target_pairs={{0,48},{16,0},{32,16},{48,32},{1,49},{17,1},{33,17},{49,33},{2,50}... | collective-permute-start | bytes 2359304 | tf_op jit(solution)/shard_map/ppermute | solution.py:33
  222.1 17.6 %collective-permute-start.20 = (bf16[48,16,512]{2,1,0:T(8,128)(2,1)}, bf16[48,16,512]{2,1,0:T(8,128)(2,1)}, u32[]{:S(2)}, u32[]{:S(2)}) collective-permute-start(bf16[48,16,512]{2,1,0:T(8,128)(2,1)} %get-tuple-element.95), channel_id=1, source_target_pairs={{0,48},{16,0},{32,16},{48,32},{1,49},{17,1},{33,17},{49,33},{2,50}... | collective-permute-start | bytes 2359304 | tf_op jit(solution)/shard_map/ppermute | solution.py:33
  224.6 18.8 %collective-permute-start.21 = (bf16[48,16,512]{2,1,0:T(8,128)(2,1)}, bf16[48,16,512]{2,1,0:T(8,128)(2,1)}, u32[]{:S(2)}, u32[]{:S(2)}) collective-permute-start(bf16[48,16,512]{2,1,0:T(8,128)(2,1)} %get-tuple-element.96), channel_id=1, source_target_pairs={{0,64},{64,0},{1,65},{65,1},{2,66},{66,2},{3,67},{67,3},{4,68},{68... | collective-permute-start | bytes 2359304 | tf_op jit(solution)/shard_map/ppermute | solution.py:25
  224.6 18.8 %collective-permute-start.19 = (bf16[48,16,512]{2,1,0:T(8,128)(2,1)}, bf16[48,16,512]{2,1,0:T(8,128)(2,1)}, u32[]{:S(2)}, u32[]{:S(2)}) collective-permute-start(bf16[48,16,512]{2,1,0:T(8,128)(2,1)} %get-tuple-element.89), channel_id=1, source_target_pairs={{0,16},{16,32},{32,48},{48,0},{1,17},{17,33},{33,49},{49,1},{2,18}... | collective-permute-start | bytes 2359304 | tf_op jit(solution)/shard_map/ppermute | solution.py:29
  224.6 31.1 %all-to-all-start.5 = ((bf16[128,16,128]{2,1,0:T(8,128)(2,1)}), bf16[128,16,128]{2,1,0:T(8,128)(2,1)S(1)}, u32[]{:S(2)}, u32[]{:S(2)}) async-start(bf16[128,16,128]{2,1,0:T(8,128)(2,1)} %shard_map.129), calls=%async_computation.5 | async-start | bytes 1048576 | tf_op jit(solution)/shard_map/all_to_all | solution.py:37
  245.9 8.3 %collective-permute-start.22 = (bf16[384,512]{1,0:T(8,128)(2,1)S(1)}, bf16[384,512]{1,0:T(8,128)(2,1)S(1)}, u32[]{:S(2)}, u32[]{:S(2)}) collective-permute-start(bf16[384,512]{1,0:T(8,128)(2,1)S(1)} %get-tuple-element.99), channel_id=1, source_target_pairs={{0,8},{8,0},{1,9},{9,1},{2,10},{10,2},{3,11},{11,3},{4,12},{12,4},... | collective-permute-start | bytes 1179656 | tf_op jit(solution)/shard_map/ppermute | solution.py:21
  (24 other events, 164.9 us)

commit v3 on v2

--- a/solution.py
+++ b/solution.py
@@ -1,3 +1,5 @@
+import functools
+
 import jax
 import jax.numpy as jnp
 from jax import lax
@@ -52,7 +54,7 @@
 def call(body, outs, *args, scratch=(), scalars=0, remote_in=0, remote_out=0, room=16):
     whole = pl.BlockSpec(memory_space=pltpu.VMEM)
     small = pl.BlockSpec(memory_space=pltpu.SMEM)
-    there = pl.BlockSpec(memory_space=pl.ANY)
+    there = pl.BlockSpec(memory_space=pltpu.HBM)
     return pl.pallas_call(
         body,
         out_shape=outs,
@@ -101,7 +103,7 @@
         copy.wait()
 
 
-def message_kernel(place, proj, mix, token, emb, message, sems):
+def message_kernel(place, proj, mix, emb, message, sems):
     copy = pltpu.make_async_copy(emb, message.at[:, pl.ds(0, 320)], sems.at[0])
     copy.start()
     here = one_where((16, 128), lambda n, lane: lane == place[3] * 16 + n)
@@ -114,8 +116,9 @@
     copy.wait()
 
 
-def piece_kernel(place, got, up, down, piece, mine_up, mine_down, sems):
+def piece_kernel(place, got, up, down, out, token, piece, mine_up, mine_down, sems):
     core = place[0]
+    token[...] = got[:16, :128]
     mine, unused = halves(core, 512)
     copies = [
         pltpu.make_async_copy(up.at[:, mine], mine_up, sems.at[0]),
@@ -132,6 +135,9 @@
     piece[:16] = rows.astype(BF).reshape(16, 16, 512)
     copies[1].wait()
     piece[16:, :, mine_at] = mine_down[...].reshape(32, 16, 256)
+    copy = pltpu.make_async_copy(piece, out, sems.at[2])
+    copy.start()
+    copy.wait()
 
 
 def total_of(refs):
@@ -141,17 +147,59 @@
     return total.astype(BF)
 
 
-def add_kernel(*refs):
+def add_kernel(parts, *refs):
+    *terms, out, held, total, sems, out_sems = refs
+    sends, taken = [], {}
+    for step in range(0, 48, 12):
+        taken[step] = []
+        for i, (start, first, count) in enumerate(parts):
+            if first <= step < first + count:
+                there = terms[i].at[pl.ds(start + step - first, 12)]
+                sem = sems.at[step // 12 * len(parts) + i]
+                copy = pltpu.make_async_copy(there, held.at[i, pl.ds(step, 12)], sem)
+                copy.start()
+                taken[step].append((i, copy))
+    for step in range(0, 48, 12):
+        at = slice(step, step + 12)
+        part = jnp.zeros((12, 16, 512), F32)
+        for i, copy in taken[step]:
+            copy.wait()
+            part += held[i, at].astype(F32)
+        total[at] = part.astype(BF)
+        if out is not None:
+            at = pl.ds(step, 12)
+            sem = out_sems.at[step // 12]
+            sends.append(pltpu.make_async_copy(total.at[at], out.at[at], sem))
+            sends[-1].start()
+    for copy in sends:
+        copy.wait()
+
+
+def add_scratch(terms):
+    return [
+        pltpu.VMEM((terms, 48, 16, 512), BF),
+        pltpu.VMEM((48, 16, 512), BF),
+        pltpu.SemaphoreType.DMA((4 * terms,)),
+        pltpu.SemaphoreType.DMA((4,)),
+    ]
+
+
+def add(*parts):
+    parts = [(array, start, *(where or (0, 48))) for array, start, *where in parts]
+    terms = [array for array, *unused in parts]
+    return call(
+        functools.partial(add_kernel, [where for unused, *where in parts]),
+        [shape((48, 16, 512))],
+        *terms,
+        scratch=add_scratch(len(terms)),
+        remote_in=len(terms),
+        remote_out=1,
+        room=60,
+    )[0]
+
+
+def sum_kernel(*refs):
     refs[-1][...] = total_of(refs[:-1])
-
-
-def add(*terms):
-    return call(add_kernel, [shape(terms[0].shape)], *terms)[0]
-
-
-def add_both_kernel(own, from_right, relayed, minus, returned, over, on):
-    over[...] = total_of((own, from_right, relayed))
-    on[...] = total_of((minus, returned))
 
 
 def join_kernel(own, got, layer, out):
@@ -159,9 +207,11 @@
     out[:, 16:] = layer[...]
 
 
-def split_kernel(place, own, one, two, three, up_kept, down_kept, sent):
+def split_kernel(place, late, one, two, three, up_kept, down_kept, sent, held, total, *sems):
     core = place[0]
-    total = total_of((own, one, two, three))
+    whole = [(start, 0, 48) for start in (0, 0, 0, 0)]
+    add_kernel(whole, late, one, two, three, None, held, total, *sems)
+    total = total[...]
     up, down = total[:16].reshape(256, 512), total[16:].reshape(512, 512)
     up_kept[...] = dot(chip_rows(core), up, ((0,), (0,))).astype(BF)
     sent[:128] = dot(chip_rows(1 - core), up, ((0,), (0,))).astype(BF)
@@ -172,12 +222,23 @@
     sent[128:, 256:] = other[256:]
 
 
-def finish_kernel(place, up_kept, down_kept, got, up, down):
+def finish_kernel(place, up_kept, down_kept, got, last, up, down, gain, mix, proj):
     mine, other = halves(place[0], 512)
     up[:, mine] = up_kept[...]
     up[:, other] = got[:128]
     down[mine, :] = down_kept[...]
     down[other, :] = jnp.concatenate([got[128:, :256], got[128:, 256:]], 0)
+    total = jnp.sum(last[...].astype(F32), axis=0)
+    gain[...] = total[2:3]
+    mix[...] = total[4:]
+    token = lax.broadcasted_iota(jnp.int32, (16, 128), 0)
+    lane = lax.broadcasted_iota(jnp.int32, (16, 128), 1)
+    rows = jnp.where(token < 8, total[0:1], total[1:2])
+    rows = jnp.where(token % 8 == lane // 16, rows, 0.0)
+    pick = one_where((128, 16), lambda r, k: r % 16 == k).astype(F32)
+    proj[...] = jnp.dot(
+        rows, pick, precision=lax.Precision.HIGHEST, preferred_element_type=F32
+    )
 
 
 def unpack(ref, width, start, size):
@@ -205,27 +266,17 @@
     return jnp.bitwise_xor(place[1], r // 4) * 4 + lax.rem(place[2] + r % 4, 4)
 
 
-def second_part(piece):
-    if len(piece) == 1:
-        return piece[0][16:].reshape(512, 512)
-    low, high = piece
-    return jnp.concatenate([low[16:].reshape(128, 512), high[...].reshape(384, 512)], 0)
-
-
-def pieces_of(refs, late, sems):
-    a, b, c, d, e, f, g, h, low, high = refs
-    copies = [
-        pltpu.make_async_copy(low, late.at[pl.ds(0, 24)], sems.at[0]),
-        pltpu.make_async_copy(high, late.at[pl.ds(24, 24)], sems.at[1]),
-    ]
-    for copy in copies:
-        copy.start()
-    return [(0, [a]), (1, [b]), (2, [c, d]), (3, [e]), (4, [f]), (5, [g]), (7, [h]), (6, [late])], copies
-
-
-def features_kernel(message, cot, payload, normal, rstds, tails):
-    for b in range(OWN):
-        payload[:, 16:, 128 * b : 128 * b + 128] = cot[:, 16 * b : 16 * b + 16]
+def fetch(place, pieces, first_held, second_held, sems):
+    first, second = [], []
+    for r, piece in enumerate(pieces):
+        at = first_held.at[:, many(chip_of(place, r) * 16, 16)]
+        first.append(pltpu.make_async_copy(piece.at[pl.ds(0, 16)], at, sems.at[r]))
+        copy = pltpu.make_async_copy(piece.at[pl.ds(16, 32)], second_held.at[r], sems.at[8 + r])
+        second.append(copy)
+    return first, second
+
+
+def features_kernel(message, payload, normal, rstds, tails):
     proj_w = message[0, 320:336].astype(F32)
     for f in range(1, 8):
         proj_w += message[f, 320:336].astype(F32)
@@ -248,49 +299,45 @@
         tails[quarter : quarter + 4, tail : tail + 128] = block[16:]
         block = block[:16].astype(BF)
         for f in range(8):
-            payload[f, :16, 128 * k : 128 * k + 128] = block
+            payload[f, :, 128 * k : 128 * k + 128] = block
     block = tails[...].astype(BF)
     for f in range(8):
-        payload[f, :16, 2048:] = block
+        payload[f, :, 2048:] = block
 
 
 def forward_kernel(place, own, sib, *refs):
-    hidden, pre, rows, held, fmb_own, fmb_sib, tail_own, tail_sib, late, sems = refs[10:]
-    weights, copies = pieces_of(refs[:10], late, sems)
-    for r, piece in weights:
-        if r == 6:
-            for copy in copies:
-                copy.wait()
-        held[:, many(chip_of(place, r) * 16, 16)] = piece[0][:16]
-    total = jnp.zeros((CHIP, 512), F32)
+    hidden, pre, rows, held, held_down, fmb_own, fmb_sib, tail_own, tail_sib, sems = refs[8:]
+    first, second = fetch(place, refs[:8], held, held_down, sems)
+    for copy in first + second:
+        copy.start()
     for j in range(8):
         part = unpack(own, 2048, 256 * j, 256) + unpack(sib, 2048, 256 * j, 256)
-        part = jnp.concatenate(part, 0)
-        rows[:, 256 * j : 256 * j + 256] = part
-        matrix = held[2 * j : 2 * j + 2].reshape(256, 512)
-        total += dot(part, matrix, ((1,), (0,)))
+        rows[:, 256 * j : 256 * j + 256] = jnp.concatenate(part, 0)
+    for copy in first:
+        copy.wait()
+    total = dot(rows[...], held[...].reshape(2048, 512), ((1,), (0,)))
     pre[...] = total
     act = (total / (1.0 + jnp.exp(-total))).astype(BF)
     hidden[...] = act
-    for r, piece in sorted(weights, key=lambda item: item[0]):
-        part = dot(act, second_part(piece), ((1,), (0,)))
+    for copy in second:
+        copy.wait()
+    for r in range(8):
+        part = dot(act, held_down[r].reshape(512, 512), ((1,), (0,)))
         pack(part[:CORE], fmb_own, tail_own, 4096, 512 * r, 512)
         pack(part[CORE:], fmb_sib, tail_sib, 4096, 512 * r, 512)
 
 
-def backward_kernel(place, d_own, d_sib, rows, hidden, pre, held, *refs):
-    grads, (dn_own, dn_sib) = refs[10:18], refs[18:20]
-    d_rows, made, made_down, tail_own, tail_sib, late, sems, out_sems = refs[20:]
-    weights, copies = pieces_of(refs[:10], late, sems)
+def backward_kernel(place, d_own, d_sib, rows, hidden, pre, held, held_down, *refs):
+    far1_low, far1_high, far0_low, far0_high, late, dn_own, dn_sib = refs[:7]
+    d_rows, made, made_down, tail_own, tail_sib, out_sems = refs[7:]
+    halves_of = {2: (far0_low, far0_high), 6: (far1_low, far1_high)}
+    starts = {0: 0, 4: 48, 5: 96, 7: 144, 1: 192, 3: 240}
     total = jnp.zeros((CHIP, 512), F32)
-    for r, piece in weights:
+    for r in range(8):
         part = unpack(d_own, 4096, 512 * r, 512) + unpack(d_sib, 4096, 512 * r, 512)
         part = jnp.concatenate(part, 0)
         d_rows[:, 512 * r : 512 * r + 512] = part
-        if r == 6:
-            for copy in copies:
-                copy.wait()
-        total += dot(part, second_part(piece), ((1,), (1,)))
+        total += dot(part, held_down[r].reshape(512, 512), ((1,), (1,)))
     sends = []
 
     def send(source, there, sem):
@@ -301,14 +348,21 @@
     for r in (6, 7, 2, 5, 4, 1, 3, 0):
         part = dot(act, d_rows[:, 512 * r : 512 * r + 512], ((1,), (0,)))
         made_down[r] = part.astype(BF).reshape(32, 16, 512)
-        send(made_down.at[r], grads[r].at[pl.ds(16, 32)], 8 + r)
+        if r in halves_of:
+            low, high = halves_of[r]
+            send(made_down.at[r, pl.ds(0, 8)], low.at[pl.ds(16, 8)], 8 + r)
+            send(made_down.at[r, pl.ds(8, 24)], high, 16 + r // 4)
+        else:
+            send(made_down.at[r], late.at[pl.ds(starts[r] + 16, 32)], 8 + r)
     sig = 1.0 / (1.0 + jnp.exp(-pre[...]))
     d_pre = (total * (sig * (1.0 + pre[...] * (1.0 - sig)))).astype(BF)
     for j in range(8):
         part = dot(rows[:, 256 * j : 256 * j + 256], d_pre, ((0,), (0,)))
         made[2 * j : 2 * j + 2] = part.astype(BF).reshape(2, 128, 512)
     for r in range(8):
-        send(made.at[:, many(chip_of(place, r) * 16, 16)], grads[r].at[pl.ds(0, 16)], r)
+        there = halves_of[r][0] if r in halves_of else late.at[pl.ds(starts[r], 48)]
+        here = made.at[:, many(chip_of(place, r) * 16, 16)]
+        send(here, there.at[pl.ds(0, 16)], r)
     for j in range(8):
         part = dot(d_pre, held[2 * j : 2 * j + 2].reshape(256, 512), ((1,), (1,)))
         pack(part[:CORE], dn_own, tail_own, 2048, 256 * j, 256)
@@ -347,7 +401,7 @@
     def sample(b, carry):
         at = many(b * 16, 16)
         tokens = message[:, at].reshape(128, 128)
-        cotan = cot[:, 16:, many(b * 128, 128)].reshape(128, 128).astype(F32)
+        cotan = cot[:, at].reshape(128, 128).astype(F32)
         lcb = dot(mixing, tokens, ((1,), (0,)))
         summed = lcb + fm[b].reshape(128, 128) + tokens.astype(F32)
         cent = summed - mean(summed)
@@ -417,28 +471,6 @@
 def unfold_kernel(back, layer):
     for b in range(OWN):
         layer[:, b] = back[:, 16:, 128 * b : 128 * b + 128]
-
-
-def finish_weights(place, own, from_left, relayed, other):
-    up_kept, down_kept, sent = call(
-        split_kernel,
-        [shape((128, 512)), shape((512, 256)), shape((384, 512))],
-        place,
-        own,
-        from_left,
-        relayed,
-        other,
-        scalars=1,
-    )
-    return call(
-        finish_kernel,
-        [shape((128, 1024)), shape((1024, 256))],
-        place,
-        up_kept,
-        down_kept,
-        sibling(sent),
-        scalars=1,
-    )
 
 
 def per_device(embeddings, proj_weight, up_weight, down_weight, mix_weight, out_gain, cotangent):
@@ -455,23 +487,23 @@
         scratch=[pltpu.SemaphoreType.DMA((3,))],
         scalars=1,
         remote_in=2,
-        room=60,
-    )
-    (mine,) = call(
+    )
+    mine, token = call(
         piece_kernel,
-        [shape((48, 16, 512))],
+        [shape((48, 16, 512)), shape((16, 128))],
         place,
         sibling(sent),
         up_weight,
         down_weight,
         scratch=[
+            pltpu.VMEM((48, 16, 512), BF),
             pltpu.VMEM((128, 512), BF),
             pltpu.VMEM((512, 256), BF),
-            pltpu.SemaphoreType.DMA((2,)),
+            pltpu.SemaphoreType.DMA((3,)),
         ],
         scalars=1,
         remote_in=2,
-        room=60,
+        remote_out=1,
     )
     other = across(mine)
     near_left, near_right = right(mine), left(mine)
@@ -481,38 +513,40 @@
         place,
         proj_weight,
         mix_weight.T,
-        sibling(mine[0]),
         embeddings.reshape(8, 320, 128),
         scratch=[pltpu.SemaphoreType.DMA((1,))],
         scalars=1,
         remote_in=1,
-        room=60,
-    )
+    )
+    message, token = together(message, sibling(token))
     message = exchange(message, FEAT)
     message, near_left, near_right, other = together(message, near_left, near_right, other)
     other_left, other_right = right(other), left(other)
-    far_low, far_high = right(near_left[:24]), left(near_right[24:])
 
     payload, normal1, rstd1 = call(
         features_kernel,
-        [shape((8, 32, 2560)), shape((OWN, 16, 128), F32), shape((OWN, 16, 128), F32)],
+        [shape((8, 16, 2560)), shape((OWN, 16, 128), F32), shape((OWN, 16, 128), F32)],
         message,
-        cotangent.reshape(8, 320, 128),
         scratch=[pltpu.VMEM((16, 512), F32)],
     )
-    payload, far_low, far_high = together(payload, far_low, far_high)
+    payload, cotangent = together(payload, cotangent)
+    cotan = exchange(cotangent.reshape(8, 320, 128), FEAT)
+    payload, cotan, token, near_left, other_left, other_right = together(
+        payload, cotan, token, near_left, other_left, other_right
+    )
+    far, other_far = right(near_left), left(other_right)
+    payload, token = together(payload, sibling(token))
     normed = exchange(payload, FEAT)
-    normed, other_left, other_right = together(normed, other_left, other_right)
-    other_low, other_high = right(other_left[:24]), left(other_right[24:])
-    weights = [mine, near_right, far_low, far_high, near_left]
-    weights += [other, other_right, other_left, other_low, other_high]
-    hidden, pre, rows, first, fmb_own, fmb_sib = call(
+    normed, far, other_far = together(normed, far, other_far)
+    weights = [mine, near_right, far, near_left, other, other_right, other_far, other_left]
+    hidden, pre, rows, first, second, fmb_own, fmb_sib = call(
         forward_kernel,
         [
             shape((CHIP, 512)),
             shape((CHIP, 512), F32),
             shape((CHIP, 2048)),
             shape((16, 128, 512)),
+            shape((8, 32, 16, 512)),
             shape((8, 16, 5120)),
             shape((8, 16, 5120)),
         ],
@@ -523,13 +557,13 @@
         scratch=[
             pltpu.VMEM((128, 1024), F32),
             pltpu.VMEM((128, 1024), F32),
-            pltpu.VMEM((48, 16, 512), BF),
-            pltpu.SemaphoreType.DMA((2,)),
+            pltpu.SemaphoreType.DMA((16,)),
         ],
         scalars=1,
-        remote_in=2,
-    )
-    fmb = exchange(add(fmb_own, sibling(fmb_sib)), FEAT)
+        remote_in=8,
+    )
+    (fmb,) = call(sum_kernel, [shape((8, 16, 5120))], fmb_own, sibling(fmb_sib))
+    fmb = exchange(fmb, FEAT)
 
     layer_out, d_fmb, mix_part, gain_part = call(
         norm_kernel,
@@ -542,7 +576,7 @@
         place,
         fmb,
         message,
-        normed,
+        cotan,
         out_gain.reshape(1, 128),
         scratch=[
             pltpu.VMEM((OWN, 8, 16, 128), F32),
@@ -553,9 +587,9 @@
     )
 
     d_fmb = exchange(d_fmb, FEAT)
-    outs = call(
+    far1_low, far1_high, far0_low, far0_high, late, dn_own, dn_sib = call(
         backward_kernel,
-        [shape((48, 16, 512))] * 8 + [shape((8, 16, 2560))] * 2,
+        [shape((24, 16, 512))] * 4 + [shape((288, 16, 512))] + [shape((8, 16, 2560))] * 2,
         place,
         d_fmb,
         sibling(d_fmb),
@@ -563,29 +597,32 @@
         hidden,
         pre,
         first,
-        *weights,
+        second,
         scratch=[
             pltpu.VMEM((CHIP, 4096), BF),
             pltpu.VMEM((16, 128, 512), BF),
             pltpu.VMEM((8, 32, 16, 512), BF),
             pltpu.VMEM((128, 512), F32),
             pltpu.VMEM((128, 512), F32),
-            pltpu.VMEM((48, 16, 512), BF),
-            pltpu.SemaphoreType.DMA((2,)),
-            pltpu.SemaphoreType.DMA((16,)),
+            pltpu.SemaphoreType.DMA((18,)),
         ],
         scalars=1,
-        remote_in=2,
-        remote_out=8,
+        remote_out=5,
         room=24,
     )
-    own0, plus0, far0, minus0, own1, plus1, far1, minus1, dn_own, dn_sib = outs
-
-    from_left, from_right = right(far1), left(minus1)
+
+    low1, high1 = right(far1_low), left(far1_high)
+    low0, high0 = right(far0_low), left(far0_high)
     (back,) = call(join_kernel, [shape((8, 32, 2560))], dn_own, sibling(dn_sib), layer_out)
     back = exchange(back, FEAT)
-    from_left, from_right, far0 = together(from_left, from_right, far0)
-    relayed, returned = right(add(plus1, from_left)), left(far0)
+    plus1 = add((late, 96), (low1, 0, 0, 24))
+    minus1 = add((late, 144), (high1, 0, 24, 24))
+    plus1, minus1, low0, high0 = together(plus1, minus1, low0, high0)
+    from_left1, from_right1 = right(plus1), left(minus1)
+    plus0 = add((late, 192), (low0, 0, 0, 24))
+    minus0 = add((late, 240), (high0, 0, 24, 24))
+    back, plus0, minus0 = together(back, plus0, minus0)
+    from_left0, from_right0 = right(plus0), left(minus0)
     (last,) = call(
         last_kernel,
         [shape((128, 16, 128))],
@@ -597,26 +634,42 @@
         gain_part,
         scratch=[pltpu.VMEM((OWN, 16, 128), F32), pltpu.VMEM((16, 128), F32)],
     )
-    relayed, returned, plus0, last = together(relayed, returned, plus0, last)
-    from_left = right(plus0)
-    over, on = call(
-        add_both_kernel,
-        [shape((48, 16, 512))] * 2,
-        own1,
-        from_right,
-        relayed,
-        minus0,
-        returned,
-    )
-    other, relayed = across(over), left(on)
-    last = exchange(last, ALL)
-    up_grad, down_grad = finish_weights(place, own0, from_left, relayed, other)
-    up_grad, down_grad, last = together(up_grad, down_grad, last)
+    from_left1, from_right1, last = together(from_left1, from_right1, last)
+    over = add((late, 48), (from_left1, 0), (from_right1, 0))
+    over, last = together(over, last)
+    other = across(over)
+    last, other = together(exchange(last, ALL), other)
+    up_kept, down_kept, sent = call(
+        split_kernel,
+        [shape((128, 512)), shape((512, 256)), shape((384, 512))],
+        place,
+        late,
+        from_left0,
+        from_right0,
+        other,
+        scratch=add_scratch(4),
+        scalars=1,
+        remote_in=4,
+        room=60,
+    )
+    up_grad, down_grad, gain_grad, mix_grad, proj_grad = call(
+        finish_kernel,
+        [
+            shape((128, 1024)),
+            shape((1024, 256)),
+            shape((1, 128), F32),
+            shape((12, 128), F32),
+            shape((16, 16), F32),
+        ],
+        place,
+        up_kept,
+        down_kept,
+        sibling(sent),
+        last,
+        scalars=1,
+    )
     (layer_out,) = call(unfold_kernel, [shape((8, OWN, 16, 128))], back)
-    last = jnp.sum(last.astype(F32), 0)
-    proj_grad = last[:2].reshape(16, 16)
-    mix_grad = last[4:].T
-    gain_grad = last[2]
+    gain_grad, mix_grad = gain_grad.reshape(128), mix_grad.T
     layer_out = layer_out.reshape(160, 16, 128)
     return (layer_out, gain_grad, mix_grad, up_grad, down_grad, proj_grad)
 

time: 259 us -> 237 us (0.915)
  blocking collectives: 67.5 us -> 123 us
  waiting for transfers between devices: 75 us -> 26.6 us
  starting transfers between devices: 50 us -> 33.4 us
  local copies, waits for them, and re-layouts: 17.2 us -> 5.07 us
    all_to_all x3 -> x6, blocking collectives: 67.5 us -> 123 us  [exchange(): return lax.all_to_all(a, axes, 0, 0, tiled=True)]
    ppermute x7, waiting for transfers between devices: 37.1 us -> 14.9 us  [right(): return lax.ppermute(a, 'x', FWD)]
    ppermute x7, waiting for transfers between devices: 22.1 us -> 0.02 us  [left(): return lax.ppermute(a, 'x', BWD)]
    all_to_all x3 -> x1, starting transfers between devices: 15.9 us -> 3.57 us  [exchange(): return lax.all_to_all(a, axes, 0, 0, tiled=True)]
    unnamed x60 -> x26, local copies, waits for them, and re-layouts: 12.6 us -> 5.07 us
    ppermute x7 -> x6, starting transfers between devices: 14.7 us -> 9.41 us  [sibling(): return lax.ppermute(a, 'core', SWAP)]
    ppermute x2, waiting for transfers between devices: 3.7 us -> 0.01 us  [across(): return lax.ppermute(a, 'zlo', SWAP)]
    pallas_call x15 -> x18, Pallas kernels: 46.1 us -> 47.2 us  [call(): pl.pallas_call(body, out_shape=outs, in_specs=[small] * scalars + [whole]...]
  transfers between devices with their start and end apart: 26 -> 23, of which waited for: 16 -> 10; matrix products, arithmetic and copies ran while one was open for 1% -> 0% of each run, Pallas kernels for 7% -> 8%
where the time goes in v3:
time: 237 us; the launch traced here: 236 us
  blocking collectives  123 us (52%)
  Pallas kernels  47.2 us (20%)
  starting transfers between devices  33.4 us (14%)
  waiting for transfers between devices  26.6 us (11%)
  local copies, waits for them, and re-layouts  5.07 us (2%)
    all_to_all x6, blocking collectives, exchange(): return lax.all_to_all(a, axes, 0, 0, tiled=True)  123 us
    pallas_call x18, Pallas kernels, call(): pl.pallas_call(body, out_shape=outs, in_specs=[small] * scalars + [whole]...  47.2 us
    ppermute x7, starting transfers between devices, left(): return lax.ppermute(a, 'x', BWD)  16.8 us
    ppermute x7, waiting for transfers between devices, right(): return lax.ppermute(a, 'x', FWD)  14.9 us
    ppermute x6, starting transfers between devices, sibling(): return lax.ppermute(a, 'core', SWAP)  9.41 us
    ppermute x6, waiting for transfers between devices, sibling(): return lax.ppermute(a, 'core', SWAP)  9.01 us
    unnamed x26, local copies, waits for them, and re-layouts  5.07 us
  transfers between devices with their start and end apart: 23, of which 10 were waited for; matrix products, arithmetic and copies ran while one was open for 0% of the time, Pallas kernels for 8%

profile of v3, /device:TPU:1, one launch (start us, length us, event | category | flops | bytes accessed | tf_op | source)
XLA Modules:
  0.0 236.0 jit_solution(6459108058730904771)
XLA Ops:
  9.6 2.5 %collective-permute-start.2 = (bf16[48,16,512]{2,1,0:T(8,128)(2,1)S(1)}, bf16[48,16,512]{2,1,0:T(8,128)(2,1)S(1)}, u32[]{:S(2)}, u32[]{:S(2)}) collective-permute-start(bf16[48,16,512]{2,1,0:T(8,128)(2,1)S(1)} %get-tuple-element.64.refs_0_), channel_id=1, source_target_pairs={{0,48},{16,0},{32,16},{48,32},{1,49},{17,1},{33,17},{49,33},{2,50}... | collective-permute-start | bytes 2359304 | tf_op jit(solution)/shard_map/ppermute | solution.py:35
  12.9 25.0 %all_to_all.35.message = bf16[8,352,128]{2,1,0:T(8,128)(2,1)S(1)} all-to-all(bf16[8,352,128]{2,1,0:T(8,128)(2,1)S(1)} %shard_map.118), channel_id=1, replica_groups=mesh['zlo'=2,'x'=4,'core'=2,'zhi'=2,'y'=4] {'zhi','y'}, dimensions={0} | all-to-all | bytes 1441792 | tf_op jit(solution)/shard_map/all_to_all | solution.py:39
  37.9 2.5 %collective-permute-start.5 = (bf16[48,16,512]{2,1,0:T(8,128)(2,1)S(1)}, bf16[48,16,512]{2,1,0:T(8,128)(2,1)S(1)}, u32[]{:S(2)}, u32[]{:S(2)}) collective-permute-start(bf16[48,16,512]{2,1,0:T(8,128)(2,1)S(1)} %collective-permute-done.3.refs_4_), channel_id=1, source_target_pairs={{0,48},{16,0},{32,16},{48,32},{1,49},{17,1},{33,17},{49,33},{2,50}... | collective-permute-start | bytes 2359304 | tf_op jit(solution)/shard_map/ppermute | solution.py:35
  40.5 4.1 %shard_map.121 = (bf16[8,16,2560]{2,1,0:T(8,128)(2,1)S(1)}, f32[20,16,128]{2,1,0:T(8,128)S(1)}, f32[20,16,128]{2,1,0:T(8,128)S(1)}) custom-call(bf16[8,352,128]{2,1,0:T(8,128)(2,1)S(1)} %all_to_all.35.message), custom_call_target="tpu_custom_call" | custom-call | tf_op jit(solution)/shard_map/pallas_call | solution.py:58
  44.6 15.4 %all_to_all.36.cot = bf16[8,320,128]{2,1,0:T(8,128)(2,1)S(1)} all-to-all(bf16[8,320,128]{2,1,0:T(8,128)(2,1)S(1)} %bitcast.14), channel_id=1, replica_groups=mesh['zlo'=2,'x'=4,'core'=2,'zhi'=2,'y'=4] {'zhi','y'}, dimensions={0} | all-to-all | bytes 1310720 | tf_op jit(solution)/shard_map/all_to_all | solution.py:39
  60.1 2.5 %collective-permute-start.7 = (bf16[48,16,512]{2,1,0:T(8,128)(2,1)S(1)}, bf16[48,16,512]{2,1,0:T(8,128)(2,1)S(1)}, u32[]{:S(2)}, u32[]{:S(2)}) collective-permute-start(bf16[48,16,512]{2,1,0:T(8,128)(2,1)S(1)} %collective-permute-done.5.refs_5_), channel_id=1, source_target_pairs={{0,48},{16,0},{32,16},{48,32},{1,49},{17,1},{33,17},{49,33},{2,50}... | collective-permute-start | bytes 2359304 | tf_op jit(solution)/shard_map/ppermute | solution.py:35
  62.6 13.1 %all_to_all.37.own = bf16[8,16,2560]{2,1,0:T(8,128)(2,1)S(1)} all-to-all(bf16[8,16,2560]{2,1,0:T(8,128)(2,1)S(1)} %get-tuple-element.71), channel_id=1, replica_groups=mesh['zlo'=2,'x'=4,'core'=2,'zhi'=2,'y'=4] {'zhi','y'}, dimensions={0} | all-to-all | bytes 1310720 | tf_op jit(solution)/shard_map/all_to_all | solution.py:39
  77.6 3.5 %collective-permute-start.8 = (bf16[8,16,2560]{2,1,0:T(8,128)(2,1)S(1)}, bf16[8,16,2560]{2,1,0:T(8,128)(2,1)S(1)}, u32[]{:S(2)}, u32[]{:S(2)}) collective-permute-start(bf16[8,16,2560]{2,1,0:T(8,128)(2,1)S(1)} %all_to_all.37.own), channel_id=1, source_target_pairs={{0,8},{8,0},{1,9},{9,1},{2,10},{10,2},{3,11},{11,3},{4,12},{12,4},... | collective-permute-start | bytes 1966088 | tf_op jit(solution)/shard_map/ppermute | solution.py:23
  82.8 3.9 %shard_map.122 = (bf16[320,512]{1,0:T(8,128)(2,1)S(1)}, f32[320,512]{1,0:T(8,128)S(1)}, bf16[320,2048]{1,0:T(8,128)(2,1)S(1)}, bf16[16,128,512]{2,1,0:T(8,128)(2...) custom-call(s32[4]{0:T(128)S(1)} %pad_add_fusion.place, ...), custom_call_target="tpu_custom_call" | custom-call | tf_op jit(solution)/shard_map/pallas_call | solution.py:58
  87.2 2.7 %collective-permute-done.9.refs_1_ = bf16[8,16,5120]{2,1,0:T(8,128)(2,1)S(1)} collective-permute-done((bf16[8,16,5120]{2,1,0:T(8,128)(2,1)S(1)}, bf16[8,16,5120]{2,1,0:T(8,128)(2,1)S(1)}, u32[]{:S(2)}, u32[]{:S(2)}) %collective-permute-start.9) | collective-permute-done | bytes 1310752 | tf_op jit(solution)/shard_map/ppermute | solution.py:23
  90.2 22.7 %all_to_all.38.parts = bf16[8,16,5120]{2,1,0:T(8,128)(2,1)S(1)} all-to-all(bf16[8,16,5120]{2,1,0:T(8,128)(2,1)S(1)} %shard_map.123), channel_id=1, replica_groups=mesh['zlo'=2,'x'=4,'core'=2,'zhi'=2,'y'=4] {'zhi','y'}, dimensions={0} | all-to-all | bytes 2621440 | tf_op jit(solution)/shard_map/all_to_all | solution.py:39
  112.9 5.5 %shard_map.124 = (bf16[8,16,2560]{2,1,0:T(8,128)(2,1)S(1)}, bf16[8,16,5120]{2,1,0:T(8,128)(2,1)S(1)}, f32[128,128]{1,0:T(8,128)S(1)}, f32[8,128]{1,0:T(8,128)S(1)}) custom-call(s32[4]{0:T(128)S(1)} %pad_add_fusion.place, bf16[8,16,5120]{2,1,0:T(8,128)(2,1)S(1)} %all_to_all.38.parts, bf16[8,352,128]{2,1,0:T(8,128)(2,1)S(1)} %all_to_all.35.message, ...), custom_call_target="tpu_custom_call" | custom-call | tf_op jit(solution)/shard_map/pallas_call | solution.py:58
  118.4 21.2 %all_to_all.39.d_own = bf16[8,16,5120]{2,1,0:T(8,128)(2,1)S(1)} all-to-all(bf16[8,16,5120]{2,1,0:T(8,128)(2,1)S(1)} %get-tuple-element.82), channel_id=1, replica_groups=mesh['zlo'=2,'x'=4,'core'=2,'zhi'=2,'y'=4] {'zhi','y'}, dimensions={0} | all-to-all | bytes 2621440 | tf_op jit(solution)/shard_map/all_to_all | solution.py:39
  139.6 2.2 collective-permute-start.10
  141.8 2.7 %collective-permute-done.10.d_sib = bf16[8,16,5120]{2,1,0:T(8,128)(2,1)S(1)} collective-permute-done((bf16[8,16,5120]{2,1,0:T(8,128)(2,1)S(1)}, bf16[8,16,5120]{2,1,0:T(8,128)(2,1)S(1)}, u32[]{:S(2)}, u32[]{:S(2)}) %collective-permute-start.10) | collective-permute-done | bytes 1310752 | tf_op jit(solution)/shard_map/ppermute | solution.py:23
  144.4 8.6 %shard_map.125 = (bf16[24,16,512]{2,1,0:T(8,128)(2,1)}, bf16[24,16,512]{2,1,0:T(8,128)(2,1)}, bf16[24,16,512]{2,1,0:T(8,128)(2,1)S(1)}, bf16[24,16,512]{2,1,0:T(...) custom-call(s32[4]{0:T(128)S(1)} %pad_add_fusion.place, ...), custom_call_target="tpu_custom_call" | custom-call | tf_op jit(solution)/shard_map/pallas_call | solution.py:58
  153.0 2.1 copy-done
  158.2 2.7 %collective-permute-start.15 = (bf16[24,16,512]{2,1,0:T(8,128)(2,1)S(1)}, bf16[24,16,512]{2,1,0:T(8,128)(2,1)}, u32[]{:S(2)}, u32[]{:S(2)}) collective-permute-start(bf16[24,16,512]{2,1,0:T(8,128)(2,1)S(1)} %get-tuple-element.95), channel_id=1, source_target_pairs={{0,48},{16,0},{32,16},{48,32},{1,49},{17,1},{33,17},{49,33},{2,50}... | collective-permute-start | bytes 1179656 | tf_op jit(solution)/shard_map/ppermute | solution.py:35
  162.1 3.6 %all-to-all-start.5 = ((bf16[8,32,2560]{2,1,0:T(8,128)(2,1)}), bf16[8,32,2560]{2,1,0:T(8,128)(2,1)S(1)}, u32[]{:S(2)}, u32[]{:S(2)}) async-start(bf16[8,32,2560]{2,1,0:T(8,128)(2,1)} %shard_map.126), calls=%async_computation.5 | async-start | bytes 2621440 | tf_op jit(solution)/shard_map/all_to_all | solution.py:39
  167.6 2.2 shard_map.127
  169.8 2.2 shard_map.128
  172.0 4.0 %collective-permute-done.14.refs_1_ = bf16[24,16,512]{2,1,0:T(8,128)(2,1)} collective-permute-done((bf16[24,16,512]{2,1,0:T(8,128)(2,1)S(1)}, bf16[24,16,512]{2,1,0:T(8,128)(2,1)}, u32[]{:S(2)}, u32[]{:S(2)}) %collective-permute-start.14) | collective-permute-done | bytes 393248 | tf_op jit(solution)/shard_map/ppermute | solution.py:31
  176.7 2.1 collective-permute-start.19
  178.7 2.2 shard_map.129
  180.9 2.2 shard_map.130
  183.1 2.7 %all-to-all-done.5.back = bf16[8,32,2560]{2,1,0:T(8,128)(2,1)S(1)} async-done(((bf16[8,32,2560]{2,1,0:T(8,128)(2,1)}), bf16[8,32,2560]{2,1,0:T(8,128)(2,1)S(1)}, u32[]{:S(2)}, u32[]{:S(2)}) %all-to-all-start.5) | async-done | bytes 1310752 | tf_op jit(solution)/shard_map/all_to_all | solution.py:39
  185.8 2.9 %shard_map.132 = bf16[128,16,128]{2,1,0:T(8,128)(2,1)S(1)} custom-call(bf16[8,32,2560]{2,1,0:T(8,128)(2,1)S(1)} %all-to-all-done.5.back, f32[20,16,128]{2,1,0:T(8,128)S(1)} %get-tuple-element.103.normal, f32[20,16,128]{2,1,0:T(8,128)S(1)} %get-tuple-element.104.rstds, bf16[8,352,128]{2,1,0:T(8,128)(2,1)S(1)} %all_to_all.35.message, ...), custom_call_target="tpu_custom_call" | custom-call | tf_op jit(solution)/shard_map/pallas_call | solution.py:58
  188.7 7.0 %collective-permute-done.18.refs_1_ = bf16[48,16,512]{2,1,0:T(8,128)(2,1)} collective-permute-done((bf16[48,16,512]{2,1,0:T(8,128)(2,1)}, bf16[48,16,512]{2,1,0:T(8,128)(2,1)}, u32[]{:S(2)}, u32[]{:S(2)}) %collective-permute-start.18) | collective-permute-done | bytes 786464 | tf_op jit(solution)/shard_map/ppermute | solution.py:31
  195.7 2.5 %shard_map.133 = bf16[48,16,512]{2,1,0:T(8,128)(2,1)} custom-call(bf16[288,16,512]{2,1,0:T(8,128)(2,1)} %copy-done, bf16[48,16,512]{2,1,0:T(8,128)(2,1)} %collective-permute-done.18.refs_1_, bf16[48,16,512]{2,1,0:T(8,128)(2,1)} %collective-permute-done.19.refs_2_), custom_call_target="tpu_custom_call" | custom-call | tf_op jit(solution)/shard_map/pallas_call | solution.py:58
  198.6 2.5 %collective-permute-start.17 = (bf16[48,16,512]{2,1,0:T(8,128)(2,1)}, bf16[48,16,512]{2,1,0:T(8,128)(2,1)}, u32[]{:S(2)}, u32[]{:S(2)}) collective-permute-start(bf16[48,16,512]{2,1,0:T(8,128)(2,1)} %shard_map.130), channel_id=1, source_target_pairs={{0,48},{16,0},{32,16},{48,32},{1,49},{17,1},{33,17},{49,33},{2,50}... | collective-permute-start | bytes 2359304 | tf_op jit(solution)/shard_map/ppermute | solution.py:35
  201.1 25.5 %all_to_all.40.last = bf16[128,16,128]{2,1,0:T(8,128)(2,1)S(1)} all-to-all(bf16[128,16,128]{2,1,0:T(8,128)(2,1)S(1)} %shard_map.132), channel_id=1, replica_groups=mesh['zlo'=2,'x'=4,'core'=2,'zhi'=2,'y'=4] {'zlo','x','core','zhi','y'}, dimensions={0} | all-to-all | bytes 1048576 | tf_op jit(solution)/shard_map/all_to_all | solution.py:39
  227.5 3.9 %shard_map.134 = (bf16[128,512]{1,0:T(8,128)(2,1)}, bf16[512,256]{1,0:T(8,128)(2,1)}, bf16[384,512]{1,0:T(8,128)(2,1)}) custom-call(s32[4]{0:T(128)} %copy-done.6, bf16[288,16,512]{2,1,0:T(8,128)(2,1)} %copy-done, bf16[48,16,512]{2,1,0:T(8,128)(2,1)} %collective-permute-done.16.one, bf16[48,16,512]{2,1,0:T(8,128)(2,1)} %collective-permute-done.17.two, ...), custom_call_target="tpu_custom_call" | custom-call | tf_op jit(solution)/shard_map/pallas_call | solution.py:58
  (65 shorter events, 27.1 us)
Async XLA Ops:
  0.6 11.5 %copy-start.9 = (bf16[128,12]{0,1:T(8,128)(2,1)S(1)}, bf16[128,12]{0,1:T(8,128)(2,1)}, u32[]{:S(2)}) copy-start(bf16[128,12]{0,1:T(8,128)(2,1)} %param.11) | copy-start | bytes 9220
  0.6 11.5 %copy-start.8 = (bf16[16,16]{1,0:T(8,128)(2,1)S(1)}, bf16[16,16]{1,0:T(8,128)(2,1)}, u32[]{:S(2)}) copy-start(bf16[16,16]{1,0:T(8,128)(2,1)} %proj.1) | copy-start | bytes 1540
  2.7 141.7 %copy-start.6 = (s32[4]{0:T(128)}, s32[4]{0:T(128)S(1)}, u32[]{:S(2)}) copy-start(s32[4]{0:T(128)S(1)} %pad_add_fusion.place) | copy-start | bytes 52
  2.7 9.4 %copy-start.3 = (bf16[160,16,128]{2,1,0:T(8,128)(2,1)S(1)}, bf16[160,16,128]{2,1,0:T(8,128)(2,1)}, u32[]{:S(2)}) copy-start(bf16[160,16,128]{2,1,0:T(8,128)(2,1)} %param.7) | copy-start | bytes 1966084
  3.4 2.9 %collective-permute-start = (bf16[384,512]{1,0:T(8,128)(2,1)S(1)}, bf16[384,512]{1,0:T(8,128)(2,1)S(1)}, u32[]{:S(2)}, u32[]{:S(2)}) collective-permute-start(bf16[384,512]{1,0:T(8,128)(2,1)S(1)} %shard_map.119), channel_id=1, source_target_pairs={{0,8},{8,0},{1,9},{9,1},{2,10},{10,2},{3,11},{11,3},{4,12},{12,4},... | collective-permute-start | bytes 1179656 | tf_op jit(solution)/shard_map/ppermute | solution.py:23
  7.8 30.1 %collective-permute-start.3 = (bf16[48,16,512]{2,1,0:T(8,128)(2,1)S(1)}, bf16[48,16,512]{2,1,0:T(8,128)(2,1)S(1)}, u32[]{:S(2)}, u32[]{:S(2)}) collective-permute-start(bf16[48,16,512]{2,1,0:T(8,128)(2,1)S(1)} %get-tuple-element.64.refs_0_), channel_id=1, source_target_pairs={{0,64},{64,0},{1,65},{65,1},{2,66},{66,2},{3,67},{67,3},{4,68},{68... | collective-permute-start | bytes 2359304 | tf_op jit(solution)/shard_map/ppermute | solution.py:27
  9.6 28.3 %collective-permute-start.2 = (bf16[48,16,512]{2,1,0:T(8,128)(2,1)S(1)}, bf16[48,16,512]{2,1,0:T(8,128)(2,1)S(1)}, u32[]{:S(2)}, u32[]{:S(2)}) collective-permute-start(bf16[48,16,512]{2,1,0:T(8,128)(2,1)S(1)} %get-tuple-element.64.refs_0_), channel_id=1, source_target_pairs={{0,48},{16,0},{32,16},{48,32},{1,49},{17,1},{33,17},{49,33},{2,50}... | collective-permute-start | bytes 2359304 | tf_op jit(solution)/shard_map/ppermute | solution.py:35
  12.1 25.8 %collective-permute-start.1 = (bf16[48,16,512]{2,1,0:T(8,128)(2,1)S(1)}, bf16[48,16,512]{2,1,0:T(8,128)(2,1)S(1)}, u32[]{:S(2)}, u32[]{:S(2)}) collective-permute-start(bf16[48,16,512]{2,1,0:T(8,128)(2,1)S(1)} %get-tuple-element.64.refs_0_), channel_id=1, source_target_pairs={{0,16},{16,32},{32,48},{48,0},{1,17},{17,33},{33,49},{49,1},{2,18}... | collective-permute-start | bytes 2359304 | tf_op jit(solution)/shard_map/ppermute | solution.py:31
  12.9 31.6 %copy-start.12 = (bf16[160,16,128]{2,1,0:T(8,128)(2,1)S(1)}, bf16[160,16,128]{2,1,0:T(8,128)(2,1)}, u32[]{:S(2)}) copy-start(bf16[160,16,128]{2,1,0:T(8,128)(2,1)} %param.13) | copy-start | bytes 1966084
  37.9 22.0 %collective-permute-start.5 = (bf16[48,16,512]{2,1,0:T(8,128)(2,1)S(1)}, bf16[48,16,512]{2,1,0:T(8,128)(2,1)S(1)}, u32[]{:S(2)}, u32[]{:S(2)}) collective-permute-start(bf16[48,16,512]{2,1,0:T(8,128)(2,1)S(1)} %collective-permute-done.3.refs_4_), channel_id=1, source_target_pairs={{0,48},{16,0},{32,16},{48,32},{1,49},{17,1},{33,17},{49,33},{2,50}... | collective-permute-start | bytes 2359304 | tf_op jit(solution)/shard_map/ppermute | solution.py:35
  40.5 19.4 %collective-permute-start.4 = (bf16[48,16,512]{2,1,0:T(8,128)(2,1)S(1)}, bf16[48,16,512]{2,1,0:T(8,128)(2,1)S(1)}, u32[]{:S(2)}, u32[]{:S(2)}) collective-permute-start(bf16[48,16,512]{2,1,0:T(8,128)(2,1)S(1)} %collective-permute-done.3.refs_4_), channel_id=1, source_target_pairs={{0,16},{16,32},{32,48},{48,0},{1,17},{17,33},{33,49},{49,1},{2,18}... | collective-permute-start | bytes 2359304 | tf_op jit(solution)/shard_map/ppermute | solution.py:31
  59.9 17.7 %collective-permute-start.6 = (bf16[48,16,512]{2,1,0:T(8,128)(2,1)S(1)}, bf16[48,16,512]{2,1,0:T(8,128)(2,1)S(1)}, u32[]{:S(2)}, u32[]{:S(2)}) collective-permute-start(bf16[48,16,512]{2,1,0:T(8,128)(2,1)S(1)} %collective-permute-done.1.refs_3_), channel_id=1, source_target_pairs={{0,16},{16,32},{32,48},{48,0},{1,17},{17,33},{33,49},{49,1},{2,18}... | collective-permute-start | bytes 2359304 | tf_op jit(solution)/shard_map/ppermute | solution.py:31
  60.1 17.5 %collective-permute-start.7 = (bf16[48,16,512]{2,1,0:T(8,128)(2,1)S(1)}, bf16[48,16,512]{2,1,0:T(8,128)(2,1)S(1)}, u32[]{:S(2)}, u32[]{:S(2)}) collective-permute-start(bf16[48,16,512]{2,1,0:T(8,128)(2,1)S(1)} %collective-permute-done.5.refs_5_), channel_id=1, source_target_pairs={{0,48},{16,0},{32,16},{48,32},{1,49},{17,1},{33,17},{49,33},{2,50}... | collective-permute-start | bytes 2359304 | tf_op jit(solution)/shard_map/ppermute | solution.py:35
  77.6 5.2 %collective-permute-start.8 = (bf16[8,16,2560]{2,1,0:T(8,128)(2,1)S(1)}, bf16[8,16,2560]{2,1,0:T(8,128)(2,1)S(1)}, u32[]{:S(2)}, u32[]{:S(2)}) collective-permute-start(bf16[8,16,2560]{2,1,0:T(8,128)(2,1)S(1)} %all_to_all.37.own), channel_id=1, source_target_pairs={{0,8},{8,0},{1,9},{9,1},{2,10},{10,2},{3,11},{11,3},{4,12},{12,4},... | collective-permute-start | bytes 1966088 | tf_op jit(solution)/shard_map/ppermute | solution.py:23
  86.7 3.1 %collective-permute-start.9 = (bf16[8,16,5120]{2,1,0:T(8,128)(2,1)S(1)}, bf16[8,16,5120]{2,1,0:T(8,128)(2,1)S(1)}, u32[]{:S(2)}, u32[]{:S(2)}) collective-permute-start(bf16[8,16,5120]{2,1,0:T(8,128)(2,1)S(1)} %get-tuple-element.80), channel_id=1, source_target_pairs={{0,8},{8,0},{1,9},{9,1},{2,10},{10,2},{3,11},{11,3},{4,12},{12,4},... | collective-permute-start | bytes 3932168 | tf_op jit(solution)/shard_map/ppermute | solution.py:23
  90.1 22.7 %copy-start.10 = (f32[128]{0:T(128)S(1)}, f32[128]{0:T(128)}, u32[]{:S(2)}) copy-start(f32[128]{0:T(128)} %param.12) | copy-start | bytes 1540
  139.6 4.9 %collective-permute-start.10 = (bf16[8,16,5120]{2,1,0:T(8,128)(2,1)S(1)}, bf16[8,16,5120]{2,1,0:T(8,128)(2,1)S(1)}, u32[]{:S(2)}, u32[]{:S(2)}) collective-permute-start(bf16[8,16,5120]{2,1,0:T(8,128)(2,1)S(1)} %all_to_all.39.d_own), channel_id=1, source_target_pairs={{0,8},{8,0},{1,9},{9,1},{2,10},{10,2},{3,11},{11,3},{4,12},{12,4},... | collective-permute-start | bytes 3932168 | tf_op jit(solution)/shard_map/ppermute | solution.py:23
  155.1 5.7 %collective-permute-start.11 = (bf16[8,16,2560]{2,1,0:T(8,128)(2,1)S(1)}, bf16[8,16,2560]{2,1,0:T(8,128)(2,1)S(1)}, u32[]{:S(2)}, u32[]{:S(2)}) collective-permute-start(bf16[8,16,2560]{2,1,0:T(8,128)(2,1)S(1)} %get-tuple-element.89), channel_id=1, source_target_pairs={{0,8},{8,0},{1,9},{9,1},{2,10},{10,2},{3,11},{11,3},{4,12},{12,4},... | collective-permute-start | bytes 1966088 | tf_op jit(solution)/shard_map/ppermute | solution.py:23
  155.5 12.1 %collective-permute-start.12 = (bf16[24,16,512]{2,1,0:T(8,128)(2,1)}, bf16[24,16,512]{2,1,0:T(8,128)(2,1)}, u32[]{:S(2)}, u32[]{:S(2)}) collective-permute-start(bf16[24,16,512]{2,1,0:T(8,128)(2,1)} %get-tuple-element.92), channel_id=1, source_target_pairs={{0,16},{16,32},{32,48},{48,0},{1,17},{17,33},{33,49},{49,1},{2,18}... | collective-permute-start | bytes 1179656 | tf_op jit(solution)/shard_map/ppermute | solution.py:31
  156.2 13.6 %collective-permute-start.13 = (bf16[24,16,512]{2,1,0:T(8,128)(2,1)}, bf16[24,16,512]{2,1,0:T(8,128)(2,1)}, u32[]{:S(2)}, u32[]{:S(2)}) collective-permute-start(bf16[24,16,512]{2,1,0:T(8,128)(2,1)} %get-tuple-element.93), channel_id=1, source_target_pairs={{0,48},{16,0},{32,16},{48,32},{1,49},{17,1},{33,17},{49,33},{2,50}... | collective-permute-start | bytes 1179656 | tf_op jit(solution)/shard_map/ppermute | solution.py:35
  158.2 17.9 %collective-permute-start.14 = (bf16[24,16,512]{2,1,0:T(8,128)(2,1)S(1)}, bf16[24,16,512]{2,1,0:T(8,128)(2,1)}, u32[]{:S(2)}, u32[]{:S(2)}) collective-permute-start(bf16[24,16,512]{2,1,0:T(8,128)(2,1)S(1)} %get-tuple-element.94), channel_id=1, source_target_pairs={{0,16},{16,32},{32,48},{48,0},{1,17},{17,33},{33,49},{49,1},{2,18}... | collective-permute-start | bytes 1179656 | tf_op jit(solution)/shard_map/ppermute | solution.py:31
  158.2 17.9 %collective-permute-start.15 = (bf16[24,16,512]{2,1,0:T(8,128)(2,1)S(1)}, bf16[24,16,512]{2,1,0:T(8,128)(2,1)}, u32[]{:S(2)}, u32[]{:S(2)}) collective-permute-start(bf16[24,16,512]{2,1,0:T(8,128)(2,1)S(1)} %get-tuple-element.95), channel_id=1, source_target_pairs={{0,48},{16,0},{32,16},{48,32},{1,49},{17,1},{33,17},{49,33},{2,50}... | collective-permute-start | bytes 1179656 | tf_op jit(solution)/shard_map/ppermute | solution.py:35
  162.1 23.6 %all-to-all-start.5 = ((bf16[8,32,2560]{2,1,0:T(8,128)(2,1)}), bf16[8,32,2560]{2,1,0:T(8,128)(2,1)S(1)}, u32[]{:S(2)}, u32[]{:S(2)}) async-start(bf16[8,32,2560]{2,1,0:T(8,128)(2,1)} %shard_map.126), calls=%async_computation.5 | async-start | bytes 2621440 | tf_op jit(solution)/shard_map/all_to_all | solution.py:39
  176.0 19.6 %collective-permute-start.18 = (bf16[48,16,512]{2,1,0:T(8,128)(2,1)}, bf16[48,16,512]{2,1,0:T(8,128)(2,1)}, u32[]{:S(2)}, u32[]{:S(2)}) collective-permute-start(bf16[48,16,512]{2,1,0:T(8,128)(2,1)} %shard_map.127), channel_id=1, source_target_pairs={{0,16},{16,32},{32,48},{48,0},{1,17},{17,33},{33,49},{49,1},{2,18}... | collective-permute-start | bytes 2359304 | tf_op jit(solution)/shard_map/ppermute | solution.py:31
  176.7 19.0 %collective-permute-start.19 = (bf16[48,16,512]{2,1,0:T(8,128)(2,1)}, bf16[48,16,512]{2,1,0:T(8,128)(2,1)}, u32[]{:S(2)}, u32[]{:S(2)}) collective-permute-start(bf16[48,16,512]{2,1,0:T(8,128)(2,1)} %shard_map.128), channel_id=1, source_target_pairs={{0,48},{16,0},{32,16},{48,32},{1,49},{17,1},{33,17},{49,33},{2,50}... | collective-permute-start | bytes 2359304 | tf_op jit(solution)/shard_map/ppermute | solution.py:35
  198.2 28.3 %collective-permute-start.20 = (bf16[48,16,512]{2,1,0:T(8,128)(2,1)}, bf16[48,16,512]{2,1,0:T(8,128)(2,1)S(1)}, u32[]{:S(2)}, u32[]{:S(2)}) collective-permute-start(bf16[48,16,512]{2,1,0:T(8,128)(2,1)} %shard_map.133), channel_id=1, source_target_pairs={{0,64},{64,0},{1,65},{65,1},{2,66},{66,2},{3,67},{67,3},{4,68},{68... | collective-permute-start | bytes 2359304 | tf_op jit(solution)/shard_map/ppermute | solution.py:27
  198.3 28.2 %collective-permute-start.16 = (bf16[48,16,512]{2,1,0:T(8,128)(2,1)}, bf16[48,16,512]{2,1,0:T(8,128)(2,1)}, u32[]{:S(2)}, u32[]{:S(2)}) collective-permute-start(bf16[48,16,512]{2,1,0:T(8,128)(2,1)} %shard_map.129), channel_id=1, source_target_pairs={{0,16},{16,32},{32,48},{48,0},{1,17},{17,33},{33,49},{49,1},{2,18}... | collective-permute-start | bytes 2359304 | tf_op jit(solution)/shard_map/ppermute | solution.py:31
  198.6 28.0 %collective-permute-start.17 = (bf16[48,16,512]{2,1,0:T(8,128)(2,1)}, bf16[48,16,512]{2,1,0:T(8,128)(2,1)}, u32[]{:S(2)}, u32[]{:S(2)}) collective-permute-start(bf16[48,16,512]{2,1,0:T(8,128)(2,1)} %shard_map.130), channel_id=1, source_target_pairs={{0,48},{16,0},{32,16},{48,32},{1,49},{17,1},{33,17},{49,33},{2,50}... | collective-permute-start | bytes 2359304 | tf_op jit(solution)/shard_map/ppermute | solution.py:35
  231.4 3.0 %copy-start.4 = (bf16[512,256]{1,0:T(8,128)(2,1)S(1)}, bf16[512,256]{1,0:T(8,128)(2,1)}, u32[]{:S(2)}) copy-start(bf16[512,256]{1,0:T(8,128)(2,1)} %get-tuple-element.114.down_kept) | copy-start | bytes 786436
  231.4 3.0 %copy-start.5 = (bf16[128,512]{1,0:T(8,128)(2,1)S(1)}, bf16[128,512]{1,0:T(8,128)(2,1)}, u32[]{:S(2)}) copy-start(bf16[128,512]{1,0:T(8,128)(2,1)} %get-tuple-element.113.up_kept) | copy-start | bytes 393220
  231.4 3.0 %copy-start.7 = (s32[4]{0:T(128)S(1)}, s32[4]{0:T(128)}, u32[]{:S(2)}) copy-start(s32[4]{0:T(128)} %copy-done.6) | copy-start | bytes 52
  231.4 2.9 %collective-permute-start.21 = (bf16[384,512]{1,0:T(8,128)(2,1)}, bf16[384,512]{1,0:T(8,128)(2,1)S(1)}, u32[]{:S(2)}, u32[]{:S(2)}) collective-permute-start(bf16[384,512]{1,0:T(8,128)(2,1)} %get-tuple-element.115), channel_id=1, source_target_pairs={{0,8},{8,0},{1,9},{9,1},{2,10},{10,2},{3,11},{11,3},{4,12},{12,4},... | collective-permute-start | bytes 1179656 | tf_op jit(solution)/shard_map/ppermute | solution.py:23
  (4 other events, 5.1 us)

commit v4 on v3

--- a/solution.py
+++ b/solution.py
@@ -207,10 +207,9 @@
     out[:, 16:] = layer[...]
 
 
-def split_kernel(place, late, one, two, three, up_kept, down_kept, sent, held, total, *sems):
+def split_kernel(place, one, two, up_kept, down_kept, sent, held, total, *sems):
     core = place[0]
-    whole = [(start, 0, 48) for start in (0, 0, 0, 0)]
-    add_kernel(whole, late, one, two, three, None, held, total, *sems)
+    add_kernel([(0, 0, 48)] * 2, one, two, None, held, total, *sems)
     total = total[...]
     up, down = total[:16].reshape(256, 512), total[16:].reshape(512, 512)
     up_kept[...] = dot(chip_rows(core), up, ((0,), (0,))).astype(BF)
@@ -292,7 +291,7 @@
         rstds[b] = jnp.broadcast_to(rstd, (16, 128))
         return carry
 
-    lax.fori_loop(0, OWN, sample, 0, unroll=5)
+    lax.fori_loop(0, OWN, sample, 0, unroll=10)
     for k in range(16):
         block = normal[:, k, :]
         quarter, tail = k // 4 * 4, k % 4 * 128
@@ -415,7 +414,7 @@
         mix_part[...] += dot(dsum.astype(BF), tokens, ((1,), (1,)))
         return carry
 
-    lax.fori_loop(0, OWN, sample, 0, unroll=5)
+    lax.fori_loop(0, OWN, sample, 0, unroll=10)
     for r in range(8):
         quarter, tail = r // 2 * 4, r % 2 * 512
         for u in range(4):
@@ -450,7 +449,7 @@
         proj_part[...] += dot(d_proj.astype(BF), tokens, ((1,), (1,)))
         return carry
 
-    lax.fori_loop(0, OWN, sample, 0, unroll=5)
+    lax.fori_loop(0, OWN, sample, 0, unroll=10)
     repeat = one_where((16, 128), lambda k, lane: lane % 16 == k)
     spread = dot(proj_part[...].astype(BF), repeat, ((0,), (0,)))
     token = lax.broadcasted_iota(jnp.int32, (128, 128), 0)
@@ -636,20 +635,17 @@
     )
     from_left1, from_right1, last = together(from_left1, from_right1, last)
     over = add((late, 48), (from_left1, 0), (from_right1, 0))
-    over, last = together(over, last)
     other = across(over)
-    last, other = together(exchange(last, ALL), other)
+    last = exchange(last, ALL)
     up_kept, down_kept, sent = call(
         split_kernel,
         [shape((128, 512)), shape((512, 256)), shape((384, 512))],
         place,
-        late,
-        from_left0,
-        from_right0,
+        add((late, 0), (from_left0, 0), (from_right0, 0)),
         other,
-        scratch=add_scratch(4),
-        scalars=1,
-        remote_in=4,
+        scratch=add_scratch(2),
+        scalars=1,
+        remote_in=2,
         room=60,
     )
     up_grad, down_grad, gain_grad, mix_grad, proj_grad = call(

time: 237 us -> 231 us (0.975)
  blocking collectives: 123 us -> 98.7 us
  starting transfers between devices: 33.4 us -> 46 us
  waiting for transfers between devices: 26.6 us -> 31.4 us
    all_to_all x6 -> x5, blocking collectives: 123 us -> 98.7 us  [exchange(): return lax.all_to_all(a, axes, 0, 0, tiled=True)]
    all_to_all x1 -> x2, starting transfers between devices: 3.57 us -> 13 us  [exchange(): return lax.all_to_all(a, axes, 0, 0, tiled=True)]
    ppermute x2, waiting for transfers between devices: 0.01 us -> 3.54 us  [across(): return lax.ppermute(a, 'zlo', SWAP)]
    ppermute x6, starting transfers between devices: 9.41 us -> 12.7 us  [sibling(): return lax.ppermute(a, 'core', SWAP)]
    pallas_call x18 -> x19, Pallas kernels: 47.2 us -> 47.8 us  [call(): pl.pallas_call(body, out_shape=outs, in_specs=[small] * scalars + [whole]...]
  transfers between devices with their start and end apart: 23 -> 24, of which waited for: 10 -> 13; matrix products, arithmetic and copies ran while one was open for 0% -> 0% of each run, Pallas kernels for 8% -> 12%
where the time goes in v4:
time: 231 us; the launch traced here: 230 us
  blocking collectives  98.7 us (43%)
  Pallas kernels  47.8 us (21%)
  starting transfers between devices  46 us (20%)
  waiting for transfers between devices  31.4 us (14%)
  local copies, waits for them, and re-layouts  5.05 us (2%)
    all_to_all x5, blocking collectives, exchange(): return lax.all_to_all(a, axes, 0, 0, tiled=True)  98.7 us
    pallas_call x19, Pallas kernels, call(): pl.pallas_call(body, out_shape=outs, in_specs=[small] * scalars + [whole]...  47.8 us
    ppermute x7, starting transfers between devices, left(): return lax.ppermute(a, 'x', BWD)  17.5 us
    ppermute x7, waiting for transfers between devices, right(): return lax.ppermute(a, 'x', FWD)  16.1 us
    all_to_all x2, starting transfers between devices, exchange(): return lax.all_to_all(a, axes, 0, 0, tiled=True)  13 us
    ppermute x6, starting transfers between devices, sibling(): return lax.ppermute(a, 'core', SWAP)  12.7 us
    ppermute x6, waiting for transfers between devices, sibling(): return lax.ppermute(a, 'core', SWAP)  9.01 us
    unnamed x26, local copies, waits for them, and re-layouts  5.05 us
  transfers between devices with their start and end apart: 24, of which 13 were waited for; matrix products, arithmetic and copies ran while one was open for 0% of the time, Pallas kernels for 12%

profile of v4, /device:TPU:1, one launch (start us, length us, event | category | flops | bytes accessed | tf_op | source)
XLA Modules:
  0.0 229.9 jit_solution(8654926469067054674)
XLA Ops:
  9.6 2.5 %collective-permute-start.2 = (bf16[48,16,512]{2,1,0:T(8,128)(2,1)S(1)}, bf16[48,16,512]{2,1,0:T(8,128)(2,1)S(1)}, u32[]{:S(2)}, u32[]{:S(2)}) collective-permute-start(bf16[48,16,512]{2,1,0:T(8,128)(2,1)S(1)} %get-tuple-element.60.refs_0_), channel_id=1, source_target_pairs={{0,48},{16,0},{32,16},{48,32},{1,49},{17,1},{33,17},{49,33},{2,50}... | collective-permute-start | bytes 2359304 | tf_op jit(solution)/shard_map/ppermute | solution.py:35
  12.9 25.0 %all_to_all.35.message = bf16[8,352,128]{2,1,0:T(8,128)(2,1)S(1)} all-to-all(bf16[8,352,128]{2,1,0:T(8,128)(2,1)S(1)} %shard_map.118), channel_id=1, replica_groups=mesh['zlo'=2,'x'=4,'core'=2,'zhi'=2,'y'=4] {'zhi','y'}, dimensions={0} | all-to-all | bytes 1441792 | tf_op jit(solution)/shard_map/all_to_all | solution.py:39
  37.9 2.5 %collective-permute-start.5 = (bf16[48,16,512]{2,1,0:T(8,128)(2,1)S(1)}, bf16[48,16,512]{2,1,0:T(8,128)(2,1)S(1)}, u32[]{:S(2)}, u32[]{:S(2)}) collective-permute-start(bf16[48,16,512]{2,1,0:T(8,128)(2,1)S(1)} %collective-permute-done.3.refs_4_), channel_id=1, source_target_pairs={{0,48},{16,0},{32,16},{48,32},{1,49},{17,1},{33,17},{49,33},{2,50}... | collective-permute-start | bytes 2359304 | tf_op jit(solution)/shard_map/ppermute | solution.py:35
  40.5 3.3 %shard_map.121 = (bf16[8,16,2560]{2,1,0:T(8,128)(2,1)S(1)}, f32[20,16,128]{2,1,0:T(8,128)S(1)}, f32[20,16,128]{2,1,0:T(8,128)S(1)}) custom-call(bf16[8,352,128]{2,1,0:T(8,128)(2,1)S(1)} %all_to_all.35.message), custom_call_target="tpu_custom_call" | custom-call | tf_op jit(solution)/shard_map/pallas_call | solution.py:58
  43.8 15.4 %all_to_all.36.cot = bf16[8,320,128]{2,1,0:T(8,128)(2,1)S(1)} all-to-all(bf16[8,320,128]{2,1,0:T(8,128)(2,1)S(1)} %bitcast.14), channel_id=1, replica_groups=mesh['zlo'=2,'x'=4,'core'=2,'zhi'=2,'y'=4] {'zhi','y'}, dimensions={0} | all-to-all | bytes 1310720 | tf_op jit(solution)/shard_map/all_to_all | solution.py:39
  59.3 2.6 %collective-permute-start.7 = (bf16[48,16,512]{2,1,0:T(8,128)(2,1)S(1)}, bf16[48,16,512]{2,1,0:T(8,128)(2,1)S(1)}, u32[]{:S(2)}, u32[]{:S(2)}) collective-permute-start(bf16[48,16,512]{2,1,0:T(8,128)(2,1)S(1)} %collective-permute-done.5.refs_5_), channel_id=1, source_target_pairs={{0,48},{16,0},{32,16},{48,32},{1,49},{17,1},{33,17},{49,33},{2,50}... | collective-permute-start | bytes 2359304 | tf_op jit(solution)/shard_map/ppermute | solution.py:35
  61.9 13.8 %all_to_all.37.own = bf16[8,16,2560]{2,1,0:T(8,128)(2,1)S(1)} all-to-all(bf16[8,16,2560]{2,1,0:T(8,128)(2,1)S(1)} %get-tuple-element.67), channel_id=1, replica_groups=mesh['zlo'=2,'x'=4,'core'=2,'zhi'=2,'y'=4] {'zhi','y'}, dimensions={0} | all-to-all | bytes 1310720 | tf_op jit(solution)/shard_map/all_to_all | solution.py:39
  77.0 3.4 %collective-permute-start.8 = (bf16[8,16,2560]{2,1,0:T(8,128)(2,1)S(1)}, bf16[8,16,2560]{2,1,0:T(8,128)(2,1)S(1)}, u32[]{:S(2)}, u32[]{:S(2)}) collective-permute-start(bf16[8,16,2560]{2,1,0:T(8,128)(2,1)S(1)} %all_to_all.37.own), channel_id=1, source_target_pairs={{0,8},{8,0},{1,9},{9,1},{2,10},{10,2},{3,11},{11,3},{4,12},{12,4},... | collective-permute-start | bytes 1966088 | tf_op jit(solution)/shard_map/ppermute | solution.py:23
  82.1 3.9 %shard_map.122 = (bf16[320,512]{1,0:T(8,128)(2,1)S(1)}, f32[320,512]{1,0:T(8,128)S(1)}, bf16[320,2048]{1,0:T(8,128)(2,1)S(1)}, bf16[16,128,512]{2,1,0:T(8,128)(2...) custom-call(s32[4]{0:T(128)S(1)} %pad_add_fusion.place, ...), custom_call_target="tpu_custom_call" | custom-call | tf_op jit(solution)/shard_map/pallas_call | solution.py:58
  86.5 2.7 %collective-permute-done.9.refs_1_ = bf16[8,16,5120]{2,1,0:T(8,128)(2,1)S(1)} collective-permute-done((bf16[8,16,5120]{2,1,0:T(8,128)(2,1)S(1)}, bf16[8,16,5120]{2,1,0:T(8,128)(2,1)S(1)}, u32[]{:S(2)}, u32[]{:S(2)}) %collective-permute-start.9) | collective-permute-done | bytes 1310752 | tf_op jit(solution)/shard_map/ppermute | solution.py:23
  89.5 23.4 %all_to_all.38.parts = bf16[8,16,5120]{2,1,0:T(8,128)(2,1)S(1)} all-to-all(bf16[8,16,5120]{2,1,0:T(8,128)(2,1)S(1)} %shard_map.123), channel_id=1, replica_groups=mesh['zlo'=2,'x'=4,'core'=2,'zhi'=2,'y'=4] {'zhi','y'}, dimensions={0} | all-to-all | bytes 2621440 | tf_op jit(solution)/shard_map/all_to_all | solution.py:39
  112.9 4.7 %shard_map.124 = (bf16[8,16,2560]{2,1,0:T(8,128)(2,1)S(1)}, bf16[8,16,5120]{2,1,0:T(8,128)(2,1)S(1)}, f32[128,128]{1,0:T(8,128)S(1)}, f32[8,128]{1,0:T(8,128)S(1)}) custom-call(s32[4]{0:T(128)S(1)} %pad_add_fusion.place, bf16[8,16,5120]{2,1,0:T(8,128)(2,1)S(1)} %all_to_all.38.parts, bf16[8,352,128]{2,1,0:T(8,128)(2,1)S(1)} %all_to_all.35.message, ...), custom_call_target="tpu_custom_call" | custom-call | tf_op jit(solution)/shard_map/pallas_call | solution.py:58
  117.5 21.2 %all_to_all.39.d_own = bf16[8,16,5120]{2,1,0:T(8,128)(2,1)S(1)} all-to-all(bf16[8,16,5120]{2,1,0:T(8,128)(2,1)S(1)} %get-tuple-element.78), channel_id=1, replica_groups=mesh['zlo'=2,'x'=4,'core'=2,'zhi'=2,'y'=4] {'zhi','y'}, dimensions={0} | all-to-all | bytes 2621440 | tf_op jit(solution)/shard_map/all_to_all | solution.py:39
  138.7 2.2 collective-permute-start.10
  140.9 2.7 %collective-permute-done.10.d_sib = bf16[8,16,5120]{2,1,0:T(8,128)(2,1)S(1)} collective-permute-done((bf16[8,16,5120]{2,1,0:T(8,128)(2,1)S(1)}, bf16[8,16,5120]{2,1,0:T(8,128)(2,1)S(1)}, u32[]{:S(2)}, u32[]{:S(2)}) %collective-permute-start.10) | collective-permute-done | bytes 1310752 | tf_op jit(solution)/shard_map/ppermute | solution.py:23
  143.6 8.6 %shard_map.125 = (bf16[24,16,512]{2,1,0:T(8,128)(2,1)}, bf16[24,16,512]{2,1,0:T(8,128)(2,1)}, bf16[24,16,512]{2,1,0:T(8,128)(2,1)S(1)}, bf16[24,16,512]{2,1,0:T(...) custom-call(s32[4]{0:T(128)S(1)} %pad_add_fusion.place, ...), custom_call_target="tpu_custom_call" | custom-call | tf_op jit(solution)/shard_map/pallas_call | solution.py:58
  154.7 2.7 %collective-permute-start.13 = (bf16[24,16,512]{2,1,0:T(8,128)(2,1)}, bf16[24,16,512]{2,1,0:T(8,128)(2,1)}, u32[]{:S(2)}, u32[]{:S(2)}) collective-permute-start(bf16[24,16,512]{2,1,0:T(8,128)(2,1)} %get-tuple-element.89), channel_id=1, source_target_pairs={{0,48},{16,0},{32,16},{48,32},{1,49},{17,1},{33,17},{49,33},{2,50}... | collective-permute-start | bytes 1179656 | tf_op jit(solution)/shard_map/ppermute | solution.py:35
  157.4 2.7 %collective-permute-start.15 = (bf16[24,16,512]{2,1,0:T(8,128)(2,1)S(1)}, bf16[24,16,512]{2,1,0:T(8,128)(2,1)}, u32[]{:S(2)}, u32[]{:S(2)}) collective-permute-start(bf16[24,16,512]{2,1,0:T(8,128)(2,1)S(1)} %get-tuple-element.91), channel_id=1, source_target_pairs={{0,48},{16,0},{32,16},{48,32},{1,49},{17,1},{33,17},{49,33},{2,50}... | collective-permute-start | bytes 1179656 | tf_op jit(solution)/shard_map/ppermute | solution.py:35
  161.3 3.6 %all-to-all-start.5 = ((bf16[8,32,2560]{2,1,0:T(8,128)(2,1)}), bf16[8,32,2560]{2,1,0:T(8,128)(2,1)S(1)}, u32[]{:S(2)}, u32[]{:S(2)}) async-start(bf16[8,32,2560]{2,1,0:T(8,128)(2,1)} %shard_map.126), calls=%async_computation.5 | async-start | bytes 2621440 | tf_op jit(solution)/shard_map/all_to_all | solution.py:39
  166.8 2.2 shard_map.127
  171.2 4.0 %collective-permute-done.14.refs_1_ = bf16[24,16,512]{2,1,0:T(8,128)(2,1)} collective-permute-done((bf16[24,16,512]{2,1,0:T(8,128)(2,1)S(1)}, bf16[24,16,512]{2,1,0:T(8,128)(2,1)}, u32[]{:S(2)}, u32[]{:S(2)}) %collective-permute-start.14) | collective-permute-done | bytes 393248 | tf_op jit(solution)/shard_map/ppermute | solution.py:31
  182.2 2.7 %all-to-all-done.5.back = bf16[8,32,2560]{2,1,0:T(8,128)(2,1)S(1)} async-done(((bf16[8,32,2560]{2,1,0:T(8,128)(2,1)}), bf16[8,32,2560]{2,1,0:T(8,128)(2,1)S(1)}, u32[]{:S(2)}, u32[]{:S(2)}) %all-to-all-start.5) | async-done | bytes 1310752 | tf_op jit(solution)/shard_map/all_to_all | solution.py:39
  185.0 2.7 %collective-permute-start.17 = (bf16[48,16,512]{2,1,0:T(8,128)(2,1)}, bf16[48,16,512]{2,1,0:T(8,128)(2,1)}, u32[]{:S(2)}, u32[]{:S(2)}) collective-permute-start(bf16[48,16,512]{2,1,0:T(8,128)(2,1)} %shard_map.130), channel_id=1, source_target_pairs={{0,48},{16,0},{32,16},{48,32},{1,49},{17,1},{33,17},{49,33},{2,50}... | collective-permute-start | bytes 2359304 | tf_op jit(solution)/shard_map/ppermute | solution.py:35
  187.6 3.1 %shard_map.133 = bf16[128,16,128]{2,1,0:T(8,128)(2,1)} custom-call(bf16[8,32,2560]{2,1,0:T(8,128)(2,1)S(1)} %all-to-all-done.5.back, f32[20,16,128]{2,1,0:T(8,128)S(1)} %get-tuple-element.99.normal, f32[20,16,128]{2,1,0:T(8,128)S(1)} %get-tuple-element.100.rstds, bf16[8,352,128]{2,1,0:T(8,128)(2,1)S(1)} %all_to_all.35.message, ...), custom_call_target="tpu_custom_call" | custom-call | tf_op jit(solution)/shard_map/pallas_call | solution.py:58
  190.7 4.1 %collective-permute-done.18.refs_1_ = bf16[48,16,512]{2,1,0:T(8,128)(2,1)} collective-permute-done((bf16[48,16,512]{2,1,0:T(8,128)(2,1)}, bf16[48,16,512]{2,1,0:T(8,128)(2,1)}, u32[]{:S(2)}, u32[]{:S(2)}) %collective-permute-start.18) | collective-permute-done | bytes 786464 | tf_op jit(solution)/shard_map/ppermute | solution.py:31
  194.9 2.5 %shard_map.134 = bf16[48,16,512]{2,1,0:T(8,128)(2,1)} custom-call(bf16[288,16,512]{2,1,0:T(8,128)(2,1)} %copy-done, bf16[48,16,512]{2,1,0:T(8,128)(2,1)} %collective-permute-done.18.refs_1_, bf16[48,16,512]{2,1,0:T(8,128)(2,1)} %collective-permute-done.19.refs_2_), custom_call_target="tpu_custom_call" | custom-call | tf_op jit(solution)/shard_map/pallas_call | solution.py:58
  197.5 9.4 %all-to-all-start.6 = ((bf16[128,16,128]{2,1,0:T(8,128)(2,1)}), bf16[128,16,128]{2,1,0:T(8,128)(2,1)S(1)}, u32[]{:S(2)}, u32[]{:S(2)}) async-start(bf16[128,16,128]{2,1,0:T(8,128)(2,1)} %shard_map.133), calls=%async_computation.6 | async-start | bytes 1048576 | tf_op jit(solution)/shard_map/all_to_all | solution.py:39
  206.9 4.7 %collective-permute-done.16.refs_1_ = bf16[48,16,512]{2,1,0:T(8,128)(2,1)S(1)} collective-permute-done((bf16[48,16,512]{2,1,0:T(8,128)(2,1)}, bf16[48,16,512]{2,1,0:T(8,128)(2,1)S(1)}, u32[]{:S(2)}, u32[]{:S(2)}) %collective-permute-start.16) | collective-permute-done | bytes 786464 | tf_op jit(solution)/shard_map/ppermute | solution.py:31
  212.5 2.5 %shard_map.132.one = bf16[48,16,512]{2,1,0:T(8,128)(2,1)} custom-call(bf16[288,16,512]{2,1,0:T(8,128)(2,1)} %copy-done, bf16[48,16,512]{2,1,0:T(8,128)(2,1)} %copy-done.11, bf16[48,16,512]{2,1,0:T(8,128)(2,1)} %collective-permute-done.17.refs_2_), custom_call_target="tpu_custom_call" | custom-call | tf_op jit(solution)/shard_map/pallas_call | solution.py:58
  215.0 3.5 %collective-permute-done.20.two = bf16[48,16,512]{2,1,0:T(8,128)(2,1)} collective-permute-done((bf16[48,16,512]{2,1,0:T(8,128)(2,1)}, bf16[48,16,512]{2,1,0:T(8,128)(2,1)}, u32[]{:S(2)}, u32[]{:S(2)}) %collective-permute-start.20) | collective-permute-done | bytes 786464 | tf_op jit(solution)/shard_map/ppermute | solution.py:27
  218.6 3.4 %shard_map.135 = (bf16[128,512]{1,0:T(8,128)(2,1)}, bf16[512,256]{1,0:T(8,128)(2,1)}, bf16[384,512]{1,0:T(8,128)(2,1)}) custom-call(s32[4]{0:T(128)} %copy-done.6, bf16[48,16,512]{2,1,0:T(8,128)(2,1)} %shard_map.132.one, bf16[48,16,512]{2,1,0:T(8,128)(2,1)} %collective-permute-done.20.two), custom_call_target="tpu_custom_call" | custom-call | tf_op jit(solution)/shard_map/pallas_call | solution.py:58
  222.0 4.7 %collective-permute-start.21 = (bf16[384,512]{1,0:T(8,128)(2,1)}, bf16[384,512]{1,0:T(8,128)(2,1)S(1)}, u32[]{:S(2)}, u32[]{:S(2)}) collective-permute-start(bf16[384,512]{1,0:T(8,128)(2,1)} %get-tuple-element.107), channel_id=1, source_target_pairs={{0,8},{8,0},{1,9},{9,1},{2,10},{10,2},{3,11},{11,3},{4,12},{12,4},... | collective-permute-start | bytes 1179656 | tf_op jit(solution)/shard_map/ppermute | solution.py:23
  (67 shorter events, 32.8 us)
Async XLA Ops:
  0.6 11.5 %copy-start.9 = (bf16[128,12]{0,1:T(8,128)(2,1)S(1)}, bf16[128,12]{0,1:T(8,128)(2,1)}, u32[]{:S(2)}) copy-start(bf16[128,12]{0,1:T(8,128)(2,1)} %param.11) | copy-start | bytes 9220
  0.6 11.5 %copy-start.8 = (bf16[16,16]{1,0:T(8,128)(2,1)S(1)}, bf16[16,16]{1,0:T(8,128)(2,1)}, u32[]{:S(2)}) copy-start(bf16[16,16]{1,0:T(8,128)(2,1)} %proj.1) | copy-start | bytes 1540
  2.7 140.9 %copy-start.6 = (s32[4]{0:T(128)}, s32[4]{0:T(128)S(1)}, u32[]{:S(2)}) copy-start(s32[4]{0:T(128)S(1)} %pad_add_fusion.place) | copy-start | bytes 52
  2.7 9.4 %copy-start.3 = (bf16[160,16,128]{2,1,0:T(8,128)(2,1)S(1)}, bf16[160,16,128]{2,1,0:T(8,128)(2,1)}, u32[]{:S(2)}) copy-start(bf16[160,16,128]{2,1,0:T(8,128)(2,1)} %param.7) | copy-start | bytes 1966084
  3.4 2.9 %collective-permute-start = (bf16[384,512]{1,0:T(8,128)(2,1)S(1)}, bf16[384,512]{1,0:T(8,128)(2,1)S(1)}, u32[]{:S(2)}, u32[]{:S(2)}) collective-permute-start(bf16[384,512]{1,0:T(8,128)(2,1)S(1)} %shard_map.119), channel_id=1, source_target_pairs={{0,8},{8,0},{1,9},{9,1},{2,10},{10,2},{3,11},{11,3},{4,12},{12,4},... | collective-permute-start | bytes 1179656 | tf_op jit(solution)/shard_map/ppermute | solution.py:23
  7.8 30.1 %collective-permute-start.3 = (bf16[48,16,512]{2,1,0:T(8,128)(2,1)S(1)}, bf16[48,16,512]{2,1,0:T(8,128)(2,1)S(1)}, u32[]{:S(2)}, u32[]{:S(2)}) collective-permute-start(bf16[48,16,512]{2,1,0:T(8,128)(2,1)S(1)} %get-tuple-element.60.refs_0_), channel_id=1, source_target_pairs={{0,64},{64,0},{1,65},{65,1},{2,66},{66,2},{3,67},{67,3},{4,68},{68... | collective-permute-start | bytes 2359304 | tf_op jit(solution)/shard_map/ppermute | solution.py:27
  9.6 28.3 %collective-permute-start.2 = (bf16[48,16,512]{2,1,0:T(8,128)(2,1)S(1)}, bf16[48,16,512]{2,1,0:T(8,128)(2,1)S(1)}, u32[]{:S(2)}, u32[]{:S(2)}) collective-permute-start(bf16[48,16,512]{2,1,0:T(8,128)(2,1)S(1)} %get-tuple-element.60.refs_0_), channel_id=1, source_target_pairs={{0,48},{16,0},{32,16},{48,32},{1,49},{17,1},{33,17},{49,33},{2,50}... | collective-permute-start | bytes 2359304 | tf_op jit(solution)/shard_map/ppermute | solution.py:35
  12.1 25.8 %collective-permute-start.1 = (bf16[48,16,512]{2,1,0:T(8,128)(2,1)S(1)}, bf16[48,16,512]{2,1,0:T(8,128)(2,1)S(1)}, u32[]{:S(2)}, u32[]{:S(2)}) collective-permute-start(bf16[48,16,512]{2,1,0:T(8,128)(2,1)S(1)} %get-tuple-element.60.refs_0_), channel_id=1, source_target_pairs={{0,16},{16,32},{32,48},{48,0},{1,17},{17,33},{33,49},{49,1},{2,18}... | collective-permute-start | bytes 2359304 | tf_op jit(solution)/shard_map/ppermute | solution.py:31
  12.9 30.9 %copy-start.12 = (bf16[160,16,128]{2,1,0:T(8,128)(2,1)S(1)}, bf16[160,16,128]{2,1,0:T(8,128)(2,1)}, u32[]{:S(2)}) copy-start(bf16[160,16,128]{2,1,0:T(8,128)(2,1)} %param.13) | copy-start | bytes 1966084
  37.9 21.2 %collective-permute-start.5 = (bf16[48,16,512]{2,1,0:T(8,128)(2,1)S(1)}, bf16[48,16,512]{2,1,0:T(8,128)(2,1)S(1)}, u32[]{:S(2)}, u32[]{:S(2)}) collective-permute-start(bf16[48,16,512]{2,1,0:T(8,128)(2,1)S(1)} %collective-permute-done.3.refs_4_), channel_id=1, source_target_pairs={{0,48},{16,0},{32,16},{48,32},{1,49},{17,1},{33,17},{49,33},{2,50}... | collective-permute-start | bytes 2359304 | tf_op jit(solution)/shard_map/ppermute | solution.py:35
  40.5 18.8 %collective-permute-start.4 = (bf16[48,16,512]{2,1,0:T(8,128)(2,1)S(1)}, bf16[48,16,512]{2,1,0:T(8,128)(2,1)S(1)}, u32[]{:S(2)}, u32[]{:S(2)}) collective-permute-start(bf16[48,16,512]{2,1,0:T(8,128)(2,1)S(1)} %collective-permute-done.3.refs_4_), channel_id=1, source_target_pairs={{0,16},{16,32},{32,48},{48,0},{1,17},{17,33},{33,49},{49,1},{2,18}... | collective-permute-start | bytes 2359304 | tf_op jit(solution)/shard_map/ppermute | solution.py:31
  59.2 17.7 %collective-permute-start.6 = (bf16[48,16,512]{2,1,0:T(8,128)(2,1)S(1)}, bf16[48,16,512]{2,1,0:T(8,128)(2,1)S(1)}, u32[]{:S(2)}, u32[]{:S(2)}) collective-permute-start(bf16[48,16,512]{2,1,0:T(8,128)(2,1)S(1)} %collective-permute-done.1.refs_3_), channel_id=1, source_target_pairs={{0,16},{16,32},{32,48},{48,0},{1,17},{17,33},{33,49},{49,1},{2,18}... | collective-permute-start | bytes 2359304 | tf_op jit(solution)/shard_map/ppermute | solution.py:31
  59.3 17.7 %collective-permute-start.7 = (bf16[48,16,512]{2,1,0:T(8,128)(2,1)S(1)}, bf16[48,16,512]{2,1,0:T(8,128)(2,1)S(1)}, u32[]{:S(2)}, u32[]{:S(2)}) collective-permute-start(bf16[48,16,512]{2,1,0:T(8,128)(2,1)S(1)} %collective-permute-done.5.refs_5_), channel_id=1, source_target_pairs={{0,48},{16,0},{32,16},{48,32},{1,49},{17,1},{33,17},{49,33},{2,50}... | collective-permute-start | bytes 2359304 | tf_op jit(solution)/shard_map/ppermute | solution.py:35
  77.0 5.1 %collective-permute-start.8 = (bf16[8,16,2560]{2,1,0:T(8,128)(2,1)S(1)}, bf16[8,16,2560]{2,1,0:T(8,128)(2,1)S(1)}, u32[]{:S(2)}, u32[]{:S(2)}) collective-permute-start(bf16[8,16,2560]{2,1,0:T(8,128)(2,1)S(1)} %all_to_all.37.own), channel_id=1, source_target_pairs={{0,8},{8,0},{1,9},{9,1},{2,10},{10,2},{3,11},{11,3},{4,12},{12,4},... | collective-permute-start | bytes 1966088 | tf_op jit(solution)/shard_map/ppermute | solution.py:23
  86.0 3.1 %collective-permute-start.9 = (bf16[8,16,5120]{2,1,0:T(8,128)(2,1)S(1)}, bf16[8,16,5120]{2,1,0:T(8,128)(2,1)S(1)}, u32[]{:S(2)}, u32[]{:S(2)}) collective-permute-start(bf16[8,16,5120]{2,1,0:T(8,128)(2,1)S(1)} %get-tuple-element.76), channel_id=1, source_target_pairs={{0,8},{8,0},{1,9},{9,1},{2,10},{10,2},{3,11},{11,3},{4,12},{12,4},... | collective-permute-start | bytes 3932168 | tf_op jit(solution)/shard_map/ppermute | solution.py:23
  89.5 23.4 %copy-start.10 = (f32[128]{0:T(128)S(1)}, f32[128]{0:T(128)}, u32[]{:S(2)}) copy-start(f32[128]{0:T(128)} %param.12) | copy-start | bytes 1540
  138.7 4.9 %collective-permute-start.10 = (bf16[8,16,5120]{2,1,0:T(8,128)(2,1)S(1)}, bf16[8,16,5120]{2,1,0:T(8,128)(2,1)S(1)}, u32[]{:S(2)}, u32[]{:S(2)}) collective-permute-start(bf16[8,16,5120]{2,1,0:T(8,128)(2,1)S(1)} %all_to_all.39.d_own), channel_id=1, source_target_pairs={{0,8},{8,0},{1,9},{9,1},{2,10},{10,2},{3,11},{11,3},{4,12},{12,4},... | collective-permute-start | bytes 3932168 | tf_op jit(solution)/shard_map/ppermute | solution.py:23
  154.3 5.7 %collective-permute-start.11 = (bf16[8,16,2560]{2,1,0:T(8,128)(2,1)S(1)}, bf16[8,16,2560]{2,1,0:T(8,128)(2,1)S(1)}, u32[]{:S(2)}, u32[]{:S(2)}) collective-permute-start(bf16[8,16,2560]{2,1,0:T(8,128)(2,1)S(1)} %get-tuple-element.85), channel_id=1, source_target_pairs={{0,8},{8,0},{1,9},{9,1},{2,10},{10,2},{3,11},{11,3},{4,12},{12,4},... | collective-permute-start | bytes 1966088 | tf_op jit(solution)/shard_map/ppermute | solution.py:23
  154.7 12.1 %collective-permute-start.12 = (bf16[24,16,512]{2,1,0:T(8,128)(2,1)}, bf16[24,16,512]{2,1,0:T(8,128)(2,1)}, u32[]{:S(2)}, u32[]{:S(2)}) collective-permute-start(bf16[24,16,512]{2,1,0:T(8,128)(2,1)} %get-tuple-element.88), channel_id=1, source_target_pairs={{0,16},{16,32},{32,48},{48,0},{1,17},{17,33},{33,49},{49,1},{2,18}... | collective-permute-start | bytes 1179656 | tf_op jit(solution)/shard_map/ppermute | solution.py:31
  154.7 14.3 %collective-permute-start.13 = (bf16[24,16,512]{2,1,0:T(8,128)(2,1)}, bf16[24,16,512]{2,1,0:T(8,128)(2,1)}, u32[]{:S(2)}, u32[]{:S(2)}) collective-permute-start(bf16[24,16,512]{2,1,0:T(8,128)(2,1)} %get-tuple-element.89), channel_id=1, source_target_pairs={{0,48},{16,0},{32,16},{48,32},{1,49},{17,1},{33,17},{49,33},{2,50}... | collective-permute-start | bytes 1179656 | tf_op jit(solution)/shard_map/ppermute | solution.py:35
  157.4 17.9 %collective-permute-start.14 = (bf16[24,16,512]{2,1,0:T(8,128)(2,1)S(1)}, bf16[24,16,512]{2,1,0:T(8,128)(2,1)}, u32[]{:S(2)}, u32[]{:S(2)}) collective-permute-start(bf16[24,16,512]{2,1,0:T(8,128)(2,1)S(1)} %get-tuple-element.90), channel_id=1, source_target_pairs={{0,16},{16,32},{32,48},{48,0},{1,17},{17,33},{33,49},{49,1},{2,18}... | collective-permute-start | bytes 1179656 | tf_op jit(solution)/shard_map/ppermute | solution.py:31
  157.4 17.9 %collective-permute-start.15 = (bf16[24,16,512]{2,1,0:T(8,128)(2,1)S(1)}, bf16[24,16,512]{2,1,0:T(8,128)(2,1)}, u32[]{:S(2)}, u32[]{:S(2)}) collective-permute-start(bf16[24,16,512]{2,1,0:T(8,128)(2,1)S(1)} %get-tuple-element.91), channel_id=1, source_target_pairs={{0,48},{16,0},{32,16},{48,32},{1,49},{17,1},{33,17},{49,33},{2,50}... | collective-permute-start | bytes 1179656 | tf_op jit(solution)/shard_map/ppermute | solution.py:35
  161.3 23.6 %all-to-all-start.5 = ((bf16[8,32,2560]{2,1,0:T(8,128)(2,1)}), bf16[8,32,2560]{2,1,0:T(8,128)(2,1)S(1)}, u32[]{:S(2)}, u32[]{:S(2)}) async-start(bf16[8,32,2560]{2,1,0:T(8,128)(2,1)} %shard_map.126), calls=%async_computation.5 | async-start | bytes 2621440 | tf_op jit(solution)/shard_map/all_to_all | solution.py:39
  175.2 19.6 %collective-permute-start.18 = (bf16[48,16,512]{2,1,0:T(8,128)(2,1)}, bf16[48,16,512]{2,1,0:T(8,128)(2,1)}, u32[]{:S(2)}, u32[]{:S(2)}) collective-permute-start(bf16[48,16,512]{2,1,0:T(8,128)(2,1)} %shard_map.127), channel_id=1, source_target_pairs={{0,16},{16,32},{32,48},{48,0},{1,17},{17,33},{33,49},{49,1},{2,18}... | collective-permute-start | bytes 2359304 | tf_op jit(solution)/shard_map/ppermute | solution.py:31
  176.1 18.8 %collective-permute-start.19 = (bf16[48,16,512]{2,1,0:T(8,128)(2,1)}, bf16[48,16,512]{2,1,0:T(8,128)(2,1)}, u32[]{:S(2)}, u32[]{:S(2)}) collective-permute-start(bf16[48,16,512]{2,1,0:T(8,128)(2,1)} %shard_map.128), channel_id=1, source_target_pairs={{0,48},{16,0},{32,16},{48,32},{1,49},{17,1},{33,17},{49,33},{2,50}... | collective-permute-start | bytes 2359304 | tf_op jit(solution)/shard_map/ppermute | solution.py:35
  185.0 26.6 %collective-permute-start.16 = (bf16[48,16,512]{2,1,0:T(8,128)(2,1)}, bf16[48,16,512]{2,1,0:T(8,128)(2,1)S(1)}, u32[]{:S(2)}, u32[]{:S(2)}) collective-permute-start(bf16[48,16,512]{2,1,0:T(8,128)(2,1)} %shard_map.129), channel_id=1, source_target_pairs={{0,16},{16,32},{32,48},{48,0},{1,17},{17,33},{33,49},{49,1},{2,18}... | collective-permute-start | bytes 2359304 | tf_op jit(solution)/shard_map/ppermute | solution.py:31
  185.0 26.6 %collective-permute-start.17 = (bf16[48,16,512]{2,1,0:T(8,128)(2,1)}, bf16[48,16,512]{2,1,0:T(8,128)(2,1)}, u32[]{:S(2)}, u32[]{:S(2)}) collective-permute-start(bf16[48,16,512]{2,1,0:T(8,128)(2,1)} %shard_map.130), channel_id=1, source_target_pairs={{0,48},{16,0},{32,16},{48,32},{1,49},{17,1},{33,17},{49,33},{2,50}... | collective-permute-start | bytes 2359304 | tf_op jit(solution)/shard_map/ppermute | solution.py:35
  197.4 21.2 %collective-permute-start.20 = (bf16[48,16,512]{2,1,0:T(8,128)(2,1)}, bf16[48,16,512]{2,1,0:T(8,128)(2,1)}, u32[]{:S(2)}, u32[]{:S(2)}) collective-permute-start(bf16[48,16,512]{2,1,0:T(8,128)(2,1)} %shard_map.134), channel_id=1, source_target_pairs={{0,64},{64,0},{1,65},{65,1},{2,66},{66,2},{3,67},{67,3},{4,68},{68... | collective-permute-start | bytes 2359304 | tf_op jit(solution)/shard_map/ppermute | solution.py:27
  197.5 30.1 %all-to-all-start.6 = ((bf16[128,16,128]{2,1,0:T(8,128)(2,1)}), bf16[128,16,128]{2,1,0:T(8,128)(2,1)S(1)}, u32[]{:S(2)}, u32[]{:S(2)}) async-start(bf16[128,16,128]{2,1,0:T(8,128)(2,1)} %shard_map.133), calls=%async_computation.6 | async-start | bytes 1048576 | tf_op jit(solution)/shard_map/all_to_all | solution.py:39
  221.9 6.3 %copy-start.4 = (bf16[512,256]{1,0:T(8,128)(2,1)S(1)}, bf16[512,256]{1,0:T(8,128)(2,1)}, u32[]{:S(2)}) copy-start(bf16[512,256]{1,0:T(8,128)(2,1)} %get-tuple-element.106.down_kept) | copy-start | bytes 786436
  221.9 6.3 %copy-start.5 = (bf16[128,512]{1,0:T(8,128)(2,1)S(1)}, bf16[128,512]{1,0:T(8,128)(2,1)}, u32[]{:S(2)}) copy-start(bf16[128,512]{1,0:T(8,128)(2,1)} %get-tuple-element.105.up_kept) | copy-start | bytes 393220
  222.0 6.3 %collective-permute-start.21 = (bf16[384,512]{1,0:T(8,128)(2,1)}, bf16[384,512]{1,0:T(8,128)(2,1)S(1)}, u32[]{:S(2)}, u32[]{:S(2)}) collective-permute-start(bf16[384,512]{1,0:T(8,128)(2,1)} %get-tuple-element.107), channel_id=1, source_target_pairs={{0,8},{8,0},{1,9},{9,1},{2,10},{10,2},{3,11},{11,3},{4,12},{12,4},... | collective-permute-start | bytes 1179656 | tf_op jit(solution)/shard_map/ppermute | solution.py:23
  (5 other events, 11.3 us)

commit v5 on v4

--- a/solution.py
+++ b/solution.py
@@ -291,7 +291,7 @@
         rstds[b] = jnp.broadcast_to(rstd, (16, 128))
         return carry
 
-    lax.fori_loop(0, OWN, sample, 0, unroll=10)
+    lax.fori_loop(0, OWN, sample, 0, unroll=20)
     for k in range(16):
         block = normal[:, k, :]
         quarter, tail = k // 4 * 4, k % 4 * 128
@@ -414,7 +414,7 @@
         mix_part[...] += dot(dsum.astype(BF), tokens, ((1,), (1,)))
         return carry
 
-    lax.fori_loop(0, OWN, sample, 0, unroll=10)
+    lax.fori_loop(0, OWN, sample, 0, unroll=20)
     for r in range(8):
         quarter, tail = r // 2 * 4, r % 2 * 512
         for u in range(4):
@@ -449,7 +449,7 @@
         proj_part[...] += dot(d_proj.astype(BF), tokens, ((1,), (1,)))
         return carry
 
-    lax.fori_loop(0, OWN, sample, 0, unroll=10)
+    lax.fori_loop(0, OWN, sample, 0, unroll=20)
     repeat = one_where((16, 128), lambda k, lane: lane % 16 == k)
     spread = dot(proj_part[...].astype(BF), repeat, ((0,), (0,)))
     token = lax.broadcasted_iota(jnp.int32, (128, 128), 0)
@@ -607,7 +607,7 @@
         ],
         scalars=1,
         remote_out=5,
-        room=24,
+        room=36,
     )
 
     low1, high1 = right(far1_low), left(far1_high)

time: 231 us -> 228 us (0.987)
    unnamed x26 -> x24, local copies, waits for them, and re-layouts: 5.05 us -> 2.92 us
  transfers between devices with their start and end apart: 24 -> 24, of which waited for: 13 -> 13; matrix products, arithmetic and copies ran while one was open for 0% -> 0% of each run, Pallas kernels for 12% -> 11%
where the time goes in v5:
time: 228 us; the launch traced here: 227 us
  blocking collectives  98.7 us (43%)
  Pallas kernels  46.1 us (20%)
  starting transfers between devices  46 us (20%)
  waiting for transfers between devices  32.3 us (14%)
  local copies, waits for them, and re-layouts  2.92 us (1%)
    all_to_all x5, blocking collectives, exchange(): return lax.all_to_all(a, axes, 0, 0, tiled=True)  98.7 us
    pallas_call x19, Pallas kernels, call(): pl.pallas_call(body, out_shape=outs, in_specs=[small] * scalars + [whole]...  46.1 us
    ppermute x7, starting transfers between devices, left(): return lax.ppermute(a, 'x', BWD)  17.5 us
    ppermute x7, waiting for transfers between devices, right(): return lax.ppermute(a, 'x', FWD)  17.1 us
    all_to_all x2, starting transfers between devices, exchange(): return lax.all_to_all(a, axes, 0, 0, tiled=True)  13 us
    ppermute x6, starting transfers between devices, sibling(): return lax.ppermute(a, 'core', SWAP)  12.7 us
    ppermute x6, waiting for transfers between devices, sibling(): return lax.ppermute(a, 'core', SWAP)  9.01 us
  transfers between devices with their start and end apart: 24, of which 13 were waited for; matrix products, arithmetic and copies ran while one was open for 0% of the time, Pallas kernels for 11%

profile of v5, /device:TPU:1, one launch (start us, length us, event | category | flops | bytes accessed | tf_op | source)
XLA Modules:
  0.0 227.0 jit_solution(9267429715820563243)
XLA Ops:
  9.6 2.5 %collective-permute-start.2 = (bf16[48,16,512]{2,1,0:T(8,128)(2,1)S(1)}, bf16[48,16,512]{2,1,0:T(8,128)(2,1)S(1)}, u32[]{:S(2)}, u32[]{:S(2)}) collective-permute-start(bf16[48,16,512]{2,1,0:T(8,128)(2,1)S(1)} %get-tuple-element.60.refs_0_), channel_id=1, source_target_pairs={{0,48},{16,0},{32,16},{48,32},{1,49},{17,1},{33,17},{49,33},{2,50}... | collective-permute-start | bytes 2359304 | tf_op jit(solution)/shard_map/ppermute | solution.py:35
  12.9 25.0 %all_to_all.35.message = bf16[8,352,128]{2,1,0:T(8,128)(2,1)S(1)} all-to-all(bf16[8,352,128]{2,1,0:T(8,128)(2,1)S(1)} %shard_map.118), channel_id=1, replica_groups=mesh['zlo'=2,'x'=4,'core'=2,'zhi'=2,'y'=4] {'zhi','y'}, dimensions={0} | all-to-all | bytes 1441792 | tf_op jit(solution)/shard_map/all_to_all | solution.py:39
  37.9 2.5 %collective-permute-start.5 = (bf16[48,16,512]{2,1,0:T(8,128)(2,1)S(1)}, bf16[48,16,512]{2,1,0:T(8,128)(2,1)S(1)}, u32[]{:S(2)}, u32[]{:S(2)}) collective-permute-start(bf16[48,16,512]{2,1,0:T(8,128)(2,1)S(1)} %collective-permute-done.3.refs_4_), channel_id=1, source_target_pairs={{0,48},{16,0},{32,16},{48,32},{1,49},{17,1},{33,17},{49,33},{2,50}... | collective-permute-start | bytes 2359304 | tf_op jit(solution)/shard_map/ppermute | solution.py:35
  40.5 2.8 %shard_map.121 = (bf16[8,16,2560]{2,1,0:T(8,128)(2,1)S(1)}, f32[20,16,128]{2,1,0:T(8,128)S(1)}, f32[20,16,128]{2,1,0:T(8,128)S(1)}) custom-call(bf16[8,352,128]{2,1,0:T(8,128)(2,1)S(1)} %all_to_all.35.message), custom_call_target="tpu_custom_call" | custom-call | tf_op jit(solution)/shard_map/pallas_call | solution.py:58
  43.3 15.4 %all_to_all.36.cot = bf16[8,320,128]{2,1,0:T(8,128)(2,1)S(1)} all-to-all(bf16[8,320,128]{2,1,0:T(8,128)(2,1)S(1)} %bitcast.14), channel_id=1, replica_groups=mesh['zlo'=2,'x'=4,'core'=2,'zhi'=2,'y'=4] {'zhi','y'}, dimensions={0} | all-to-all | bytes 1310720 | tf_op jit(solution)/shard_map/all_to_all | solution.py:39
  59.2 2.7 %collective-permute-start.7 = (bf16[48,16,512]{2,1,0:T(8,128)(2,1)S(1)}, bf16[48,16,512]{2,1,0:T(8,128)(2,1)S(1)}, u32[]{:S(2)}, u32[]{:S(2)}) collective-permute-start(bf16[48,16,512]{2,1,0:T(8,128)(2,1)S(1)} %collective-permute-done.5.refs_5_), channel_id=1, source_target_pairs={{0,48},{16,0},{32,16},{48,32},{1,49},{17,1},{33,17},{49,33},{2,50}... | collective-permute-start | bytes 2359304 | tf_op jit(solution)/shard_map/ppermute | solution.py:35
  61.9 13.8 %all_to_all.37.own = bf16[8,16,2560]{2,1,0:T(8,128)(2,1)S(1)} all-to-all(bf16[8,16,2560]{2,1,0:T(8,128)(2,1)S(1)} %get-tuple-element.67), channel_id=1, replica_groups=mesh['zlo'=2,'x'=4,'core'=2,'zhi'=2,'y'=4] {'zhi','y'}, dimensions={0} | all-to-all | bytes 1310720 | tf_op jit(solution)/shard_map/all_to_all | solution.py:39
  77.1 3.3 %collective-permute-start.8 = (bf16[8,16,2560]{2,1,0:T(8,128)(2,1)S(1)}, bf16[8,16,2560]{2,1,0:T(8,128)(2,1)S(1)}, u32[]{:S(2)}, u32[]{:S(2)}) collective-permute-start(bf16[8,16,2560]{2,1,0:T(8,128)(2,1)S(1)} %all_to_all.37.own), channel_id=1, source_target_pairs={{0,8},{8,0},{1,9},{9,1},{2,10},{10,2},{3,11},{11,3},{4,12},{12,4},... | collective-permute-start | bytes 1966088 | tf_op jit(solution)/shard_map/ppermute | solution.py:23
  82.1 3.9 %shard_map.122 = (bf16[320,512]{1,0:T(8,128)(2,1)S(1)}, f32[320,512]{1,0:T(8,128)S(1)}, bf16[320,2048]{1,0:T(8,128)(2,1)S(1)}, bf16[16,128,512]{2,1,0:T(8,128)(2...) custom-call(s32[4]{0:T(128)S(1)} %pad_add_fusion.place, ...), custom_call_target="tpu_custom_call" | custom-call | tf_op jit(solution)/shard_map/pallas_call | solution.py:58
  86.5 2.7 %collective-permute-done.9.refs_1_ = bf16[8,16,5120]{2,1,0:T(8,128)(2,1)S(1)} collective-permute-done((bf16[8,16,5120]{2,1,0:T(8,128)(2,1)S(1)}, bf16[8,16,5120]{2,1,0:T(8,128)(2,1)S(1)}, u32[]{:S(2)}, u32[]{:S(2)}) %collective-permute-start.9) | collective-permute-done | bytes 1310752 | tf_op jit(solution)/shard_map/ppermute | solution.py:23
  89.5 23.4 %all_to_all.38.parts = bf16[8,16,5120]{2,1,0:T(8,128)(2,1)S(1)} all-to-all(bf16[8,16,5120]{2,1,0:T(8,128)(2,1)S(1)} %shard_map.123), channel_id=1, replica_groups=mesh['zlo'=2,'x'=4,'core'=2,'zhi'=2,'y'=4] {'zhi','y'}, dimensions={0} | all-to-all | bytes 2621440 | tf_op jit(solution)/shard_map/all_to_all | solution.py:39
  112.9 4.5 %shard_map.124 = (bf16[8,16,2560]{2,1,0:T(8,128)(2,1)S(1)}, bf16[8,16,5120]{2,1,0:T(8,128)(2,1)S(1)}, f32[128,128]{1,0:T(8,128)S(1)}, f32[8,128]{1,0:T(8,128)S(1)}) custom-call(s32[4]{0:T(128)S(1)} %pad_add_fusion.place, bf16[8,16,5120]{2,1,0:T(8,128)(2,1)S(1)} %all_to_all.38.parts, bf16[8,352,128]{2,1,0:T(8,128)(2,1)S(1)} %all_to_all.35.message, ...), custom_call_target="tpu_custom_call" | custom-call | tf_op jit(solution)/shard_map/pallas_call | solution.py:58
  117.3 21.2 %all_to_all.39.d_own = bf16[8,16,5120]{2,1,0:T(8,128)(2,1)S(1)} all-to-all(bf16[8,16,5120]{2,1,0:T(8,128)(2,1)S(1)} %get-tuple-element.78), channel_id=1, replica_groups=mesh['zlo'=2,'x'=4,'core'=2,'zhi'=2,'y'=4] {'zhi','y'}, dimensions={0} | all-to-all | bytes 2621440 | tf_op jit(solution)/shard_map/all_to_all | solution.py:39
  138.5 2.2 collective-permute-start.10
  140.7 2.7 %collective-permute-done.10.d_sib = bf16[8,16,5120]{2,1,0:T(8,128)(2,1)S(1)} collective-permute-done((bf16[8,16,5120]{2,1,0:T(8,128)(2,1)S(1)}, bf16[8,16,5120]{2,1,0:T(8,128)(2,1)S(1)}, u32[]{:S(2)}, u32[]{:S(2)}) %collective-permute-start.10) | collective-permute-done | bytes 1310752 | tf_op jit(solution)/shard_map/ppermute | solution.py:23
  143.4 7.9 %shard_map.125 = (bf16[24,16,512]{2,1,0:T(8,128)(2,1)}, bf16[24,16,512]{2,1,0:T(8,128)(2,1)}, bf16[24,16,512]{2,1,0:T(8,128)(2,1)S(1)}, bf16[24,16,512]{2,1,0:T(...) custom-call(s32[4]{0:T(128)S(1)} %pad_add_fusion.place, ...), custom_call_target="tpu_custom_call" | custom-call | tf_op jit(solution)/shard_map/pallas_call | solution.py:58
  151.7 2.7 %collective-permute-start.13 = (bf16[24,16,512]{2,1,0:T(8,128)(2,1)}, bf16[24,16,512]{2,1,0:T(8,128)(2,1)}, u32[]{:S(2)}, u32[]{:S(2)}) collective-permute-start(bf16[24,16,512]{2,1,0:T(8,128)(2,1)} %get-tuple-element.89), channel_id=1, source_target_pairs={{0,48},{16,0},{32,16},{48,32},{1,49},{17,1},{33,17},{49,33},{2,50}... | collective-permute-start | bytes 1179656 | tf_op jit(solution)/shard_map/ppermute | solution.py:35
  154.4 2.7 %collective-permute-start.15 = (bf16[24,16,512]{2,1,0:T(8,128)(2,1)S(1)}, bf16[24,16,512]{2,1,0:T(8,128)(2,1)}, u32[]{:S(2)}, u32[]{:S(2)}) collective-permute-start(bf16[24,16,512]{2,1,0:T(8,128)(2,1)S(1)} %get-tuple-element.91), channel_id=1, source_target_pairs={{0,48},{16,0},{32,16},{48,32},{1,49},{17,1},{33,17},{49,33},{2,50}... | collective-permute-start | bytes 1179656 | tf_op jit(solution)/shard_map/ppermute | solution.py:35
  158.4 3.6 %all-to-all-start.5 = ((bf16[8,32,2560]{2,1,0:T(8,128)(2,1)}), bf16[8,32,2560]{2,1,0:T(8,128)(2,1)S(1)}, u32[]{:S(2)}, u32[]{:S(2)}) async-start(bf16[8,32,2560]{2,1,0:T(8,128)(2,1)} %shard_map.126), calls=%async_computation.5 | async-start | bytes 2621440 | tf_op jit(solution)/shard_map/all_to_all | solution.py:39
  163.8 2.2 shard_map.127
  168.2 4.0 %collective-permute-done.14.refs_1_ = bf16[24,16,512]{2,1,0:T(8,128)(2,1)} collective-permute-done((bf16[24,16,512]{2,1,0:T(8,128)(2,1)S(1)}, bf16[24,16,512]{2,1,0:T(8,128)(2,1)}, u32[]{:S(2)}, u32[]{:S(2)}) %collective-permute-start.14) | collective-permute-done | bytes 393248 | tf_op jit(solution)/shard_map/ppermute | solution.py:31
  179.3 2.7 %all-to-all-done.5.back = bf16[8,32,2560]{2,1,0:T(8,128)(2,1)S(1)} async-done(((bf16[8,32,2560]{2,1,0:T(8,128)(2,1)}), bf16[8,32,2560]{2,1,0:T(8,128)(2,1)S(1)}, u32[]{:S(2)}, u32[]{:S(2)}) %all-to-all-start.5) | async-done | bytes 1310752 | tf_op jit(solution)/shard_map/all_to_all | solution.py:39
  182.0 2.7 %collective-permute-start.17 = (bf16[48,16,512]{2,1,0:T(8,128)(2,1)}, bf16[48,16,512]{2,1,0:T(8,128)(2,1)}, u32[]{:S(2)}, u32[]{:S(2)}) collective-permute-start(bf16[48,16,512]{2,1,0:T(8,128)(2,1)} %shard_map.130), channel_id=1, source_target_pairs={{0,48},{16,0},{32,16},{48,32},{1,49},{17,1},{33,17},{49,33},{2,50}... | collective-permute-start | bytes 2359304 | tf_op jit(solution)/shard_map/ppermute | solution.py:35
  184.7 2.7 %shard_map.133 = bf16[128,16,128]{2,1,0:T(8,128)(2,1)} custom-call(bf16[8,32,2560]{2,1,0:T(8,128)(2,1)S(1)} %all-to-all-done.5.back, f32[20,16,128]{2,1,0:T(8,128)S(1)} %get-tuple-element.99.normal, f32[20,16,128]{2,1,0:T(8,128)S(1)} %get-tuple-element.100.rstds, bf16[8,352,128]{2,1,0:T(8,128)(2,1)S(1)} %all_to_all.35.message, ...), custom_call_target="tpu_custom_call" | custom-call | tf_op jit(solution)/shard_map/pallas_call | solution.py:58
  187.4 4.5 %collective-permute-done.18.refs_1_ = bf16[48,16,512]{2,1,0:T(8,128)(2,1)} collective-permute-done((bf16[48,16,512]{2,1,0:T(8,128)(2,1)}, bf16[48,16,512]{2,1,0:T(8,128)(2,1)}, u32[]{:S(2)}, u32[]{:S(2)}) %collective-permute-start.18) | collective-permute-done | bytes 786464 | tf_op jit(solution)/shard_map/ppermute | solution.py:31
  191.9 2.6 %shard_map.134 = bf16[48,16,512]{2,1,0:T(8,128)(2,1)} custom-call(bf16[288,16,512]{2,1,0:T(8,128)(2,1)} %get-tuple-element.87.refs_0_, bf16[48,16,512]{2,1,0:T(8,128)(2,1)} %collective-permute-done.18.refs_1_, bf16[48,16,512]{2,1,0:T(8,128)(2,1)} %collective-permute-done.19.refs_2_), custom_call_target="tpu_custom_call" | custom-call | tf_op jit(solution)/shard_map/pallas_call | solution.py:58
  194.6 9.4 %all-to-all-start.6 = ((bf16[128,16,128]{2,1,0:T(8,128)(2,1)}), bf16[128,16,128]{2,1,0:T(8,128)(2,1)S(1)}, u32[]{:S(2)}, u32[]{:S(2)}) async-start(bf16[128,16,128]{2,1,0:T(8,128)(2,1)} %shard_map.133), calls=%async_computation.6 | async-start | bytes 1048576 | tf_op jit(solution)/shard_map/all_to_all | solution.py:39
  204.0 4.6 %collective-permute-done.16.refs_1_ = bf16[48,16,512]{2,1,0:T(8,128)(2,1)S(1)} collective-permute-done((bf16[48,16,512]{2,1,0:T(8,128)(2,1)}, bf16[48,16,512]{2,1,0:T(8,128)(2,1)S(1)}, u32[]{:S(2)}, u32[]{:S(2)}) %collective-permute-start.16) | collective-permute-done | bytes 786464 | tf_op jit(solution)/shard_map/ppermute | solution.py:31
  209.5 2.5 %shard_map.132.one = bf16[48,16,512]{2,1,0:T(8,128)(2,1)} custom-call(bf16[288,16,512]{2,1,0:T(8,128)(2,1)} %get-tuple-element.87.refs_0_, bf16[48,16,512]{2,1,0:T(8,128)(2,1)} %copy-done.10, bf16[48,16,512]{2,1,0:T(8,128)(2,1)} %collective-permute-done.17.refs_2_), custom_call_target="tpu_custom_call" | custom-call | tf_op jit(solution)/shard_map/pallas_call | solution.py:58
  212.1 3.5 %collective-permute-done.20.two = bf16[48,16,512]{2,1,0:T(8,128)(2,1)} collective-permute-done((bf16[48,16,512]{2,1,0:T(8,128)(2,1)}, bf16[48,16,512]{2,1,0:T(8,128)(2,1)}, u32[]{:S(2)}, u32[]{:S(2)}) %collective-permute-start.20) | collective-permute-done | bytes 786464 | tf_op jit(solution)/shard_map/ppermute | solution.py:27
  215.6 3.4 %shard_map.135 = (bf16[128,512]{1,0:T(8,128)(2,1)}, bf16[512,256]{1,0:T(8,128)(2,1)}, bf16[384,512]{1,0:T(8,128)(2,1)}) custom-call(s32[4]{0:T(128)} %copy-done.5, bf16[48,16,512]{2,1,0:T(8,128)(2,1)} %shard_map.132.one, bf16[48,16,512]{2,1,0:T(8,128)(2,1)} %collective-permute-done.20.two), custom_call_target="tpu_custom_call" | custom-call | tf_op jit(solution)/shard_map/pallas_call | solution.py:58
  219.0 4.7 %collective-permute-start.21 = (bf16[384,512]{1,0:T(8,128)(2,1)}, bf16[384,512]{1,0:T(8,128)(2,1)S(1)}, u32[]{:S(2)}, u32[]{:S(2)}) collective-permute-start(bf16[384,512]{1,0:T(8,128)(2,1)} %get-tuple-element.107), channel_id=1, source_target_pairs={{0,8},{8,0},{1,9},{9,1},{2,10},{10,2},{3,11},{11,3},{4,12},{12,4},... | collective-permute-start | bytes 1179656 | tf_op jit(solution)/shard_map/ppermute | solution.py:23
  (65 shorter events, 31.3 us)
Async XLA Ops:
  0.6 11.5 %copy-start.8 = (bf16[128,12]{0,1:T(8,128)(2,1)S(1)}, bf16[128,12]{0,1:T(8,128)(2,1)}, u32[]{:S(2)}) copy-start(bf16[128,12]{0,1:T(8,128)(2,1)} %param.11) | copy-start | bytes 9220
  0.6 11.5 %copy-start.7 = (bf16[16,16]{1,0:T(8,128)(2,1)S(1)}, bf16[16,16]{1,0:T(8,128)(2,1)}, u32[]{:S(2)}) copy-start(bf16[16,16]{1,0:T(8,128)(2,1)} %proj.1) | copy-start | bytes 1540
  2.7 140.7 %copy-start.5 = (s32[4]{0:T(128)}, s32[4]{0:T(128)S(1)}, u32[]{:S(2)}) copy-start(s32[4]{0:T(128)S(1)} %pad_add_fusion.place) | copy-start | bytes 52
  2.7 9.4 %copy-start.2 = (bf16[160,16,128]{2,1,0:T(8,128)(2,1)S(1)}, bf16[160,16,128]{2,1,0:T(8,128)(2,1)}, u32[]{:S(2)}) copy-start(bf16[160,16,128]{2,1,0:T(8,128)(2,1)} %param.7) | copy-start | bytes 1966084
  3.4 2.9 %collective-permute-start = (bf16[384,512]{1,0:T(8,128)(2,1)S(1)}, bf16[384,512]{1,0:T(8,128)(2,1)S(1)}, u32[]{:S(2)}, u32[]{:S(2)}) collective-permute-start(bf16[384,512]{1,0:T(8,128)(2,1)S(1)} %shard_map.119), channel_id=1, source_target_pairs={{0,8},{8,0},{1,9},{9,1},{2,10},{10,2},{3,11},{11,3},{4,12},{12,4},... | collective-permute-start | bytes 1179656 | tf_op jit(solution)/shard_map/ppermute | solution.py:23
  7.8 30.1 %collective-permute-start.3 = (bf16[48,16,512]{2,1,0:T(8,128)(2,1)S(1)}, bf16[48,16,512]{2,1,0:T(8,128)(2,1)S(1)}, u32[]{:S(2)}, u32[]{:S(2)}) collective-permute-start(bf16[48,16,512]{2,1,0:T(8,128)(2,1)S(1)} %get-tuple-element.60.refs_0_), channel_id=1, source_target_pairs={{0,64},{64,0},{1,65},{65,1},{2,66},{66,2},{3,67},{67,3},{4,68},{68... | collective-permute-start | bytes 2359304 | tf_op jit(solution)/shard_map/ppermute | solution.py:27
  9.6 28.3 %collective-permute-start.2 = (bf16[48,16,512]{2,1,0:T(8,128)(2,1)S(1)}, bf16[48,16,512]{2,1,0:T(8,128)(2,1)S(1)}, u32[]{:S(2)}, u32[]{:S(2)}) collective-permute-start(bf16[48,16,512]{2,1,0:T(8,128)(2,1)S(1)} %get-tuple-element.60.refs_0_), channel_id=1, source_target_pairs={{0,48},{16,0},{32,16},{48,32},{1,49},{17,1},{33,17},{49,33},{2,50}... | collective-permute-start | bytes 2359304 | tf_op jit(solution)/shard_map/ppermute | solution.py:35
  12.1 25.8 %collective-permute-start.1 = (bf16[48,16,512]{2,1,0:T(8,128)(2,1)S(1)}, bf16[48,16,512]{2,1,0:T(8,128)(2,1)S(1)}, u32[]{:S(2)}, u32[]{:S(2)}) collective-permute-start(bf16[48,16,512]{2,1,0:T(8,128)(2,1)S(1)} %get-tuple-element.60.refs_0_), channel_id=1, source_target_pairs={{0,16},{16,32},{32,48},{48,0},{1,17},{17,33},{33,49},{49,1},{2,18}... | collective-permute-start | bytes 2359304 | tf_op jit(solution)/shard_map/ppermute | solution.py:31
  12.9 30.4 %copy-start.11 = (bf16[160,16,128]{2,1,0:T(8,128)(2,1)S(1)}, bf16[160,16,128]{2,1,0:T(8,128)(2,1)}, u32[]{:S(2)}) copy-start(bf16[160,16,128]{2,1,0:T(8,128)(2,1)} %param.13) | copy-start | bytes 1966084
  37.9 20.7 %collective-permute-start.5 = (bf16[48,16,512]{2,1,0:T(8,128)(2,1)S(1)}, bf16[48,16,512]{2,1,0:T(8,128)(2,1)S(1)}, u32[]{:S(2)}, u32[]{:S(2)}) collective-permute-start(bf16[48,16,512]{2,1,0:T(8,128)(2,1)S(1)} %collective-permute-done.3.refs_4_), channel_id=1, source_target_pairs={{0,48},{16,0},{32,16},{48,32},{1,49},{17,1},{33,17},{49,33},{2,50}... | collective-permute-start | bytes 2359304 | tf_op jit(solution)/shard_map/ppermute | solution.py:35
  40.5 18.8 %collective-permute-start.4 = (bf16[48,16,512]{2,1,0:T(8,128)(2,1)S(1)}, bf16[48,16,512]{2,1,0:T(8,128)(2,1)S(1)}, u32[]{:S(2)}, u32[]{:S(2)}) collective-permute-start(bf16[48,16,512]{2,1,0:T(8,128)(2,1)S(1)} %collective-permute-done.3.refs_4_), channel_id=1, source_target_pairs={{0,16},{16,32},{32,48},{48,0},{1,17},{17,33},{33,49},{49,1},{2,18}... | collective-permute-start | bytes 2359304 | tf_op jit(solution)/shard_map/ppermute | solution.py:31
  59.2 17.8 %collective-permute-start.6 = (bf16[48,16,512]{2,1,0:T(8,128)(2,1)S(1)}, bf16[48,16,512]{2,1,0:T(8,128)(2,1)S(1)}, u32[]{:S(2)}, u32[]{:S(2)}) collective-permute-start(bf16[48,16,512]{2,1,0:T(8,128)(2,1)S(1)} %collective-permute-done.1.refs_3_), channel_id=1, source_target_pairs={{0,16},{16,32},{32,48},{48,0},{1,17},{17,33},{33,49},{49,1},{2,18}... | collective-permute-start | bytes 2359304 | tf_op jit(solution)/shard_map/ppermute | solution.py:31
  59.2 17.8 %collective-permute-start.7 = (bf16[48,16,512]{2,1,0:T(8,128)(2,1)S(1)}, bf16[48,16,512]{2,1,0:T(8,128)(2,1)S(1)}, u32[]{:S(2)}, u32[]{:S(2)}) collective-permute-start(bf16[48,16,512]{2,1,0:T(8,128)(2,1)S(1)} %collective-permute-done.5.refs_5_), channel_id=1, source_target_pairs={{0,48},{16,0},{32,16},{48,32},{1,49},{17,1},{33,17},{49,33},{2,50}... | collective-permute-start | bytes 2359304 | tf_op jit(solution)/shard_map/ppermute | solution.py:35
  77.1 5.1 %collective-permute-start.8 = (bf16[8,16,2560]{2,1,0:T(8,128)(2,1)S(1)}, bf16[8,16,2560]{2,1,0:T(8,128)(2,1)S(1)}, u32[]{:S(2)}, u32[]{:S(2)}) collective-permute-start(bf16[8,16,2560]{2,1,0:T(8,128)(2,1)S(1)} %all_to_all.37.own), channel_id=1, source_target_pairs={{0,8},{8,0},{1,9},{9,1},{2,10},{10,2},{3,11},{11,3},{4,12},{12,4},... | collective-permute-start | bytes 1966088 | tf_op jit(solution)/shard_map/ppermute | solution.py:23
  86.0 3.1 %collective-permute-start.9 = (bf16[8,16,5120]{2,1,0:T(8,128)(2,1)S(1)}, bf16[8,16,5120]{2,1,0:T(8,128)(2,1)S(1)}, u32[]{:S(2)}, u32[]{:S(2)}) collective-permute-start(bf16[8,16,5120]{2,1,0:T(8,128)(2,1)S(1)} %get-tuple-element.76), channel_id=1, source_target_pairs={{0,8},{8,0},{1,9},{9,1},{2,10},{10,2},{3,11},{11,3},{4,12},{12,4},... | collective-permute-start | bytes 3932168 | tf_op jit(solution)/shard_map/ppermute | solution.py:23
  89.5 23.4 %copy-start.9 = (f32[128]{0:T(128)S(1)}, f32[128]{0:T(128)}, u32[]{:S(2)}) copy-start(f32[128]{0:T(128)} %param.12) | copy-start | bytes 1540
  138.5 4.9 %collective-permute-start.10 = (bf16[8,16,5120]{2,1,0:T(8,128)(2,1)S(1)}, bf16[8,16,5120]{2,1,0:T(8,128)(2,1)S(1)}, u32[]{:S(2)}, u32[]{:S(2)}) collective-permute-start(bf16[8,16,5120]{2,1,0:T(8,128)(2,1)S(1)} %all_to_all.39.d_own), channel_id=1, source_target_pairs={{0,8},{8,0},{1,9},{9,1},{2,10},{10,2},{3,11},{11,3},{4,12},{12,4},... | collective-permute-start | bytes 3932168 | tf_op jit(solution)/shard_map/ppermute | solution.py:23
  151.3 5.8 %collective-permute-start.11 = (bf16[8,16,2560]{2,1,0:T(8,128)(2,1)S(1)}, bf16[8,16,2560]{2,1,0:T(8,128)(2,1)S(1)}, u32[]{:S(2)}, u32[]{:S(2)}) collective-permute-start(bf16[8,16,2560]{2,1,0:T(8,128)(2,1)S(1)} %get-tuple-element.85), channel_id=1, source_target_pairs={{0,8},{8,0},{1,9},{9,1},{2,10},{10,2},{3,11},{11,3},{4,12},{12,4},... | collective-permute-start | bytes 1966088 | tf_op jit(solution)/shard_map/ppermute | solution.py:23
  151.7 12.1 %collective-permute-start.12 = (bf16[24,16,512]{2,1,0:T(8,128)(2,1)}, bf16[24,16,512]{2,1,0:T(8,128)(2,1)}, u32[]{:S(2)}, u32[]{:S(2)}) collective-permute-start(bf16[24,16,512]{2,1,0:T(8,128)(2,1)} %get-tuple-element.88), channel_id=1, source_target_pairs={{0,16},{16,32},{32,48},{48,0},{1,17},{17,33},{33,49},{49,1},{2,18}... | collective-permute-start | bytes 1179656 | tf_op jit(solution)/shard_map/ppermute | solution.py:31
  151.7 14.3 %collective-permute-start.13 = (bf16[24,16,512]{2,1,0:T(8,128)(2,1)}, bf16[24,16,512]{2,1,0:T(8,128)(2,1)}, u32[]{:S(2)}, u32[]{:S(2)}) collective-permute-start(bf16[24,16,512]{2,1,0:T(8,128)(2,1)} %get-tuple-element.89), channel_id=1, source_target_pairs={{0,48},{16,0},{32,16},{48,32},{1,49},{17,1},{33,17},{49,33},{2,50}... | collective-permute-start | bytes 1179656 | tf_op jit(solution)/shard_map/ppermute | solution.py:35
  154.4 17.8 %collective-permute-start.14 = (bf16[24,16,512]{2,1,0:T(8,128)(2,1)S(1)}, bf16[24,16,512]{2,1,0:T(8,128)(2,1)}, u32[]{:S(2)}, u32[]{:S(2)}) collective-permute-start(bf16[24,16,512]{2,1,0:T(8,128)(2,1)S(1)} %get-tuple-element.90), channel_id=1, source_target_pairs={{0,16},{16,32},{32,48},{48,0},{1,17},{17,33},{33,49},{49,1},{2,18}... | collective-permute-start | bytes 1179656 | tf_op jit(solution)/shard_map/ppermute | solution.py:31
  154.4 17.8 %collective-permute-start.15 = (bf16[24,16,512]{2,1,0:T(8,128)(2,1)S(1)}, bf16[24,16,512]{2,1,0:T(8,128)(2,1)}, u32[]{:S(2)}, u32[]{:S(2)}) collective-permute-start(bf16[24,16,512]{2,1,0:T(8,128)(2,1)S(1)} %get-tuple-element.91), channel_id=1, source_target_pairs={{0,48},{16,0},{32,16},{48,32},{1,49},{17,1},{33,17},{49,33},{2,50}... | collective-permute-start | bytes 1179656 | tf_op jit(solution)/shard_map/ppermute | solution.py:35
  158.4 23.6 %all-to-all-start.5 = ((bf16[8,32,2560]{2,1,0:T(8,128)(2,1)}), bf16[8,32,2560]{2,1,0:T(8,128)(2,1)S(1)}, u32[]{:S(2)}, u32[]{:S(2)}) async-start(bf16[8,32,2560]{2,1,0:T(8,128)(2,1)} %shard_map.126), calls=%async_computation.5 | async-start | bytes 2621440 | tf_op jit(solution)/shard_map/all_to_all | solution.py:39
  172.3 19.6 %collective-permute-start.18 = (bf16[48,16,512]{2,1,0:T(8,128)(2,1)}, bf16[48,16,512]{2,1,0:T(8,128)(2,1)}, u32[]{:S(2)}, u32[]{:S(2)}) collective-permute-start(bf16[48,16,512]{2,1,0:T(8,128)(2,1)} %shard_map.127), channel_id=1, source_target_pairs={{0,16},{16,32},{32,48},{48,0},{1,17},{17,33},{33,49},{49,1},{2,18}... | collective-permute-start | bytes 2359304 | tf_op jit(solution)/shard_map/ppermute | solution.py:31
  173.1 18.8 %collective-permute-start.19 = (bf16[48,16,512]{2,1,0:T(8,128)(2,1)}, bf16[48,16,512]{2,1,0:T(8,128)(2,1)}, u32[]{:S(2)}, u32[]{:S(2)}) collective-permute-start(bf16[48,16,512]{2,1,0:T(8,128)(2,1)} %shard_map.128), channel_id=1, source_target_pairs={{0,48},{16,0},{32,16},{48,32},{1,49},{17,1},{33,17},{49,33},{2,50}... | collective-permute-start | bytes 2359304 | tf_op jit(solution)/shard_map/ppermute | solution.py:35
  182.0 26.6 %collective-permute-start.16 = (bf16[48,16,512]{2,1,0:T(8,128)(2,1)}, bf16[48,16,512]{2,1,0:T(8,128)(2,1)S(1)}, u32[]{:S(2)}, u32[]{:S(2)}) collective-permute-start(bf16[48,16,512]{2,1,0:T(8,128)(2,1)} %shard_map.129), channel_id=1, source_target_pairs={{0,16},{16,32},{32,48},{48,0},{1,17},{17,33},{33,49},{49,1},{2,18}... | collective-permute-start | bytes 2359304 | tf_op jit(solution)/shard_map/ppermute | solution.py:31
  182.0 26.6 %collective-permute-start.17 = (bf16[48,16,512]{2,1,0:T(8,128)(2,1)}, bf16[48,16,512]{2,1,0:T(8,128)(2,1)}, u32[]{:S(2)}, u32[]{:S(2)}) collective-permute-start(bf16[48,16,512]{2,1,0:T(8,128)(2,1)} %shard_map.130), channel_id=1, source_target_pairs={{0,48},{16,0},{32,16},{48,32},{1,49},{17,1},{33,17},{49,33},{2,50}... | collective-permute-start | bytes 2359304 | tf_op jit(solution)/shard_map/ppermute | solution.py:35
  194.5 21.1 %collective-permute-start.20 = (bf16[48,16,512]{2,1,0:T(8,128)(2,1)}, bf16[48,16,512]{2,1,0:T(8,128)(2,1)}, u32[]{:S(2)}, u32[]{:S(2)}) collective-permute-start(bf16[48,16,512]{2,1,0:T(8,128)(2,1)} %shard_map.134), channel_id=1, source_target_pairs={{0,64},{64,0},{1,65},{65,1},{2,66},{66,2},{3,67},{67,3},{4,68},{68... | collective-permute-start | bytes 2359304 | tf_op jit(solution)/shard_map/ppermute | solution.py:27
  194.6 30.1 %all-to-all-start.6 = ((bf16[128,16,128]{2,1,0:T(8,128)(2,1)}), bf16[128,16,128]{2,1,0:T(8,128)(2,1)S(1)}, u32[]{:S(2)}, u32[]{:S(2)}) async-start(bf16[128,16,128]{2,1,0:T(8,128)(2,1)} %shard_map.133), calls=%async_computation.6 | async-start | bytes 1048576 | tf_op jit(solution)/shard_map/all_to_all | solution.py:39
  219.0 6.3 %copy-start.3 = (bf16[512,256]{1,0:T(8,128)(2,1)S(1)}, bf16[512,256]{1,0:T(8,128)(2,1)}, u32[]{:S(2)}) copy-start(bf16[512,256]{1,0:T(8,128)(2,1)} %get-tuple-element.106.down_kept) | copy-start | bytes 786436
  219.0 6.3 %copy-start.4 = (bf16[128,512]{1,0:T(8,128)(2,1)S(1)}, bf16[128,512]{1,0:T(8,128)(2,1)}, u32[]{:S(2)}) copy-start(bf16[128,512]{1,0:T(8,128)(2,1)} %get-tuple-element.105.up_kept) | copy-start | bytes 393220
  219.0 6.3 %collective-permute-start.21 = (bf16[384,512]{1,0:T(8,128)(2,1)}, bf16[384,512]{1,0:T(8,128)(2,1)S(1)}, u32[]{:S(2)}, u32[]{:S(2)}) collective-permute-start(bf16[384,512]{1,0:T(8,128)(2,1)} %get-tuple-element.107), channel_id=1, source_target_pairs={{0,8},{8,0},{1,9},{9,1},{2,10},{10,2},{3,11},{11,3},{4,12},{12,4},... | collective-permute-start | bytes 1179656 | tf_op jit(solution)/shard_map/ppermute | solution.py:23
  (4 other events, 9.2 us)
